TPU v7x, 32 devices: a whole 2x2x4 slice. The times are simulated.
32 devices in a mesh: image: 2 (over x), dom: 4 (over y, core), band: 4 (over z).
Axes of the slice: x: 2, y: 2, z: 4, core: 2. Of those that a mesh axis runs over, the one named last changes fastest.
Arguments:
- y_cur: float32 [8192, 2048], P(('image', 'dom'), 'band'), parts along dimension 0, may hold values from -6 to 6
- y_prev: float32 [8192, 2048], P(('image', 'dom'), 'band'), parts along dimension 0, may hold values from -3 to 3
- connect: int32 [4096, 8], P('dom'), may hold values from 0 to 2047, as said below
- face_map: int32 [4096], P('dom'), may hold values from 0 to 1023, as said below
- elem_scale: float32 [4096], P('dom'), may hold values from 0.5 to 2
- potential: float32 [8192], P(('image', 'dom')), parts along dimension 0, may hold values from 0 to 2
Outputs:
- y_next: float32 [8192, 2048], P(('image', 'dom'), 'band'), parts along dimension 0
- margin: float32 [4096, 2048], P(('image', 'band'), 'dom'), parts along dimension 0
- projected: float32 [4096, 2048], P(('image', 'band'), 'dom'), parts along dimension 0
There are 2 independent parts, one for each index of `image`. A program takes and returns all parts, laid end to end along the dimension named above; an argument that names none is the same for every part. Nothing has to cross between parts.
Inputs may be any that keep to these rules, and one draw needn't show every extreme that they name: `connect`: each domain's 1024 nodes lie on one plane at positions q = 32 * j + k of a periodic 32 * 32 grid. Its 1024 elements, in arbitrary order, are the cells (j, k) between that plane and the next domain's plane (after the last domain comes the first). Corner 4 * a + 2 * b + c (a, b, c each 0 or 1) sits at position ((j + b) mod 32) * 32 + (k + c) mod 32; its entry is the local index of the domain's own node there when a = 0, and 1024 + that position on the next domain's plane when a = 1. `face_map`: each domain's 1024 entries list, for positions q = 0 to 1023 in order, the local index of the domain's node at position q: a permutation of 0 to 1023.
All inputs are finite; a program needn't handle non-finite values.
Results may differ from a plain program's by a relative error of at most 0.0003.
Values sent between devices are 32-bit elements; how exact they have to be, the bound alone decides.
No kernel may reach another device: no remote copies, remote signals or barrier semaphores. Data moves between devices by JAX's collectives and lax.ppermute only.
A program may use at most 128 MiB of HBM per device.

v0:
```python
import functools

import jax
import jax.numpy as jnp
import numpy as np
from jax import lax
from jax.experimental import pallas as pl
from jax.experimental.pallas import tpu as pltpu
from jax.sharding import PartitionSpec as P

SIDE = 32
STATES_DEV = 512
BLOCK = 128
WINDOW = 256
MARGIN = (WINDOW - BLOCK) // 2

cheb_low = 1.0
cheb_high = 9.0
centre = 0.5 * (cheb_high + cheb_low)
half_width = 0.5 * (cheb_high - cheb_low)

OFFSETS = [(dj, dk) for dj in (-1, 0, 1) for dk in (-1, 0, 1)]
PARAMS = pltpu.CompilerParams(vmem_limit_bytes=32 * 1024 * 1024)


COST = pl.CostEstimate(flops=1, bytes_accessed=1, transcendentals=0)


def element_table():
    stiff_line = np.array([[1.0, -1.0], [-1.0, 1.0]])
    mass_line = np.array([[1.0 / 3.0, 1.0 / 6.0], [1.0 / 6.0, 1.0 / 3.0]])
    total = np.kron(stiff_line, np.kron(mass_line, mass_line))
    total = total + np.kron(mass_line, np.kron(stiff_line, mass_line))
    total = total + np.kron(mass_line, np.kron(mass_line, stiff_line))
    return total.astype(np.float32)


def halves(x):
    high = x.astype(jnp.bfloat16)
    low = (x - high.astype(jnp.float32)).astype(jnp.bfloat16)
    return high, low


def dot(a, b):
    return lax.dot_general(a, b, (((1,), (0,)), ((), ())), preferred_element_type=jnp.float32)


def call(kernel, after, *, in_specs, name, into=(), **options):
    count = len(in_specs)
    extra = [*[array for _, array in into], *after]

    def body(*refs):
        kernel(*refs[:count], *refs[count + len(extra) :])

    made = pl.pallas_call(
        body,
        in_specs=[*in_specs, *[pl.BlockSpec(memory_space=pl.ANY)] * len(extra)],
        input_output_aliases={count + at: out for at, (out, _) in enumerate(into)},
        compiler_params=PARAMS,
        cost_estimate=COST,
        name=name,
        **options,
    )
    return lambda *args: made(*args, *extra)


def join_kernel(left_ref, right_ref, out_ref, *passed):
    width = left_ref.shape[1]
    out_ref[:, :width] = left_ref[...]
    out_ref[:, width:] = right_ref[...]


def join(left, right, after, passed=()):
    nodes, width = left.shape
    rows = 256
    part = pl.BlockSpec((rows, width), lambda i: (i, 0))
    return call(
        join_kernel,
        after,
        into=[(1 + at, x) for at, x in enumerate(passed)],
        grid=(nodes // rows,),
        in_specs=[part, part],
        out_specs=[pl.BlockSpec((rows, 2 * width), lambda i: (i, 0))]
        + [pl.BlockSpec(memory_space=pl.ANY)] * len(passed),
        out_shape=[jax.ShapeDtypeStruct((nodes, 2 * width), left.dtype)]
        + [jax.ShapeDtypeStruct(x.shape, x.dtype) for x in passed],
        name="join",
    )(left, right)


def to_grid_kernel(offsets, map_ref, x_ref, *refs):
    whole_ref, outs, (high_ref, low_ref) = refs[0], refs[1:-2], refs[-2:]
    step = pl.program_id(0)

    @pl.when(step == 0)
    def _():
        high_ref[...], low_ref[...] = halves(x_ref[...])

    rows, nodes = whole_ref.shape[0], x_ref.shape[0]
    place = lax.broadcasted_iota(jnp.int32, (BLOCK, nodes), 1)
    for at in range(rows // BLOCK):
        row = map_ref[pl.ds(step * (rows // BLOCK) + at, 1), :]
        column = jnp.broadcast_to(row, (BLOCK, BLOCK)).T
        column = jnp.concatenate([column] * (nodes // BLOCK), axis=1)
        pick = jnp.where(place == column, 1.0, 0.0).astype(jnp.bfloat16)
        moved = dot(pick, high_ref[...]) + dot(pick, low_ref[...])
        out = slice(at * BLOCK, (at + 1) * BLOCK)
        whole_ref[out, :] = moved
        for first, out_ref in zip(offsets, outs):
            out_ref[out, :] = moved[:, first : first + out_ref.shape[1]]


def to_grid(face_map, x, first, width, widths=(), after=()):
    nodes = x.shape[0]
    rows = 512
    offsets = tuple(sum(widths[:at]) for at in range(len(widths)))
    sizes = (width, *widths)
    at = first // width
    return call(
        functools.partial(to_grid_kernel, offsets),
        after,
        grid=(nodes // rows,),
        in_specs=[
            pl.BlockSpec((nodes // BLOCK, BLOCK), lambda i: (0, 0)),
            pl.BlockSpec((nodes, width), lambda i: (0, at)),
        ],
        out_specs=[pl.BlockSpec((rows, size), lambda i: (i, 0)) for size in sizes],
        out_shape=[jax.ShapeDtypeStruct((nodes, size), jnp.float32) for size in sizes],
        scratch_shapes=[pltpu.VMEM((nodes, width), jnp.bfloat16)] * 2,
        name="to_grid",
    )(face_map.reshape(nodes // BLOCK, BLOCK), x)


def from_grid_kernel(map_ref, *refs):
    pieces, (out_ref, high_ref, low_ref) = refs[:-3], refs[-3:]
    step = pl.program_id(0)

    @pl.when(step == 0)
    def _():
        split_columns([[x] for x in pieces], high_ref, low_ref, 0)

    rows, nodes = out_ref.shape[0], high_ref.shape[0]
    node = lax.broadcasted_iota(jnp.int32, (rows, nodes), 0) + step * rows
    pick = jnp.where(node == map_ref[...], 1.0, 0.0).astype(jnp.bfloat16)
    out_ref[...] = dot(pick, high_ref[...]) + dot(pick, low_ref[...])


def from_grid(face_map, pieces, at, states, so_far=None, after=()):
    nodes = pieces[0].shape[0]
    width = sum(x.shape[1] for x in pieces)
    rows = 256
    return call(
        from_grid_kernel,
        after,
        into=[(0, so_far)] if at else [],
        grid=(nodes // rows,),
        in_specs=[pl.BlockSpec((1, nodes), lambda i: (0, 0))]
        + [pl.BlockSpec(x.shape, lambda i: (0, 0)) for x in pieces],
        out_specs=pl.BlockSpec((rows, width), lambda i: (i, at)),
        out_shape=jax.ShapeDtypeStruct((nodes, states), jnp.float32),
        scratch_shapes=[pltpu.VMEM((nodes, width), jnp.bfloat16)] * 2,
        name="from_grid",
    )(face_map.reshape(1, nodes), *pieces)


def plane_terms(shifted, stiff, layer):
    terms = []
    for dj, dk in OFFSETS:
        total = None
        for b in (0, 1):
            for c in (0, 1):
                if b + dj in (0, 1) and c + dk in (0, 1):
                    weight = float(stiff[2 * b + c, 4 * layer + 2 * (b + dj) + c + dk])
                    term = weight * shifted[b][c]
                    total = term if total is None else total + term
        terms.append(total)
    return terms


def write_terms(stiff, odd, own_ref, before_ref, potential_ref, terms_ref):
    nodes = own_ref.shape[1]
    column = lax.broadcasted_iota(jnp.int32, (8, nodes), 1) & (SIDE - 1)
    here, layers = None, []
    for ref in (own_ref, before_ref):
        scale = jnp.broadcast_to(0.5 * ref[...], (8, nodes))
        back = jnp.where(column == 0, pltpu.roll(scale, nodes - SIDE + 1, 1), pltpu.roll(scale, 1, 1))
        shifted = [[x, pltpu.roll(x, SIDE, 1)] for x in (scale, back)]
        shifted = [[shifted[c][b] for c in (0, 1)] for b in (0, 1)]
        mine = plane_terms(shifted, stiff, 0)
        here = mine if here is None else [a + b for a, b in zip(here, mine)]
        layers.append(plane_terms(shifted, stiff, 1))
    here[4] = here[4] + potential_ref[...]
    after, back = layers
    paired = [jnp.where(odd, b, a) for a, b in zip(after, back)]
    far = [jnp.where(odd, a, b) for a, b in zip(after, back)]
    for at, term in enumerate(here + paired + far):
        terms_ref[at : at + 1, :] = term[:1]


def write_bands(terms, out_ref):
    row = lax.broadcasted_iota(jnp.int32, (SIDE, BLOCK), 0)
    lane = lax.broadcasted_iota(jnp.int32, (SIDE, BLOCK), 1)
    turn = (lane - row) & (SIDE - 1)
    for line in range(BLOCK // SIDE):
        rows = slice(line * SIDE, (line + 1) * SIDE)
        rest = slice(BLOCK + rows.start, BLOCK + rows.stop)
        masks = {}
        for dj, dk in OFFSETS:
            tile, group = divmod(line + MARGIN // SIDE + dj, BLOCK // SIDE)
            masks[dj, dk] = tile, (turn == dk % SIDE) & ((lane >> 5) == group)
        for plane in range(3):
            totals = [jnp.zeros((SIDE, BLOCK), jnp.float32) for _ in range(WINDOW // BLOCK)]
            for at, offset in enumerate(OFFSETS):
                term = terms[rows, plane * 9 + at : plane * 9 + at + 1]
                tile, mask = masks[offset]
                totals[tile] = jnp.where(mask, term, totals[tile])
            for tile, total in enumerate(totals):
                columns = slice(tile * BLOCK, (tile + 1) * BLOCK)
                out_ref[plane, 0, rows, columns], out_ref[plane, 0, rest, columns] = halves(total)


def prepare_kernel(stiff, odd_ref, own_ref, before_ref, potential_ref, map_ref, prev_ref, *refs):
    band_ref, last_ref, terms_ref, high_ref, low_ref = refs
    step = pl.program_id(0)
    nodes = prev_ref.shape[0]

    @pl.when(step == 0)
    def _():
        write_terms(stiff, odd_ref[0] == 1, own_ref, before_ref, potential_ref, terms_ref)
        split_columns([[prev_ref]], high_ref, low_ref, 0)

    write_bands(terms_ref[:, pl.ds(pl.multiple_of(step * BLOCK, BLOCK), BLOCK)].T, band_ref)
    place = lax.broadcasted_iota(jnp.int32, (BLOCK, nodes), 1)
    column = jnp.broadcast_to(map_ref[pl.ds(step, 1), :], (BLOCK, BLOCK)).T
    column = jnp.concatenate([column] * (nodes // BLOCK), axis=1)
    pick = jnp.where(place == column, 1.0, 0.0).astype(jnp.bfloat16)
    last_ref[...] = dot(pick, high_ref[...]) + dot(pick, low_ref[...])


def prepare(stiff, odd, own, before, potential, face_map, y_prev, after):
    nodes, states = y_prev.shape
    row = pl.BlockSpec((1, nodes), lambda i: (0, 0))
    return call(
        functools.partial(prepare_kernel, stiff),
        after,
        grid=(nodes // BLOCK,),
        in_specs=[pl.BlockSpec(memory_space=pltpu.SMEM), row, row, row]
        + [pl.BlockSpec((nodes // BLOCK, BLOCK), lambda i: (0, 0))]
        + [pl.BlockSpec((nodes, states), lambda i: (0, 0))],
        out_specs=[
            pl.BlockSpec((3, 1, 2 * BLOCK, WINDOW), lambda i: (0, i, 0, 0)),
            pl.BlockSpec((BLOCK, states), lambda i: (i, 0)),
        ],
        out_shape=[
            jax.ShapeDtypeStruct((3, nodes // BLOCK, 2 * BLOCK, WINDOW), jnp.bfloat16),
            jax.ShapeDtypeStruct((nodes, states), jnp.float32),
        ],
        scratch_shapes=[pltpu.VMEM((32, nodes), jnp.float32)]
        + [pltpu.VMEM((nodes, states), jnp.bfloat16)] * 2,
        name="prepare",
    )(
        odd,
        *[x.reshape(1, nodes) for x in (own, before, potential)],
        face_map.reshape(nodes // BLOCK, BLOCK),
        y_prev,
    )


def apply_kernel(filtered, band_ref, own_ref, paired_ref, far_ref, *refs):
    wide = refs[-1]
    step = pl.program_id(0)
    nodes, width = own_ref.shape

    @pl.when(step == 0)
    def _():
        for plane, ref in enumerate((own_ref, paired_ref, far_ref)):
            for columns, part in zip((slice(0, width), slice(width, 2 * width)), halves(ref[...])):
                wide[plane, pl.ds(MARGIN, nodes), columns] = part
                wide[plane, pl.ds(0, MARGIN), columns] = part[nodes - MARGIN :]
                wide[plane, pl.ds(MARGIN + nodes, MARGIN), columns] = part[:MARGIN]

    per_step = band_ref.shape[1]
    for at in range(per_step):
        block = step * per_step + at
        first = pl.multiple_of(block * BLOCK, BLOCK)
        total = None
        for plane in range(3):
            term = dot(band_ref[plane, at], wide[plane, pl.ds(first, WINDOW), :])
            total = term if total is None else total + term
        total = total[:BLOCK] + total[BLOCK:]
        total = total[:, :width] + total[:, width:]
        rows = pl.ds(at * BLOCK, BLOCK)
        if filtered:
            last_ref, out_ref, joined_ref, turned_high, turned_low = refs[:5]
            mine = own_ref[pl.ds(first, BLOCK), :]
            total = (2.0 / half_width) * (total - centre * mine) - last_ref[rows, :]
            out_ref[rows, :] = total
            joined_ref[rows, :] = total
        else:
            turned_high, turned_low = refs[:2]
        turned_high[:, rows], turned_low[:, rows] = halves(total.T)


def apply_specs(nodes, width):
    per_step = 2
    rows = per_step * BLOCK
    return dict(
        grid=(nodes // rows,),
        scratch_shapes=[pltpu.VMEM((3, nodes + 2 * MARGIN, 2 * width), jnp.bfloat16)],
        name="apply_h",
    ), pl.BlockSpec((3, per_step, 2 * BLOCK, WINDOW), lambda i: (0, i, 0, 0)), rows


def next_degree(band, own, paired, far, last, half, at, so_far, after):
    nodes, width = far.shape
    states = own.shape[1]
    options, band_spec, rows = apply_specs(nodes, width)
    inside = at % (half // width)
    column = pl.BlockSpec((nodes, width), lambda i: (0, at))
    part = pl.BlockSpec((rows, width), lambda i: (i, at))
    turned = pl.BlockSpec((width, rows), lambda i: (at, i))
    turned_shape = jax.ShapeDtypeStruct((states, nodes), jnp.bfloat16)
    into = [(out, so_far[out - 1]) for out in (1, 2, 3) if (inside if out == 1 else at)]
    return call(
        functools.partial(apply_kernel, True),
        after,
        into=into,
        in_specs=[band_spec, column, column, pl.BlockSpec((nodes, width), lambda i: (0, 0)), part],
        out_specs=[
            pl.BlockSpec((rows, width), lambda i: (i, 0)),
            pl.BlockSpec((rows, width), lambda i: (i, inside)),
            turned,
            turned,
        ],
        out_shape=[
            jax.ShapeDtypeStruct((nodes, width), jnp.float32),
            jax.ShapeDtypeStruct((nodes, half), jnp.float32),
            turned_shape,
            turned_shape,
        ],
        **options,
    )(band, own, paired, far, last)


def applied_next(band, own, paired, far, states, at, so_far, after=()):
    nodes, width = far.shape
    options, band_spec, rows = apply_specs(nodes, width)
    whole = pl.BlockSpec((nodes, width), lambda i: (0, 0))
    turned = pl.BlockSpec((width, rows), lambda i: (at, i))
    turned_shape = jax.ShapeDtypeStruct((states, nodes), jnp.bfloat16)
    return call(
        functools.partial(apply_kernel, False),
        after,
        into=[(out, so_far[out]) for out in (0, 1) if at],
        in_specs=[band_spec, whole, whole, whole],
        out_specs=[turned, turned],
        out_shape=[turned_shape, turned_shape],
        **options,
    )(band, own, paired, far)


def split_columns(pieces, high_ref, low_ref, first):
    for group in pieces:
        piece = group[0][...]
        for other in group[1:]:
            piece = piece + other[...]
        columns = slice(first, first + piece.shape[1])
        first += piece.shape[1]
        high_ref[:, columns], low_ref[:, columns] = halves(piece)


def rows_product(left_high, left_low, high_ref, low_ref):
    total = dot(left_high[...], high_ref[...]) + dot(left_high[...], low_ref[...])
    return total + dot(left_low[...], high_ref[...])


def sorted_kernel(count, keep_ref, left_high, left_low, *refs):
    own, first = [[x] for x in refs[:count]], [[x] for x in refs[count:-4]]
    kept_ref, sent_ref, high_ref, low_ref = refs[-4:]
    width = kept_ref.shape[1]

    @pl.when((pl.program_id(0) == 0) & (keep_ref[0] == 1))
    def _():
        split_columns(own, high_ref, low_ref, 0)
        split_columns(first, high_ref, low_ref, width)

    @pl.when((pl.program_id(0) == 0) & (keep_ref[0] != 1))
    def _():
        split_columns(own, high_ref, low_ref, width)
        split_columns(first, high_ref, low_ref, 0)

    total = rows_product(left_high, left_low, high_ref, low_ref)
    kept_ref[...] = total[:, :width]
    sent_ref[...] = total[:, width:]


def sorted_products(keep, turned, own, first, after=()):
    states, nodes = turned[0].shape
    rows = 256
    width = sum(piece.shape[1] for piece in own)
    left = pl.BlockSpec((rows, nodes), lambda i: (i, 0))
    out = pl.BlockSpec((rows, width), lambda i: (i, 0))
    shape = jax.ShapeDtypeStruct((states, width), jnp.float32)
    return call(
        functools.partial(sorted_kernel, len(own)),
        after,
        grid=(states // rows,),
        in_specs=[pl.BlockSpec(memory_space=pltpu.SMEM), left, left]
        + [pl.BlockSpec(piece.shape, lambda i: (0, 0)) for piece in (*own, *first)],
        out_specs=[out, out],
        out_shape=[shape, shape],
        scratch_shapes=[pltpu.VMEM((nodes, 2 * width), jnp.bfloat16)] * 2,
        name="sorted_products",
    )(keep, *turned, *own, *first)


def both_kernel(summed, left_high, left_low, more_high, more_low, *refs):
    pieces, (out_ref, high_ref, low_ref) = refs[:-3], refs[-3:]
    step, half = pl.program_id(0), pl.num_programs(0) // 2

    @pl.when(step == 0)
    def _():
        groups = [pieces[at : at + summed] for at in range(0, len(pieces), summed)]
        split_columns(groups, high_ref, low_ref, 0)

    @pl.when(step < half)
    def _():
        out_ref[...] = rows_product(left_high, left_low, high_ref, low_ref)

    @pl.when(step >= half)
    def _():
        out_ref[...] = rows_product(more_high, more_low, high_ref, low_ref)


def both_products(y_turned, h_turned, pieces, summed=1, after=()):
    states, nodes = y_turned[0].shape
    rows = 256
    steps = states // rows
    width = sum(piece.shape[1] for piece in pieces) // summed
    first = pl.BlockSpec((rows, nodes), lambda i: (jnp.minimum(i, steps - 1), 0))
    second = pl.BlockSpec((rows, nodes), lambda i: (jnp.maximum(i - steps, 0), 0))
    return call(
        functools.partial(both_kernel, summed),
        after,
        grid=(2 * steps,),
        in_specs=[first, first, second, second]
        + [pl.BlockSpec(piece.shape, lambda i: (0, 0)) for piece in pieces],
        out_specs=pl.BlockSpec((rows, width), lambda i: (i, 0)),
        out_shape=jax.ShapeDtypeStruct((2 * states, width), jnp.float32),
        scratch_shapes=[pltpu.VMEM((nodes, width), jnp.bfloat16)] * 2,
        name="both_products",
    )(*y_turned, *h_turned, *pieces)


def finish_kernel(weight, count, states, flag_ref, base_ref, *refs):
    sums, arrived = refs[:count], refs[count : 2 * count]
    margin_ref, projected_ref = refs[2 * count :]
    mine = jnp.where(flag_ref[0] == 1, 1.0, 0.0)
    for half, out_ref in enumerate((margin_ref, projected_ref)):
        rows = slice(half * states, (half + 1) * states)
        first = 0
        for block, other in zip(sums, arrived):
            columns = slice(first, first + block.shape[1])
            first += block.shape[1]
            total = base_ref[rows, columns] + mine * block[rows, :] + other[rows, :]
            out_ref[:, columns] = weight * total


def finish(weight, flag, base, sums, arrived):
    states = base.shape[0] // 2
    shape = jax.ShapeDtypeStruct((states, base.shape[1]), jnp.float32)
    return call(
        functools.partial(finish_kernel, weight, len(sums), states),
        (),
        in_specs=[pl.BlockSpec(memory_space=pltpu.SMEM)]
        + [pl.BlockSpec(memory_space=pltpu.VMEM)] * (1 + 2 * len(sums)),
        out_specs=[pl.BlockSpec(memory_space=pltpu.VMEM)] * 2,
        out_shape=[shape, shape],
        name="finish",
    )(flag, base, *sums, *arrived)


def exchange(block, axis, pairs):
    return lax.ppermute(block, axis, pairs + [(b, a) for a, b in pairs])


def paired(block):
    return exchange(block, "dom", [(i, i + 1) for i in range(0, lax.axis_size("dom"), 2)])


def crossed(block):
    size = lax.axis_size("dom")
    return exchange(block, "dom", [(i, (i + 1) % size) for i in range(1, size, 2)])


def to_owner(block, owners, step):
    size = len(owners)
    route = []
    for band, owner in enumerate(owners):
        for to in (owner, owner ^ 2) if step == 1 else (owner,):
            route.append(((to ^ step) * size + band, to * size + band))
    return lax.ppermute(block, ("dom", "band"), route)


def on_device(y_cur, y_prev, connect, face_map, elem_scale, potential):
    stiff = element_table()
    nodes, states = y_cur.shape
    domains, band_count = lax.axis_size("dom"), lax.axis_size("band")
    me, level = lax.axis_index("dom"), lax.axis_index("band")
    swaps = domains == 4 and band_count == 4 and states == STATES_DEV
    half = states // 2
    quarter = states // 4 if swaps else half
    place = jnp.arange(nodes, dtype=jnp.int32)
    cell_place = connect[:, 4] - nodes
    own = jnp.sum(jnp.where(cell_place[:, None] == place[None, :], elem_scale[:, None], 0.0), axis=0)
    before = lax.ppermute(own, "dom", [(i, (i + 1) % domains) for i in range(domains)])
    at_grid = jnp.sum(jnp.where(place[:, None] == face_map[None, :], potential[:, None], 0.0), axis=0)
    odd = (me % 2).astype(jnp.int32).reshape(1)
    weight = 1.0 / (nodes * domains)

    current, *chunks = to_grid(face_map, y_cur, 0, states, (quarter,) * (states // quarter), after=(own,))
    current_paired = paired(current)
    far = [crossed(chunk) for chunk in chunks]
    band, last = prepare(stiff, odd, own, before, at_grid, face_map, y_prev, (current,))

    following, pair_step, joined, middle_step = [], [], [], []
    so_far, waited = [None] * 3, ()
    for at, piece in enumerate(far):
        sources = (band, current, current_paired, piece, last, half, at)
        chunk, *so_far = next_degree(*sources, so_far, waited)
        following.append(chunk)
        waited = (chunk, *pair_step[at - 1 : at]) if at else (chunk,)
        if (at + 1) * quarter % half == 0:
            joined.append(so_far[0])
        if swaps:
            pair_step.append(exchange(chunk, "band", [(0, 1), (2, 3)]))
            if at == 1:
                middle_step.append(exchange(joined[0], "band", [(1, 2)]))
    y_turned = so_far[1:]

    if not swaps:
        y_next = from_grid(face_map, joined, 0, states)
        h_turned = [None] * 2
        for at, piece in enumerate(joined):
            h_turned = applied_next(band, piece, paired(piece), crossed(piece), states, at, h_turned)
        piece = lax.all_gather(jnp.concatenate(joined, axis=1), "band", axis=1, tiled=True)
        block = both_products(y_turned, h_turned, [piece])
        parts = [
            weight * lax.psum_scatter(rows, "dom", scatter_dimension=1, tiled=True)
            for rows in (block[:states], block[states:])
        ]
        return (y_next, *parts)

    outward = [(2, 3), (1, 0)]
    core, chip, upper = me % 2, me // 2, level // 2
    keep = jnp.where(core == level % 2, 1, 0).astype(jnp.int32).reshape(1)
    near_route = [
        (((b // 2 * 2 + c) ^ 2) * 4 + b, (b // 2 * 2 + c) * 4 + b) for b in range(4) for c in (0, 1)
    ]

    def near(rows, after):
        first, sent = sorted_products(keep, rows, following, pair_step, after)
        kept = first + paired(sent)
        return kept, lax.ppermute(kept, ("dom", "band"), near_route), first

    second_out = [lax.ppermute(middle_step[0], "band", outward)]
    near_paired = paired(joined[0])
    waited = (following[3], middle_step[0], *pair_step[2:], near_paired)
    far_pair, later = join(*pair_step[:2], waited, (joined[1],))
    middle_step.append(exchange(later, "band", [(1, 2)]))
    third_middle = [exchange(far_pair, "band", [(1, 2)])]
    sources = (joined[0], near_paired, crossed(joined[0]))
    h_turned = applied_next(band, *sources, states, 0, None, (far_pair,))
    near_margin = near(y_turned, (h_turned[0],))
    (far_pair,) = join(*pair_step[2:], (near_margin[2], second_out[0], middle_step[1]))
    second_out.append(lax.ppermute(middle_step[1], "band", outward))
    third_middle.append(exchange(far_pair, "band", [(1, 2)]))
    sources = (later, paired(later), crossed(later))
    h_turned = applied_next(band, *sources, states, 1, h_turned, (far_pair,))
    near_projected = near(h_turned, (near_margin[0],))
    waited = (near_projected[2], second_out[1], third_middle[0])
    y_next = from_grid(face_map, [joined[0]], 0, states, None, waited)

    second_owner, third_owner = [2, 2, 1, 1], [3, 3, 0, 0]
    pieces = [x for pair in zip(middle_step, second_out) for x in pair]
    second = both_products(y_turned, h_turned, pieces, 2, (y_next, near_projected[0]))
    y_next = from_grid(face_map, [later], 1, states, y_next, (second, third_middle[1]))
    third_pieces = [third_middle[0], third_middle[1][:, :quarter], third_middle[1][:, quarter:]]
    third_out = [lax.ppermute(x, "band", outward) for x in third_pieces]
    waited = (y_next, near_margin[1])
    second = second + to_owner(second, second_owner, 1)
    second_far = to_owner(second, second_owner, 2)

    is_near, is_second = chip == upper, core == upper
    third, third_far = [], []
    for at, pair in enumerate(zip(third_pieces, third_out)):
        block = both_products(y_turned, h_turned, list(pair), 2, waited)
        waited = (block, second, near_projected[1]) if at == 0 else (block, third[0], second_far)
        block = block + to_owner(block, third_owner, 1)
        third.append(block)
        third_far.append(to_owner(block, third_owner, 2))
    near_rows = jnp.concatenate([sum(near_margin[:2]), sum(near_projected[:2])])
    base = jnp.where(is_near, near_rows, jnp.where(is_second, second + second_far, 0.0))
    flag = jnp.where(is_near | is_second, 0, 1).astype(jnp.int32).reshape(1)
    return (y_next, *finish(weight, flag, base, third, third_far))


def solution(mesh):
    placed = (
        P(("image", "dom"), "band"),
        P(("image", "dom"), "band"),
        P("dom", None),
        P("dom"),
        P("dom"),
        P(("image", "dom")),
    )
    return jax.shard_map(
        on_device,
        mesh=mesh,
        in_specs=placed,
        out_specs=(
            P(("image", "dom"), "band"),
            P(("image", "band"), "dom"),
            P(("image", "band"), "dom"),
        ),
        check_vma=False,
    )
```

profile of v0, /device:TPU:18, one launch (start us, length us, event | category | flops | bytes accessed | tf_op | source)
XLA Modules:
  0.0 253.8 jit_solution(9464810662631864874)
XLA Ops:
  5.0 4.2 %to_grid.1 = (f32[1024,512]{1,0:T(8,128)}, f32[1024,128]{1,0:T(8,128)}, f32[1024,128]{1,0:T(8,128)}, f32[1024,128]{1,0:T(8,128)}, f32[1024,128]{1,0:T(8,128)S(1)}) custom-call(s32[8,128]{1,0:T(8,128)S(1)} %bitcast.9, f32[1024,512]{1,0:T(8,128)S(1)} %copy-done.24, f32[1024]{0:T(1024)S(1)} %select_reduce_fusion.1.refs_2_), custom_call_target="tpu_custom_call" | custom-call | flops 1 | bytes 1 | tf_op jit(solution)/shard_map/to_grid/pallas_call | solution.py:64
  13.9 9.9 %collective-permute-done = f32[1024]{0:T(1024)S(1)} collective-permute-done((f32[1024]{0:T(1024)S(1)}, f32[1024]{0:T(1024)S(1)}, u32[]{:S(2)}, u32[]{:S(2)}) %collective-permute-start) | collective-permute-done | bytes 4128 | tf_op jit(solution)/shard_map/ppermute | solution.py:516
  25.4 7.7 %prepare.1 = (bf16[3,8,256,256]{3,2,1,0:T(8,128)(2,1)S(1)}, f32[1024,512]{1,0:T(8,128)S(1)}) custom-call(s32[1]{0:T(128)} %bitcast.1.refs_0_, f32[1,1024]{1,0:T(1,128)S(1)} %bitcast.13, f32[1,1024]{1,0:T(1,128)S(1)} %bitcast.15, f32[1,1024]{1,0:T(1,128)S(1)} %bitcast.14, s32[8,128]{1,0:T(8,128)S(1)} %bitcast.10, f32[1024,512]{1,0:T(8,128)S(1)} %copy-done.25, ...), custom_call_target="tpu_custom_call" | custom-call | flops 1 | bytes 1 | tf_op jit(solution)/shard_map/prepare/pallas_call | solution.py:64
  33.1 4.5 %apply_h.6 = (f32[1024,128]{1,0:T(8,128)S(1)}, f32[1024,256]{1,0:T(8,128)}, bf16[512,1024]{1,0:T(8,128)(2,1)S(1)}, bf16[512,1024]{1,0:T(8,128)(2,1)S(1)}) custom-call(bf16[3,8,256,256]{3,2,1,0:T(8,128)(2,1)S(1)} %get-tuple-element.39.refs_0_, f32[1024,512]{1,0:T(8,128)} %get-tuple-element.38.refs_6_.refs_1_, f32[1024,512]{1,0:T(8,128)} %collective-permute-done.1.refs_2_, ...), custom_call_target="tpu_custom_call" | custom-call | flops 1 | bytes 1 | tf_op jit(solution)/shard_map/apply_h/pallas_call | solution.py:64
  39.2 4.5 %apply_h.7 = (f32[1024,128]{1,0:T(8,128)S(1)}, f32[1024,256]{1,0:T(8,128)}, bf16[512,1024]{1,0:T(8,128)(2,1)S(1)}, bf16[512,1024]{1,0:T(8,128)(2,1)S(1)}) custom-call(bf16[3,8,256,256]{3,2,1,0:T(8,128)(2,1)S(1)} %get-tuple-element.39.refs_0_, ...), custom_call_target="tpu_custom_call", output_to_operand_aliasing={{1}: (5, {}), {2}: (6, {}), {3}: (7, {})} | custom-call | flops 1 | bytes 1 | tf_op jit(solution)/shard_map/apply_h/pallas_call | solution.py:64
  47.6 4.9 %collective-permute-done.3.refs_8_.refs_0_.refs_7_ = f32[1024,128]{1,0:T(8,128)S(1)} collective-permute-done((f32[1024,128]{1,0:T(8,128)S(1)}, f32[1024,128]{1,0:T(8,128)S(1)}, u32[]{:S(2)}, u32[]{:S(2)}) %collective-permute-start.3) | collective-permute-done | bytes 524320 | tf_op jit(solution)/shard_map/ppermute | solution.py:484
  52.5 4.6 %apply_h.8 = (f32[1024,128]{1,0:T(8,128)}, f32[1024,256]{1,0:T(8,128)}, bf16[512,1024]{1,0:T(8,128)(2,1)S(1)}, bf16[512,1024]{1,0:T(8,128)(2,1)S(1)}) custom-call(bf16[3,8,256,256]{3,2,1,0:T(8,128)(2,1)S(1)} %get-tuple-element.39.refs_0_, f32[1024,512]{1,0:T(8,128)} %get-tuple-element.38.refs_6_.refs_1_, ...), custom_call_target="tpu_custom_call", output_to_operand_aliasing={{2}: (5, {}), {3}: (6, {})} | custom-call | flops 1 | bytes 1 | tf_op jit(solution)/shard_map/apply_h/pallas_call | solution.py:64
  57.7 4.1 %collective-permute-done.5.refs_9_.refs_1_.refs_8_ = f32[1024,128]{1,0:T(8,128)S(1)} collective-permute-done((f32[1024,128]{1,0:T(8,128)S(1)}, f32[1024,128]{1,0:T(8,128)S(1)}, u32[]{:S(2)}, u32[]{:S(2)}) %collective-permute-start.5) | collective-permute-done | bytes 524320 | tf_op jit(solution)/shard_map/ppermute | solution.py:484
  61.8 4.5 %apply_h.9 = (f32[1024,128]{1,0:T(8,128)}, f32[1024,256]{1,0:T(8,128)}, bf16[512,1024]{1,0:T(8,128)(2,1)S(1)}, bf16[512,1024]{1,0:T(8,128)(2,1)S(1)}) custom-call(bf16[3,8,256,256]{3,2,1,0:T(8,128)(2,1)S(1)} %get-tuple-element.39.refs_0_, f32[1024,512]{1,0:T(8,128)} %get-tuple-element.38.refs_6_.refs_1_, ...), custom_call_target="tpu_custom_call", output_to_operand_aliasing={{1}: (5, {}), {2}: (6, {}), {3}: (7, {})} | custom-call | flops 1 | bytes 1 | tf_op jit(solution)/shard_map/apply_h/pallas_call | solution.py:64
  73.9 9.6 %collective-permute-done.10.refs_6_.refs_10_.refs_1_ = f32[1024,128]{1,0:T(8,128)} collective-permute-done((f32[1024,128]{1,0:T(8,128)}, f32[1024,128]{1,0:T(8,128)}, u32[]{:S(2)}, u32[]{:S(2)}) %collective-permute-start.10) | collective-permute-done | bytes 524320 | tf_op jit(solution)/shard_map/ppermute | solution.py:484
  83.5 10.3 %collective-permute-done.9.refs_5_.refs_9_.refs_0_ = f32[1024,128]{1,0:T(8,128)} collective-permute-done((f32[1024,128]{1,0:T(8,128)}, f32[1024,128]{1,0:T(8,128)}, u32[]{:S(2)}, u32[]{:S(2)}) %collective-permute-start.9) | collective-permute-done | bytes 524320 | tf_op jit(solution)/shard_map/ppermute | solution.py:484
  98.2 5.5 %apply_h.10 = (bf16[512,1024]{1,0:T(8,128)(2,1)S(1)}, bf16[512,1024]{1,0:T(8,128)(2,1)S(1)}) custom-call(bf16[3,8,256,256]{3,2,1,0:T(8,128)(2,1)S(1)} %get-tuple-element.39.refs_0_, f32[1024,256]{1,0:T(8,128)} %get-tuple-element.58.refs_1_, f32[1024,256]{1,0:T(8,128)} %collective-permute-done.11.refs_7_.refs_2_, ...), custom_call_target="tpu_custom_call" | custom-call | flops 1 | bytes 1 | tf_op jit(solution)/shard_map/apply_h/pallas_call | solution.py:64
  103.8 6.4 %sorted_products.2 = (f32[512,512]{1,0:T(8,128)S(1)}, f32[512,512]{1,0:T(8,128)S(1)}) custom-call(s32[1]{0:T(128)} %bitcast.7.refs_0_, bf16[512,1024]{1,0:T(8,128)(2,1)S(1)} %copy-done.1, bf16[512,1024]{1,0:T(8,128)(2,1)S(1)} %copy-done.3, f32[1024,128]{1,0:T(8,128)S(1)} %copy-done.20, f32[1024,128]{1,0:T(8,128)S(1)} %copy-done.18, ...), custom_call_target="tpu_custom_call" | custom-call | flops 1 | bytes 1 | tf_op jit(solution)/shard_map/sorted_products/pallas_call | solution.py:64
  111.0 8.6 %collective-permute-done.16.refs_4_.refs_6_ = f32[1024,256]{1,0:T(8,128)S(1)} collective-permute-done((f32[1024,256]{1,0:T(8,128)}, f32[1024,256]{1,0:T(8,128)S(1)}, u32[]{:S(2)}, u32[]{:S(2)}) %collective-permute-start.16) | collective-permute-done | bytes 1048608 | tf_op jit(solution)/shard_map/ppermute | solution.py:484
  125.3 11.0 %collective-permute-done.13.refs_3_ = f32[1024,256]{1,0:T(8,128)S(1)} collective-permute-done((f32[1024,256]{1,0:T(8,128)}, f32[1024,256]{1,0:T(8,128)S(1)}, u32[]{:S(2)}, u32[]{:S(2)}) %collective-permute-start.13) | collective-permute-done | bytes 1048608 | tf_op jit(solution)/shard_map/ppermute | solution.py:484
  136.2 4.7 %apply_h.11 = (bf16[512,1024]{1,0:T(8,128)(2,1)S(1)}, bf16[512,1024]{1,0:T(8,128)(2,1)S(1)}) custom-call(bf16[3,8,256,256]{3,2,1,0:T(8,128)(2,1)S(1)} %get-tuple-element.39.refs_0_, f32[1024,256]{1,0:T(8,128)} %get-tuple-element.59.refs_1_, f32[1024,256]{1,0:T(8,128)S(1)} %collective-permute-done.12.refs_2_, ...), custom_call_target="tpu_custom_call", output_to_operand_aliasing={{0}: (4, {}), {1}: (5, {})} | custom-call | flops 1 | bytes 1 | tf_op jit(solution)/shard_map/apply_h/pallas_call | solution.py:64
  141.0 6.4 %sorted_products.3 = (f32[512,512]{1,0:T(8,128)S(1)}, f32[512,512]{1,0:T(8,128)S(1)}) custom-call(s32[1]{0:T(128)} %bitcast.7.refs_0_, bf16[512,1024]{1,0:T(8,128)(2,1)S(1)} %get-tuple-element.66.refs_1_.refs_2_, bf16[512,1024]{1,0:T(8,128)(2,1)S(1)} %get-tuple-element.67.refs_2_.refs_3_, f32[1024,128]{1,0:T(8,128)S(1)} %copy-done.20, ...), custom_call_target="tpu_custom_call" | custom-call | flops 1 | bytes 1 | tf_op jit(solution)/shard_map/sorted_products/pallas_call | solution.py:64
  147.9 4.1 %from_grid.2.refs_8_.refs_2_ = f32[1024,512]{1,0:T(8,128)} custom-call(s32[1,1024]{1,0:T(1,128)S(1)} %bitcast.11, f32[1024,256]{1,0:T(8,128)} %get-tuple-element.58.refs_1_, f32[512,512]{1,0:T(8,128)S(1)} %get-tuple-element.69.refs_2_, f32[1024,256]{1,0:T(8,128)S(1)} %collective-permute-done.18.refs_3_.refs_7_, f32[1024,256]{1,0:T(8,128)S(1)} %collective-permute-done.19.refs_4_), custom_call_target="tpu_custom_call" | custom-call | flops 1 | bytes 1 | tf_op jit(solution)/shard_map/from_grid/pallas_call | solution.py:64
  153.6 6.0 %both_products.4.refs_3_ = f32[1024,512]{1,0:T(8,128)S(1)} custom-call(bf16[512,1024]{1,0:T(8,128)(2,1)S(1)} %copy-done.1, bf16[512,1024]{1,0:T(8,128)(2,1)S(1)} %copy-done.3, bf16[512,1024]{1,0:T(8,128)(2,1)S(1)} %get-tuple-element.66.refs_1_.refs_2_, bf16[512,1024]{1,0:T(8,128)(2,1)S(1)} %get-tuple-element.67.refs_2_.refs_3_, ...), custom_call_target="tpu_custom_call" | custom-call | flops 1 | bytes 1 | tf_op jit(solution)/shard_map/both_products/pallas_call | solution.py:64
  170.2 19.2 %collective-permute-done.21.refs_4_ = f32[1024,256]{1,0:T(8,128)S(1)} collective-permute-done((f32[1024,256]{1,0:T(8,128)S(1)}, f32[1024,256]{1,0:T(8,128)S(1)}, u32[]{:S(2)}, u32[]{:S(2)}) %collective-permute-start.21) | collective-permute-done | bytes 1048608 | tf_op jit(solution)/shard_map/ppermute | solution.py:484
  189.3 4.1 %from_grid.3.refs_6_ = f32[1024,512]{1,0:T(8,128)} custom-call(s32[1,1024]{1,0:T(1,128)S(1)} %bitcast.12, f32[1024,256]{1,0:T(8,128)} %get-tuple-element.59.refs_1_, f32[1024,512]{1,0:T(8,128)} %from_grid.2.refs_8_.refs_2_, f32[1024,512]{1,0:T(8,128)S(1)} %both_products.4.refs_3_, ...), custom_call_target="tpu_custom_call", output_to_operand_aliasing={{}: (2, {})} | custom-call | flops 1 | bytes 1 | tf_op jit(solution)/shard_map/from_grid/pallas_call | solution.py:64
  206.4 9.3 %collective-permute-done.28.refs_5_ = f32[1024,128]{1,0:T(8,128)S(1)} collective-permute-done((f32[1024,128]{1,0:T(8,128)S(1)}, f32[1024,128]{1,0:T(8,128)S(1)}, u32[]{:S(2)}, u32[]{:S(2)}) %collective-permute-start.28) | collective-permute-done | bytes 524320 | tf_op jit(solution)/shard_map/ppermute | solution.py:589
  215.7 9.3 %collective-permute-done.23.refs_8_ = f32[512,512]{1,0:T(8,128)S(1)} collective-permute-done((f32[512,512]{1,0:T(8,128)S(1)}, f32[512,512]{1,0:T(8,128)S(1)}, u32[]{:S(2)}, u32[]{:S(2)}) %collective-permute-start.23) | collective-permute-done | bytes 1048608 | tf_op jit(solution)/shard_map/ppermute | solution.py:564
  244.8 5.6 %collective-permute-done.34.refs_7_ = f32[1024,128]{1,0:T(8,128)} collective-permute-done((f32[1024,128]{1,0:T(8,128)}, f32[1024,128]{1,0:T(8,128)}, u32[]{:S(2)}, u32[]{:S(2)}) %collective-permute-start.34) | collective-permute-done | bytes 524320 | tf_op jit(solution)/shard_map/ppermute | solution.py:502
  (140 shorter events, 83.5 us)
Async XLA Ops:
  9.9 23.2 %collective-permute-start.1 = (f32[1024,512]{1,0:T(8,128)}, f32[1024,512]{1,0:T(8,128)}, u32[]{:S(2)}, u32[]{:S(2)}) collective-permute-start(f32[1024,512]{1,0:T(8,128)} %get-tuple-element.38.refs_6_.refs_1_), channel_id=1, source_target_pairs={{0,4},{8,12},{4,0},{12,8},{1,5},{9,13},{5,1},{13,9},{2,6},{10,14},... | collective-permute-start | bytes 6291464 | tf_op jit(solution)/shard_map/ppermute | solution.py:484
  9.9 23.2 %collective-permute-start.2 = (f32[1024,128]{1,0:T(8,128)}, f32[1024,128]{1,0:T(8,128)}, u32[]{:S(2)}, u32[]{:S(2)}) collective-permute-start(f32[1024,128]{1,0:T(8,128)} %get-tuple-element.40), channel_id=1, source_target_pairs={{4,8},{12,0},{8,4},{0,12},{5,9},{13,1},{9,5},{1,13},{6,10},{14,2},... | collective-permute-start | bytes 1572872 | tf_op jit(solution)/shard_map/ppermute | solution.py:484
  11.6 27.6 %collective-permute-start.4 = (f32[1024,128]{1,0:T(8,128)}, f32[1024,128]{1,0:T(8,128)}, u32[]{:S(2)}, u32[]{:S(2)}) collective-permute-start(f32[1024,128]{1,0:T(8,128)} %get-tuple-element.43), channel_id=1, source_target_pairs={{4,8},{12,0},{8,4},{0,12},{5,9},{13,1},{9,5},{1,13},{6,10},{14,2},... | collective-permute-start | bytes 1572872 | tf_op jit(solution)/shard_map/ppermute | solution.py:484
  13.3 33.3 %collective-permute-start.7 = (f32[1024,128]{1,0:T(8,128)}, f32[1024,128]{1,0:T(8,128)}, u32[]{:S(2)}, u32[]{:S(2)}) collective-permute-start(f32[1024,128]{1,0:T(8,128)} %get-tuple-element.49), channel_id=1, source_target_pairs={{4,8},{12,0},{8,4},{0,12},{5,9},{13,1},{9,5},{1,13},{6,10},{14,2},... | collective-permute-start | bytes 1572872 | tf_op jit(solution)/shard_map/ppermute | solution.py:484
  39.2 18.5 %collective-permute-start.6 = (f32[1024,128]{1,0:T(8,128)S(1)}, f32[1024,128]{1,0:T(8,128)S(1)}, u32[]{:S(2)}, u32[]{:S(2)}) collective-permute-start(f32[1024,128]{1,0:T(8,128)S(1)} %copy-done.29), channel_id=1, source_target_pairs={{4,8},{12,0},{8,4},{0,12},{5,9},{13,1},{9,5},{1,13},{6,10},{14,2},... | collective-permute-start | bytes 1572872 | tf_op jit(solution)/shard_map/ppermute | solution.py:484
  43.7 18.1 %collective-permute-start.5 = (f32[1024,128]{1,0:T(8,128)S(1)}, f32[1024,128]{1,0:T(8,128)S(1)}, u32[]{:S(2)}, u32[]{:S(2)}) collective-permute-start(f32[1024,128]{1,0:T(8,128)S(1)} %get-tuple-element.47.refs_7_.refs_4_), channel_id=1, source_target_pairs={{0,1},{2,3},{1,0},{3,2},{4,5},{6,7},{5,4},{7,6},{8,9},{10,11},{9,8... | collective-permute-start | bytes 1572872 | tf_op jit(solution)/shard_map/ppermute | solution.py:484
  44.1 28.0 %collective-permute-start.8 = (f32[1024,256]{1,0:T(8,128)}, f32[1024,256]{1,0:T(8,128)}, u32[]{:S(2)}, u32[]{:S(2)}) collective-permute-start(f32[1024,256]{1,0:T(8,128)} %get-tuple-element.58.refs_1_), channel_id=1, source_target_pairs={{1,2},{2,1},{5,6},{6,5},{9,10},{10,9},{13,14},{14,13},{17,18},{18,... | collective-permute-start | bytes 3145736 | tf_op jit(solution)/shard_map/ppermute | solution.py:484
  46.6 27.3 %collective-permute-start.11 = (f32[1024,256]{1,0:T(8,128)}, f32[1024,256]{1,0:T(8,128)}, u32[]{:S(2)}, u32[]{:S(2)}) collective-permute-start(f32[1024,256]{1,0:T(8,128)} %get-tuple-element.58.refs_1_), channel_id=1, source_target_pairs={{0,4},{8,12},{4,0},{12,8},{1,5},{9,13},{5,1},{13,9},{2,6},{10,14},... | collective-permute-start | bytes 3145736 | tf_op jit(solution)/shard_map/ppermute | solution.py:484
  52.5 45.7 %collective-permute-start.14 = (f32[1024,256]{1,0:T(8,128)}, f32[1024,256]{1,0:T(8,128)}, u32[]{:S(2)}, u32[]{:S(2)}) collective-permute-start(f32[1024,256]{1,0:T(8,128)} %get-tuple-element.58.refs_1_), channel_id=1, source_target_pairs={{4,8},{12,0},{8,4},{0,12},{5,9},{13,1},{9,5},{1,13},{6,10},{14,2},... | collective-permute-start | bytes 3145736 | tf_op jit(solution)/shard_map/ppermute | solution.py:484
  68.3 15.2 %collective-permute-start.10 = (f32[1024,128]{1,0:T(8,128)}, f32[1024,128]{1,0:T(8,128)}, u32[]{:S(2)}, u32[]{:S(2)}) collective-permute-start(f32[1024,128]{1,0:T(8,128)} %get-tuple-element.57.refs_3_.refs_6_), channel_id=1, source_target_pairs={{0,1},{2,3},{1,0},{3,2},{4,5},{6,7},{5,4},{7,6},{8,9},{10,11},{9,8... | collective-permute-start | bytes 1572872 | tf_op jit(solution)/shard_map/ppermute | solution.py:484
  69.9 23.9 %collective-permute-start.9 = (f32[1024,128]{1,0:T(8,128)}, f32[1024,128]{1,0:T(8,128)}, u32[]{:S(2)}, u32[]{:S(2)}) collective-permute-start(f32[1024,128]{1,0:T(8,128)} %get-tuple-element.55.refs_8_.refs_5_), channel_id=1, source_target_pairs={{0,1},{2,3},{1,0},{3,2},{4,5},{6,7},{5,4},{7,6},{8,9},{10,11},{9,8... | collective-permute-start | bytes 1572872 | tf_op jit(solution)/shard_map/ppermute | solution.py:484
  72.1 49.4 %collective-permute-start.15 = (f32[1024,256]{1,0:T(8,128)}, f32[1024,256]{1,0:T(8,128)S(1)}, u32[]{:S(2)}, u32[]{:S(2)}) collective-permute-start(f32[1024,256]{1,0:T(8,128)} %collective-permute-done.8.refs_4_), channel_id=1, source_target_pairs={{2,3},{1,0},{6,7},{5,4},{10,11},{9,8},{14,15},{13,12},{18,19},{17,... | collective-permute-start | bytes 3145736 | tf_op jit(solution)/shard_map/ppermute | solution.py:566
  96.0 23.5 %collective-permute-start.16 = (f32[1024,256]{1,0:T(8,128)}, f32[1024,256]{1,0:T(8,128)S(1)}, u32[]{:S(2)}, u32[]{:S(2)}) collective-permute-start(f32[1024,256]{1,0:T(8,128)} %get-tuple-element.59.refs_1_), channel_id=1, source_target_pairs={{1,2},{2,1},{5,6},{6,5},{9,10},{10,9},{13,14},{14,13},{17,18},{18,... | collective-permute-start | bytes 3145736 | tf_op jit(solution)/shard_map/ppermute | solution.py:484
  110.3 14.9 %collective-permute-start.12 = (f32[1024,256]{1,0:T(8,128)}, f32[1024,256]{1,0:T(8,128)S(1)}, u32[]{:S(2)}, u32[]{:S(2)}) collective-permute-start(f32[1024,256]{1,0:T(8,128)} %get-tuple-element.59.refs_1_), channel_id=1, source_target_pairs={{0,4},{8,12},{4,0},{12,8},{1,5},{9,13},{5,1},{13,9},{2,6},{10,14},... | collective-permute-start | bytes 3145736 | tf_op jit(solution)/shard_map/ppermute | solution.py:484
  110.8 25.4 %collective-permute-start.13 = (f32[1024,256]{1,0:T(8,128)}, f32[1024,256]{1,0:T(8,128)S(1)}, u32[]{:S(2)}, u32[]{:S(2)}) collective-permute-start(f32[1024,256]{1,0:T(8,128)} %get-tuple-element.59.refs_1_), channel_id=1, source_target_pairs={{4,8},{12,0},{8,4},{0,12},{5,9},{13,1},{9,5},{1,13},{6,10},{14,2},... | collective-permute-start | bytes 3145736 | tf_op jit(solution)/shard_map/ppermute | solution.py:484
  119.6 28.3 %collective-permute-start.19 = (f32[1024,256]{1,0:T(8,128)S(1)}, f32[1024,256]{1,0:T(8,128)S(1)}, u32[]{:S(2)}, u32[]{:S(2)}) collective-permute-start(f32[1024,256]{1,0:T(8,128)S(1)} %get-tuple-element.60.refs_4_), channel_id=1, source_target_pairs={{1,2},{2,1},{5,6},{6,5},{9,10},{10,9},{13,14},{14,13},{17,18},{18,... | collective-permute-start | bytes 3145736 | tf_op jit(solution)/shard_map/ppermute | solution.py:484
  121.5 26.4 %collective-permute-start.18 = (f32[1024,256]{1,0:T(8,128)S(1)}, f32[1024,256]{1,0:T(8,128)S(1)}, u32[]{:S(2)}, u32[]{:S(2)}) collective-permute-start(f32[1024,256]{1,0:T(8,128)S(1)} %collective-permute-done.16.refs_4_.refs_6_), channel_id=1, source_target_pairs={{2,3},{1,0},{6,7},{5,4},{10,11},{9,8},{14,15},{13,12},{18,19},{17,... | collective-permute-start | bytes 3145736 | tf_op jit(solution)/shard_map/ppermute | solution.py:576
  161.7 27.6 %collective-permute-start.21 = (f32[1024,256]{1,0:T(8,128)S(1)}, f32[1024,256]{1,0:T(8,128)S(1)}, u32[]{:S(2)}, u32[]{:S(2)}) collective-permute-start(f32[1024,256]{1,0:T(8,128)S(1)} %join.3.refs_6_), channel_id=1, source_target_pairs={{1,2},{2,1},{5,6},{6,5},{9,10},{10,9},{13,14},{14,13},{17,18},{18,... | collective-permute-start | bytes 3145736 | tf_op jit(solution)/shard_map/ppermute | solution.py:484
  164.8 28.7 %collective-permute-start.22 = (f32[512,512]{1,0:T(8,128)S(1)}, f32[512,512]{1,0:T(8,128)S(1)}, u32[]{:S(2)}, u32[]{:S(2)}) collective-permute-start(f32[512,512]{1,0:T(8,128)S(1)} %add.41.refs_11_), channel_id=1, source_target_pairs={{8,0},{12,4},{9,1},{13,5},{2,10},{6,14},{3,11},{7,15},{24,16},{28,... | collective-permute-start | bytes 3145736 | tf_op jit(solution)/shard_map/ppermute | solution.py:564
  167.5 26.0 %collective-permute-start.26 = (f32[1024,256]{1,0:T(8,128)S(1)}, f32[1024,256]{1,0:T(8,128)S(1)}, u32[]{:S(2)}, u32[]{:S(2)}) collective-permute-start(f32[1024,256]{1,0:T(8,128)S(1)} %collective-permute-done.19.refs_4_), channel_id=1, source_target_pairs={{2,3},{1,0},{6,7},{5,4},{10,11},{9,8},{14,15},{13,12},{18,19},{17,... | collective-permute-start | bytes 3145736 | tf_op jit(solution)/shard_map/ppermute | solution.py:589
  169.3 59.4 %collective-permute-start.25 = (f32[1024,512]{1,0:T(8,128)S(1)}, f32[1024,512]{1,0:T(8,128)S(1)}, u32[]{:S(2)}, u32[]{:S(2)}) collective-permute-start(f32[1024,512]{1,0:T(8,128)S(1)} %add.45.refs_7_), channel_id=1, source_target_pairs={{0,8},{1,9},{14,6},{15,7},{16,24},{17,25},{30,22},{31,23}} | collective-permute-start | bytes 6291464 | tf_op jit(solution)/shard_map/ppermute | solution.py:502
  199.3 25.7 %collective-permute-start.23 = (f32[512,512]{1,0:T(8,128)S(1)}, f32[512,512]{1,0:T(8,128)S(1)}, u32[]{:S(2)}, u32[]{:S(2)}) collective-permute-start(f32[512,512]{1,0:T(8,128)S(1)} %add.42.refs_9_), channel_id=1, source_target_pairs={{8,0},{12,4},{9,1},{13,5},{2,10},{6,14},{3,11},{7,15},{24,16},{28,... | collective-permute-start | bytes 3145736 | tf_op jit(solution)/shard_map/ppermute | solution.py:564
  203.7 25.1 %collective-permute-start.30 = (f32[1024,128]{1,0:T(8,128)S(1)}, f32[1024,128]{1,0:T(8,128)S(1)}, u32[]{:S(2)}, u32[]{:S(2)}) collective-permute-start(f32[1024,128]{1,0:T(8,128)S(1)} %get-tuple-element.73.refs_4_), channel_id=1, source_target_pairs={{2,3},{1,0},{6,7},{5,4},{10,11},{9,8},{14,15},{13,12},{18,19},{17,... | collective-permute-start | bytes 1572872 | tf_op jit(solution)/shard_map/ppermute | solution.py:589
  205.1 36.6 %collective-permute-start.32 = (f32[1024,256]{1,0:T(8,128)S(1)}, f32[1024,256]{1,0:T(8,128)}, u32[]{:S(2)}, u32[]{:S(2)}) collective-permute-start(f32[1024,256]{1,0:T(8,128)S(1)} %add.47.refs_7_.refs_2_), channel_id=1, source_target_pairs={{4,12},{5,13},{10,2},{11,3},{20,28},{21,29},{26,18},{27,19}} | collective-permute-start | bytes 3145736 | tf_op jit(solution)/shard_map/ppermute | solution.py:502
  (42 other events, 328.2 us)
where the time goes:
time: 255 us; the launch traced here: 254 us
  waiting for transfers between devices  108 us (42%)
  Pallas kernels  80.3 us (31%)
  starting transfers between devices  42.5 us (17%)
  local copies, waits for them, and re-layouts  13.9 us (5%)
  other arithmetic  8.17 us (3%)
    pallas_call x19, Pallas kernels, call(): return lambda *args: made(*args, *extra)  80.3 us
    ppermute x19, waiting for transfers between devices, exchange(): return lax.ppermute(block, axis, pairs + [(b, a) for a, b in pairs])  70.2 us
    ppermute x19, starting transfers between devices, exchange(): return lax.ppermute(block, axis, pairs + [(b, a) for a, b in pairs])  19.1 us
    unnamed x62, local copies, waits for them, and re-layouts  13.8 us
    ppermute x8, starting transfers between devices, to_owner(): return lax.ppermute(block, ('dom', 'band'), route)  10.7 us
    ppermute x1, waiting for transfers between devices, on_device(): lax.ppermute(own, 'dom', [(i, (i + 1) % domains) for i in range(domains)])  9.91 us
    ppermute x2, waiting for transfers between devices, near(): return (kept, lax.ppermute(kept, ('dom', 'band'), near_route), first)  9.34 us
    ppermute x3, waiting for transfers between devices, on_device(): third_out = [lax.ppermute(x, 'band', outward) for x in third_pieces]  9.27 us
  transfers between devices with their start and end apart: 35, of which 16 were waited for; matrix products, arithmetic and copies ran while one was open for 2% of the time, Pallas kernels for 26%

commit v1 on v0

--- a/solution.py
+++ b/solution.py
@@ -23,7 +23,7 @@
 PARAMS = pltpu.CompilerParams(vmem_limit_bytes=32 * 1024 * 1024)
 
 
-COST = pl.CostEstimate(flops=1, bytes_accessed=1, transcendentals=0)
+COST = pl.CostEstimate(flops=10**12, bytes_accessed=1, transcendentals=0)
 
 
 def element_table():
@@ -45,17 +45,34 @@
     return lax.dot_general(a, b, (((1,), (0,)), ((), ())), preferred_element_type=jnp.float32)
 
 
-def call(kernel, after, *, in_specs, name, into=(), **options):
+def corner(x):
+    rows = 32 // x.dtype.itemsize
+    return pl.BlockSpec((rows, 128), lambda *_: (0, 0))
+
+
+def call(kernel, after, *, in_specs, out_specs, out_shape, name, into=(), passed=(), **options):
     count = len(in_specs)
-    extra = [*[array for _, array in into], *after]
+    extra = [*[array for _, array in into], *passed, *after]
+    aliases = {count + at: out for at, (out, _) in enumerate(into)}
+    outs = len(out_shape) if isinstance(out_shape, (list, tuple)) else 1
+    if passed:
+        out_specs = [*out_specs, *map(corner, passed)]
+        out_shape = [*out_shape, *[jax.ShapeDtypeStruct(x.shape, x.dtype) for x in passed]]
+        aliases |= {count + len(into) + at: outs + at for at in range(len(passed))}
 
     def body(*refs):
-        kernel(*refs[:count], *refs[count + len(extra) :])
+        rest = refs[count + len(extra) :]
+        kernel(*refs[:count], *rest[:outs], *rest[outs + len(passed) :])
+        first = count + len(into)
+        for x_ref, out_ref in zip(refs[first : first + len(passed)], rest[outs : outs + len(passed)]):
+            out_ref[...] = x_ref[...]
 
     made = pl.pallas_call(
         body,
-        in_specs=[*in_specs, *[pl.BlockSpec(memory_space=pl.ANY)] * len(extra)],
-        input_output_aliases={count + at: out for at, (out, _) in enumerate(into)},
+        in_specs=[*in_specs, *map(corner, extra)],
+        out_specs=out_specs,
+        out_shape=out_shape,
+        input_output_aliases=aliases,
         compiler_params=PARAMS,
         cost_estimate=COST,
         name=name,
@@ -64,39 +81,37 @@
     return lambda *args: made(*args, *extra)
 
 
-def join_kernel(left_ref, right_ref, out_ref, *passed):
-    width = left_ref.shape[1]
-    out_ref[:, :width] = left_ref[...]
-    out_ref[:, width:] = right_ref[...]
-
-
-def join(left, right, after, passed=()):
-    nodes, width = left.shape
-    rows = 256
-    part = pl.BlockSpec((rows, width), lambda i: (i, 0))
-    return call(
-        join_kernel,
-        after,
-        into=[(1 + at, x) for at, x in enumerate(passed)],
-        grid=(nodes // rows,),
+def gate(arrays, after):
+    return call(lambda: None, after, passed=arrays, grid=(1,), in_specs=[], out_specs=[], out_shape=[], name="gate")()
+
+
+def plus_kernel(left_ref, right_ref, out_ref):
+    out_ref[...] = left_ref[...] + right_ref[...]
+
+
+def plus(left, right, after, passed=()):
+    rows = min(512, left.shape[0])
+    part = pl.BlockSpec((rows, left.shape[1]), lambda i: (i, 0))
+    return call(
+        plus_kernel,
+        after,
+        grid=(left.shape[0] // rows,),
         in_specs=[part, part],
-        out_specs=[pl.BlockSpec((rows, 2 * width), lambda i: (i, 0))]
-        + [pl.BlockSpec(memory_space=pl.ANY)] * len(passed),
-        out_shape=[jax.ShapeDtypeStruct((nodes, 2 * width), left.dtype)]
-        + [jax.ShapeDtypeStruct(x.shape, x.dtype) for x in passed],
-        name="join",
+        out_specs=[part],
+        out_shape=[jax.ShapeDtypeStruct(left.shape, left.dtype)],
+        passed=passed,
+        name="plus",
     )(left, right)
 
 
-def to_grid_kernel(offsets, map_ref, x_ref, *refs):
-    whole_ref, outs, (high_ref, low_ref) = refs[0], refs[1:-2], refs[-2:]
+def to_grid_kernel(map_ref, x_ref, out_ref, whole_ref, high_ref, low_ref):
     step = pl.program_id(0)
 
     @pl.when(step == 0)
     def _():
         high_ref[...], low_ref[...] = halves(x_ref[...])
 
-    rows, nodes = whole_ref.shape[0], x_ref.shape[0]
+    rows, nodes = out_ref.shape[0], x_ref.shape[0]
     place = lax.broadcasted_iota(jnp.int32, (BLOCK, nodes), 1)
     for at in range(rows // BLOCK):
         row = map_ref[pl.ds(step * (rows // BLOCK) + at, 1), :]
@@ -105,62 +120,63 @@
         pick = jnp.where(place == column, 1.0, 0.0).astype(jnp.bfloat16)
         moved = dot(pick, high_ref[...]) + dot(pick, low_ref[...])
         out = slice(at * BLOCK, (at + 1) * BLOCK)
+        out_ref[out, :] = moved
         whole_ref[out, :] = moved
-        for first, out_ref in zip(offsets, outs):
-            out_ref[out, :] = moved[:, first : first + out_ref.shape[1]]
-
-
-def to_grid(face_map, x, first, width, widths=(), after=()):
-    nodes = x.shape[0]
+
+
+def to_grid(face_map, x, at, width, so_far, after):
+    nodes, states = x.shape
     rows = 512
-    offsets = tuple(sum(widths[:at]) for at in range(len(widths)))
-    sizes = (width, *widths)
-    at = first // width
-    return call(
-        functools.partial(to_grid_kernel, offsets),
-        after,
+    return call(
+        to_grid_kernel,
+        after,
+        into=[(1, so_far)] if at else [],
         grid=(nodes // rows,),
         in_specs=[
             pl.BlockSpec((nodes // BLOCK, BLOCK), lambda i: (0, 0)),
             pl.BlockSpec((nodes, width), lambda i: (0, at)),
         ],
-        out_specs=[pl.BlockSpec((rows, size), lambda i: (i, 0)) for size in sizes],
-        out_shape=[jax.ShapeDtypeStruct((nodes, size), jnp.float32) for size in sizes],
+        out_specs=[pl.BlockSpec((rows, width), lambda i: (i, 0)), pl.BlockSpec((rows, width), lambda i: (i, at))],
+        out_shape=[
+            jax.ShapeDtypeStruct((nodes, width), jnp.float32),
+            jax.ShapeDtypeStruct((nodes, states), jnp.float32),
+        ],
         scratch_shapes=[pltpu.VMEM((nodes, width), jnp.bfloat16)] * 2,
         name="to_grid",
     )(face_map.reshape(nodes // BLOCK, BLOCK), x)
 
 
-def from_grid_kernel(map_ref, *refs):
-    pieces, (out_ref, high_ref, low_ref) = refs[:-3], refs[-3:]
+def from_grid_kernel(map_ref, x_ref, out_ref, again_ref, half_ref, high_ref, low_ref):
     step = pl.program_id(0)
 
     @pl.when(step == 0)
     def _():
-        split_columns([[x] for x in pieces], high_ref, low_ref, 0)
+        high_ref[...], low_ref[...] = halves(x_ref[...])
 
     rows, nodes = out_ref.shape[0], high_ref.shape[0]
     node = lax.broadcasted_iota(jnp.int32, (rows, nodes), 0) + step * rows
     pick = jnp.where(node == map_ref[...], 1.0, 0.0).astype(jnp.bfloat16)
     out_ref[...] = dot(pick, high_ref[...]) + dot(pick, low_ref[...])
-
-
-def from_grid(face_map, pieces, at, states, so_far=None, after=()):
-    nodes = pieces[0].shape[0]
-    width = sum(x.shape[1] for x in pieces)
+    again = x_ref[pl.ds(pl.multiple_of(step * rows, rows), rows), :]
+    again_ref[...] = again
+    half_ref[...] = again[:, half_ref.shape[1] :]
+
+
+def from_grid(face_map, x, after=(), passed=()):
+    nodes, states = x.shape
     rows = 256
+    part = pl.BlockSpec((rows, states), lambda i: (i, 0))
     return call(
         from_grid_kernel,
         after,
-        into=[(0, so_far)] if at else [],
+        passed=passed,
         grid=(nodes // rows,),
-        in_specs=[pl.BlockSpec((1, nodes), lambda i: (0, 0))]
-        + [pl.BlockSpec(x.shape, lambda i: (0, 0)) for x in pieces],
-        out_specs=pl.BlockSpec((rows, width), lambda i: (i, at)),
-        out_shape=jax.ShapeDtypeStruct((nodes, states), jnp.float32),
-        scratch_shapes=[pltpu.VMEM((nodes, width), jnp.bfloat16)] * 2,
+        in_specs=[pl.BlockSpec((1, nodes), lambda i: (0, 0)), pl.BlockSpec((nodes, states), lambda i: (0, 0))],
+        out_specs=[part, part, pl.BlockSpec((rows, states // 2), lambda i: (i, 0))],
+        out_shape=[jax.ShapeDtypeStruct((nodes, size), jnp.float32) for size in (states, states, states // 2)],
+        scratch_shapes=[pltpu.VMEM((nodes, states), jnp.bfloat16)] * 2,
         name="from_grid",
-    )(face_map.reshape(1, nodes), *pieces)
+    )(face_map.reshape(1, nodes), x)
 
 
 def plane_terms(shifted, stiff, layer):
@@ -266,15 +282,18 @@
     )
 
 
-def apply_kernel(filtered, band_ref, own_ref, paired_ref, far_ref, *refs):
-    wide = refs[-1]
+def apply_kernel(filtered, pieces, band_ref, own_ref, paired_ref, *refs):
+    far_refs, refs, wide = refs[:pieces], refs[pieces:], refs[-1]
     step = pl.program_id(0)
     nodes, width = own_ref.shape
 
     @pl.when(step == 0)
     def _():
-        for plane, ref in enumerate((own_ref, paired_ref, far_ref)):
-            for columns, part in zip((slice(0, width), slice(width, 2 * width)), halves(ref[...])):
+        sources = [(0, 0, own_ref), (1, 0, paired_ref)]
+        sources += [(2, at * width // pieces, ref) for at, ref in enumerate(far_refs)]
+        for plane, first, ref in sources:
+            for start, part in zip((first, width + first), halves(ref[...])):
+                columns = slice(start, start + part.shape[1])
                 wide[plane, pl.ds(MARGIN, nodes), columns] = part
                 wide[plane, pl.ds(0, MARGIN), columns] = part[nodes - MARGIN :]
                 wide[plane, pl.ds(MARGIN + nodes, MARGIN), columns] = part[:MARGIN]
@@ -291,11 +310,11 @@
         total = total[:, :width] + total[:, width:]
         rows = pl.ds(at * BLOCK, BLOCK)
         if filtered:
-            last_ref, out_ref, joined_ref, turned_high, turned_low = refs[:5]
+            last_ref, out_ref, whole_ref, turned_high, turned_low = refs[:5]
             mine = own_ref[pl.ds(first, BLOCK), :]
             total = (2.0 / half_width) * (total - centre * mine) - last_ref[rows, :]
             out_ref[rows, :] = total
-            joined_ref[rows, :] = total
+            whole_ref[rows, :] = total
         else:
             turned_high, turned_low = refs[:2]
         turned_high[:, rows], turned_low[:, rows] = halves(total.T)
@@ -311,30 +330,23 @@
     ), pl.BlockSpec((3, per_step, 2 * BLOCK, WINDOW), lambda i: (0, i, 0, 0)), rows
 
 
-def next_degree(band, own, paired, far, last, half, at, so_far, after):
+def next_degree(band, own, paired, far, last, at, so_far, after):
     nodes, width = far.shape
     states = own.shape[1]
     options, band_spec, rows = apply_specs(nodes, width)
-    inside = at % (half // width)
     column = pl.BlockSpec((nodes, width), lambda i: (0, at))
     part = pl.BlockSpec((rows, width), lambda i: (i, at))
     turned = pl.BlockSpec((width, rows), lambda i: (at, i))
     turned_shape = jax.ShapeDtypeStruct((states, nodes), jnp.bfloat16)
-    into = [(out, so_far[out - 1]) for out in (1, 2, 3) if (inside if out == 1 else at)]
-    return call(
-        functools.partial(apply_kernel, True),
-        after,
-        into=into,
+    return call(
+        functools.partial(apply_kernel, True, 1),
+        after,
+        into=[(out, so_far[out - 1]) for out in (1, 2, 3) if at],
         in_specs=[band_spec, column, column, pl.BlockSpec((nodes, width), lambda i: (0, 0)), part],
-        out_specs=[
-            pl.BlockSpec((rows, width), lambda i: (i, 0)),
-            pl.BlockSpec((rows, width), lambda i: (i, inside)),
-            turned,
-            turned,
-        ],
+        out_specs=[pl.BlockSpec((rows, width), lambda i: (i, 0)), part, turned, turned],
         out_shape=[
             jax.ShapeDtypeStruct((nodes, width), jnp.float32),
-            jax.ShapeDtypeStruct((nodes, half), jnp.float32),
+            jax.ShapeDtypeStruct((nodes, states), jnp.float32),
             turned_shape,
             turned_shape,
         ],
@@ -342,21 +354,20 @@
     )(band, own, paired, far, last)
 
 
-def applied_next(band, own, paired, far, states, at, so_far, after=()):
-    nodes, width = far.shape
-    options, band_spec, rows = apply_specs(nodes, width)
-    whole = pl.BlockSpec((nodes, width), lambda i: (0, 0))
-    turned = pl.BlockSpec((width, rows), lambda i: (at, i))
+def applied_next(band, own, paired, far, after=()):
+    nodes, states = own.shape
+    options, band_spec, rows = apply_specs(nodes, states)
+    whole = pl.BlockSpec((nodes, states), lambda i: (0, 0))
+    turned = pl.BlockSpec((states, rows), lambda i: (0, i))
     turned_shape = jax.ShapeDtypeStruct((states, nodes), jnp.bfloat16)
     return call(
-        functools.partial(apply_kernel, False),
-        after,
-        into=[(out, so_far[out]) for out in (0, 1) if at],
-        in_specs=[band_spec, whole, whole, whole],
+        functools.partial(apply_kernel, False, len(far)),
+        after,
+        in_specs=[band_spec, whole, whole] + [pl.BlockSpec(x.shape, lambda i: (0, 0)) for x in far],
         out_specs=[turned, turned],
         out_shape=[turned_shape, turned_shape],
         **options,
-    )(band, own, paired, far)
+    )(band, own, paired, *far)
 
 
 def split_columns(pieces, high_ref, low_ref, first):
@@ -394,17 +405,20 @@
     sent_ref[...] = total[:, width:]
 
 
-def sorted_products(keep, turned, own, first, after=()):
+def sorted_products(keep, turned, own, first, at, so_far, after=(), passed=()):
     states, nodes = turned[0].shape
     rows = 256
+    steps = states // rows
     width = sum(piece.shape[1] for piece in own)
     left = pl.BlockSpec((rows, nodes), lambda i: (i, 0))
-    out = pl.BlockSpec((rows, width), lambda i: (i, 0))
-    shape = jax.ShapeDtypeStruct((states, width), jnp.float32)
+    out = pl.BlockSpec((rows, width), lambda i: (i + at * steps, 0))
+    shape = jax.ShapeDtypeStruct((2 * states, width), jnp.float32)
     return call(
         functools.partial(sorted_kernel, len(own)),
         after,
-        grid=(states // rows,),
+        into=list(enumerate(so_far)) if at else [],
+        passed=passed,
+        grid=(steps,),
         in_specs=[pl.BlockSpec(memory_space=pltpu.SMEM), left, left]
         + [pl.BlockSpec(piece.shape, lambda i: (0, 0)) for piece in (*own, *first)],
         out_specs=[out, out],
@@ -432,7 +446,7 @@
         out_ref[...] = rows_product(more_high, more_low, high_ref, low_ref)
 
 
-def both_products(y_turned, h_turned, pieces, summed=1, after=()):
+def both_products(y_turned, h_turned, pieces, summed=1, after=(), passed=()):
     states, nodes = y_turned[0].shape
     rows = 256
     steps = states // rows
@@ -445,39 +459,109 @@
         grid=(2 * steps,),
         in_specs=[first, first, second, second]
         + [pl.BlockSpec(piece.shape, lambda i: (0, 0)) for piece in pieces],
-        out_specs=pl.BlockSpec((rows, width), lambda i: (i, 0)),
-        out_shape=jax.ShapeDtypeStruct((2 * states, width), jnp.float32),
+        out_specs=[pl.BlockSpec((rows, width), lambda i: (i, 0))],
+        out_shape=[jax.ShapeDtypeStruct((2 * states, width), jnp.float32)],
+        passed=passed,
         scratch_shapes=[pltpu.VMEM((nodes, width), jnp.bfloat16)] * 2,
         name="both_products",
     )(*y_turned, *h_turned, *pieces)
 
 
-def finish_kernel(weight, count, states, flag_ref, base_ref, *refs):
-    sums, arrived = refs[:count], refs[count : 2 * count]
-    margin_ref, projected_ref = refs[2 * count :]
-    mine = jnp.where(flag_ref[0] == 1, 1.0, 0.0)
-    for half, out_ref in enumerate((margin_ref, projected_ref)):
+def pair_kernel(keep_ref, left_high, left_low, more_high, more_low, block_ref, piece_ref, other_ref, *refs):
+    kept_ref, sent_ref, high_ref, low_ref = refs
+    step, half = pl.program_id(0), pl.num_programs(0) // 2
+
+    @pl.when(step == 0)
+    def _():
+        split_columns([[piece_ref, other_ref]], high_ref, low_ref, 0)
+
+    def write(total):
+        keeps = keep_ref[0] == 1
+        kept_ref[...] = jnp.where(keeps, block_ref[...], total)
+        sent_ref[...] = jnp.where(keeps, total, block_ref[...])
+
+    @pl.when(step < half)
+    def _():
+        write(rows_product(left_high, left_low, high_ref, low_ref))
+
+    @pl.when(step >= half)
+    def _():
+        write(rows_product(more_high, more_low, high_ref, low_ref))
+
+
+def pair_products(keep, y_turned, h_turned, block, piece, other, after):
+    states, nodes = y_turned[0].shape
+    rows = 256
+    steps = states // rows
+    width = piece.shape[1]
+    first = pl.BlockSpec((rows, nodes), lambda i: (jnp.minimum(i, steps - 1), 0))
+    second = pl.BlockSpec((rows, nodes), lambda i: (jnp.maximum(i - steps, 0), 0))
+    whole = pl.BlockSpec((nodes, width), lambda i: (0, 0))
+    out = pl.BlockSpec((rows, width), lambda i: (i, 0))
+    return call(
+        pair_kernel,
+        after,
+        grid=(2 * steps,),
+        in_specs=[pl.BlockSpec(memory_space=pltpu.SMEM), first, first, second, second, out, whole, whole],
+        out_specs=[out, out],
+        out_shape=[jax.ShapeDtypeStruct((2 * states, width), jnp.float32)] * 2,
+        scratch_shapes=[pltpu.VMEM((nodes, width), jnp.bfloat16)] * 2,
+        name="pair_products",
+    )(keep, *y_turned, *h_turned, block, piece, other)
+
+
+def near_kernel(flags_ref, mine_ref, arrived_ref, out_ref):
+    out_ref[...] = jnp.where(flags_ref[0] == 1, 1.0, 0.0) * (mine_ref[...] + arrived_ref[...])
+
+
+def near_rows(flags, mine, arrived, after):
+    whole = pl.BlockSpec(mine.shape, lambda i: (0, 0))
+    return call(
+        near_kernel,
+        after,
+        grid=(1,),
+        in_specs=[pl.BlockSpec(memory_space=pltpu.SMEM), whole, whole],
+        out_specs=whole,
+        out_shape=jax.ShapeDtypeStruct(mine.shape, jnp.float32),
+        name="near_rows",
+    )(flags, mine, arrived)
+
+
+def mark(after):
+    shape = jax.ShapeDtypeStruct((8, 128), jnp.float32)
+
+    def kernel(out_ref):
+        out_ref[...] = jnp.zeros_like(out_ref)
+
+    return call(kernel, after, in_specs=[], grid=(1,), out_specs=corner(shape), out_shape=shape, name="mark")()
+
+
+def finish_kernel(weight, flags_ref, base_ref, one_ref, one_far, two_ref, two_far, *outs):
+    one, two = [jnp.where(flags_ref[band] == 1, 1.0, 0.0) for band in (1, 2)]
+    states = outs[0].shape[0]
+    for half, out_ref in enumerate(outs):
         rows = slice(half * states, (half + 1) * states)
-        first = 0
-        for block, other in zip(sums, arrived):
-            columns = slice(first, first + block.shape[1])
-            first += block.shape[1]
-            total = base_ref[rows, columns] + mine * block[rows, :] + other[rows, :]
-            out_ref[:, columns] = weight * total
-
-
-def finish(weight, flag, base, sums, arrived):
-    states = base.shape[0] // 2
+        total = base_ref[rows, :] + one * (one_ref[rows, :] + one_far[rows, :])
+        out_ref[...] = weight * (total + two * (two_ref[rows, :] + two_far[rows, :]))
+
+
+def finish(weight, at, flags, base, one, one_far, two, two_far, so_far, after):
+    rows, width = one.shape
+    states = rows // 2
+    whole = pl.BlockSpec((rows, width), lambda i: (0, 0))
+    part = pl.BlockSpec((states, width), lambda i: (0, at))
     shape = jax.ShapeDtypeStruct((states, base.shape[1]), jnp.float32)
     return call(
-        functools.partial(finish_kernel, weight, len(sums), states),
-        (),
-        in_specs=[pl.BlockSpec(memory_space=pltpu.SMEM)]
-        + [pl.BlockSpec(memory_space=pltpu.VMEM)] * (1 + 2 * len(sums)),
-        out_specs=[pl.BlockSpec(memory_space=pltpu.VMEM)] * 2,
+        functools.partial(finish_kernel, weight),
+        after,
+        into=[(out, x) for out, x in enumerate(so_far)],
+        grid=(1,),
+        in_specs=[pl.BlockSpec(memory_space=pltpu.SMEM), pl.BlockSpec((rows, width), lambda i: (0, at))]
+        + [whole] * 4,
+        out_specs=[part, part],
         out_shape=[shape, shape],
         name="finish",
-    )(flag, base, *sums, *arrived)
+    )(flags, base, one, one_far, two, two_far)
 
 
 def exchange(block, axis, pairs):
@@ -509,7 +593,6 @@
     me, level = lax.axis_index("dom"), lax.axis_index("band")
     swaps = domains == 4 and band_count == 4 and states == STATES_DEV
     half = states // 2
-    quarter = states // 4 if swaps else half
     place = jnp.arange(nodes, dtype=jnp.int32)
     cell_place = connect[:, 4] - nodes
     own = jnp.sum(jnp.where(cell_place[:, None] == place[None, :], elem_scale[:, None], 0.0), axis=0)
@@ -518,33 +601,28 @@
     odd = (me % 2).astype(jnp.int32).reshape(1)
     weight = 1.0 / (nodes * domains)
 
-    current, *chunks = to_grid(face_map, y_cur, 0, states, (quarter,) * (states // quarter), after=(own,))
+    far, current, waited = [], None, ()
+    for at in (0, 1):
+        chunk, current = to_grid(face_map, y_cur, at, half, current, waited)
+        far.append(crossed(chunk))
+        waited = (chunk,)
     current_paired = paired(current)
-    far = [crossed(chunk) for chunk in chunks]
     band, last = prepare(stiff, odd, own, before, at_grid, face_map, y_prev, (current,))
 
-    following, pair_step, joined, middle_step = [], [], [], []
-    so_far, waited = [None] * 3, ()
+    following, so_far, waited = [], [None] * 3, ()
     for at, piece in enumerate(far):
-        sources = (band, current, current_paired, piece, last, half, at)
-        chunk, *so_far = next_degree(*sources, so_far, waited)
+        chunk, *so_far = next_degree(band, current, current_paired, piece, last, at, so_far, waited)
         following.append(chunk)
-        waited = (chunk, *pair_step[at - 1 : at]) if at else (chunk,)
-        if (at + 1) * quarter % half == 0:
-            joined.append(so_far[0])
-        if swaps:
-            pair_step.append(exchange(chunk, "band", [(0, 1), (2, 3)]))
-            if at == 1:
-                middle_step.append(exchange(joined[0], "band", [(1, 2)]))
-    y_turned = so_far[1:]
+        waited = (chunk,)
+    whole, *y_turned = so_far
+    next_far = [crossed(following[0])]
 
     if not swaps:
-        y_next = from_grid(face_map, joined, 0, states)
-        h_turned = [None] * 2
-        for at, piece in enumerate(joined):
-            h_turned = applied_next(band, piece, paired(piece), crossed(piece), states, at, h_turned)
-        piece = lax.all_gather(jnp.concatenate(joined, axis=1), "band", axis=1, tiled=True)
-        block = both_products(y_turned, h_turned, [piece])
+        y_next, again, other = from_grid(face_map, whole)
+        next_far.append(crossed(other))
+        h_turned = applied_next(band, whole, paired(again), next_far)
+        piece = lax.all_gather(whole, "band", axis=1, tiled=True)
+        (block,) = both_products(y_turned, h_turned, [piece])
         parts = [
             weight * lax.psum_scatter(rows, "dom", scatter_dimension=1, tiled=True)
             for rows in (block[:states], block[states:])
@@ -557,52 +635,55 @@
     near_route = [
         (((b // 2 * 2 + c) ^ 2) * 4 + b, (b // 2 * 2 + c) * 4 + b) for b in range(4) for c in (0, 1)
     ]
-
-    def near(rows, after):
-        first, sent = sorted_products(keep, rows, following, pair_step, after)
-        kept = first + paired(sent)
-        return kept, lax.ppermute(kept, ("dom", "band"), near_route), first
-
-    second_out = [lax.ppermute(middle_step[0], "band", outward)]
-    near_paired = paired(joined[0])
-    waited = (following[3], middle_step[0], *pair_step[2:], near_paired)
-    far_pair, later = join(*pair_step[:2], waited, (joined[1],))
-    middle_step.append(exchange(later, "band", [(1, 2)]))
-    third_middle = [exchange(far_pair, "band", [(1, 2)])]
-    sources = (joined[0], near_paired, crossed(joined[0]))
-    h_turned = applied_next(band, *sources, states, 0, None, (far_pair,))
-    near_margin = near(y_turned, (h_turned[0],))
-    (far_pair,) = join(*pair_step[2:], (near_margin[2], second_out[0], middle_step[1]))
-    second_out.append(lax.ppermute(middle_step[1], "band", outward))
-    third_middle.append(exchange(far_pair, "band", [(1, 2)]))
-    sources = (later, paired(later), crossed(later))
-    h_turned = applied_next(band, *sources, states, 1, h_turned, (far_pair,))
-    near_projected = near(h_turned, (near_margin[0],))
-    waited = (near_projected[2], second_out[1], third_middle[0])
-    y_next = from_grid(face_map, [joined[0]], 0, states, None, waited)
-
+    near_across = lambda x: lax.ppermute(x, ("dom", "band"), near_route)
     second_owner, third_owner = [2, 2, 1, 1], [3, 3, 0, 0]
-    pieces = [x for pair in zip(middle_step, second_out) for x in pair]
-    second = both_products(y_turned, h_turned, pieces, 2, (y_next, near_projected[0]))
-    y_next = from_grid(face_map, [later], 1, states, y_next, (second, third_middle[1]))
-    third_pieces = [third_middle[0], third_middle[1][:, :quarter], third_middle[1][:, quarter:]]
-    third_out = [lax.ppermute(x, "band", outward) for x in third_pieces]
-    waited = (y_next, near_margin[1])
-    second = second + to_owner(second, second_owner, 1)
+
+    ends, middle = [(0, 1), (2, 3)], [(1, 2)]
+    first = [exchange(x, "band", ends) for x in following]
+    second_middle = [exchange(x, "band", middle) for x in following]
+    waited = (first[0], second_middle[0], next_far[0])
+    y_next, again, other, second_middle[0] = from_grid(face_map, whole, waited, second_middle[:1])
+    next_far.append(crossed(other))
+    second_out = [lax.ppermute(second_middle[0], "band", outward)]
+    whole_paired = paired(again)
+    (first[0],) = gate(first[:1], (mark((y_next,)), whole_paired, second_middle[1]))
+    third_middle = [exchange(first[0], "band", middle)]
+    *near, second_middle[1] = sorted_products(keep, y_turned, following, first, 0, (), (), second_middle[1:])
+    second_out.append(lax.ppermute(second_middle[1], "band", outward))
+    h_turned = applied_next(band, whole, whole_paired, next_far, (near[0],))
+    (first[1],) = gate(first[1:], (h_turned[0], third_middle[0]))
+    third_middle.append(exchange(first[1], "band", middle))
+    kept, sent, third_middle[0] = sorted_products(keep, h_turned, following, first, 1, near, (), third_middle[:1])
+    third_out = [lax.ppermute(third_middle[0], "band", outward)]
+    sent = paired(sent)
+
+    blocks = [*both_products(y_turned, h_turned, [second_middle[0], second_out[0]], 2, (kept,))]
+    cores = [to_owner(blocks[0], second_owner, 1)]
+    (near,) = plus(kept, sent, (blocks[0],))
+    near_far = near_across(near)
+    blocks += both_products(y_turned, h_turned, [second_middle[1], second_out[1]], 2, (near, third_middle[1]))
+    second, third_middle[1] = plus(blocks[0], cores[0], (blocks[1],), third_middle[1:])
     second_far = to_owner(second, second_owner, 2)
-
+    third_out.append(lax.ppermute(third_middle[1], "band", outward))
+    keep = jnp.where(core == upper, 1, 0).astype(jnp.int32).reshape(1)
+    pieces = (blocks[1], third_middle[0], third_out[0])
+    kept, sent = pair_products(keep, y_turned, h_turned, *pieces, (second,))
+    sent = paired(sent)
+    (pair,) = plus(kept, sent, (mark((kept,)),))
+    pair_route = [
+        (((2 - b // 2 * 2 + c) ^ 2) * 4 + b, (2 - b // 2 * 2 + c) * 4 + b) for b in range(4) for c in (0, 1)
+    ]
+    pair_far = lax.ppermute(pair, ("dom", "band"), pair_route)
+    (block,) = both_products(y_turned, h_turned, [third_middle[1], third_out[1]], 2, (pair,))
+    cores.append(to_owner(block, third_owner, 1))
     is_near, is_second = chip == upper, core == upper
-    third, third_far = [], []
-    for at, pair in enumerate(zip(third_pieces, third_out)):
-        block = both_products(y_turned, h_turned, list(pair), 2, waited)
-        waited = (block, second, near_projected[1]) if at == 0 else (block, third[0], second_far)
-        block = block + to_owner(block, third_owner, 1)
-        third.append(block)
-        third_far.append(to_owner(block, third_owner, 2))
-    near_rows = jnp.concatenate([sum(near_margin[:2]), sum(near_projected[:2])])
-    base = jnp.where(is_near, near_rows, jnp.where(is_second, second + second_far, 0.0))
-    flag = jnp.where(is_near | is_second, 0, 1).astype(jnp.int32).reshape(1)
-    return (y_next, *finish(weight, flag, base, third, third_far))
+    flags = jnp.stack([is_near, ~is_near & is_second, ~is_near & ~is_second]).astype(jnp.int32)
+    base = near_rows(flags, near, near_far, (block, second_far))
+    (third,) = plus(block, cores[1], (base,))
+    third_far = to_owner(third, third_owner, 2)
+    pieces = (second, second_far, pair, pair_far, third, third_far)
+    outs = finish(weight, 0, flags, base, *pieces[:4], (), (third,))
+    return (y_next, *finish(weight, 1, flags, base, *pieces[2:], outs, ()))
 
 
 def solution(mesh):

time: 255 us -> 220 us (0.86)
  waiting for transfers between devices: 108 us -> 69 us
  Pallas kernels: 80.3 us -> 95.4 us
  local copies, waits for them, and re-layouts: 13.9 us -> 6.21 us
  other arithmetic: 8.17 us -> 3.18 us
    ppermute x19 -> x14, waiting for transfers between devices: 70.2 us -> 41.3 us  [exchange(): return lax.ppermute(block, axis, pairs + [(b, a) for a, b in pairs])]
    pallas_call x19 -> x24, Pallas kernels: 80.3 us -> 95.4 us  [call(): return lambda *args: made(*args, *extra)]
    ppermute x1, waiting for transfers between devices: 9.91 us -> 0.01 us  [on_device(): lax.ppermute(own, 'dom', [(i, (i + 1) % domains) for i in range(domains)])]
    unnamed x62 -> x27, local copies, waits for them, and re-layouts: 13.8 us -> 6.21 us
    add x8 -> x0, other arithmetic: 4.87 us -> none  [the longest x2 2.1 us: on_device(): near_rows = jnp.concatenate([sum(near_margin[:2]), sum(near_projected[:2])])]
    ppermute x7 -> x6, starting transfers between devices: 12.7 us -> 16.8 us  [the longest x1 4.46 us: on_device(): second_out = [lax.ppermute(second_middle[0], 'band', outward)]]
    ppermute x8 -> x4, starting transfers between devices: 10.7 us -> 7.56 us  [to_owner(): return lax.ppermute(block, ('dom', 'band'), route)]
    ppermute x19 -> x14, starting transfers between devices: 19.1 us -> 18.3 us  [exchange(): return lax.ppermute(block, axis, pairs + [(b, a) for a, b in pairs])]
  transfers between devices with their start and end apart: 35 -> 25, of which waited for: 16 -> 13; matrix products, arithmetic and copies ran while one was open for 2% -> 1% of each run, Pallas kernels for 26% -> 42%
where the time goes in v1:
time: 220 us; the launch traced here: 217 us
  Pallas kernels  95.4 us (43%)
  waiting for transfers between devices  69 us (31%)
  starting transfers between devices  42.7 us (19%)
  local copies, waits for them, and re-layouts  6.21 us (3%)
  other arithmetic  3.18 us (1%)
    pallas_call x24, Pallas kernels, call(): return lambda *args: made(*args, *extra)  95.4 us
    ppermute x14, waiting for transfers between devices, exchange(): return lax.ppermute(block, axis, pairs + [(b, a) for a, b in pairs])  41.3 us
    ppermute x14, starting transfers between devices, exchange(): return lax.ppermute(block, axis, pairs + [(b, a) for a, b in pairs])  18.3 us
    ppermute x4, waiting for transfers between devices, to_owner(): return lax.ppermute(block, ('dom', 'band'), route)  9.67 us
    ppermute x1, waiting for transfers between devices, on_device(): third_out.append(lax.ppermute(third_middle[1], 'band', outward))  8.83 us
    ppermute x4, starting transfers between devices, to_owner(): return lax.ppermute(block, ('dom', 'band'), route)  7.56 us
    unnamed x27, local copies, waits for them, and re-layouts  6.21 us
    ppermute x1, waiting for transfers between devices, on_device(): third_out = [lax.ppermute(third_middle[0], 'band', outward)]  5.3 us
  transfers between devices with their start and end apart: 25, of which 13 were waited for; matrix products, arithmetic and copies ran while one was open for 1% of the time, Pallas kernels for 42%

profile of v1, /device:TPU:18, one launch (start us, length us, event | category | flops | bytes accessed | tf_op | source)
XLA Modules:
  0.0 217.4 jit_solution(14916076031641674824)
XLA Ops:
  10.1 3.7 %to_grid.3 = (f32[1024,256]{1,0:T(8,128)}, f32[1024,512]{1,0:T(8,128)}) custom-call(s32[8,128]{1,0:T(8,128)S(1)} %bitcast.13, f32[1024,512]{1,0:T(8,128)S(1)} %copy-done.2, f32[1024,512]{1,0:T(8,128)} %get-tuple-element.37.refs_2_, f32[1024,256]{1,0:T(8,128)} %get-tuple-element.38.refs_3_), custom_call_target="tpu_custom_call", output_to_operand_aliasing={{1}: (2, {})} | custom-call | flops 999999995904 | bytes 1 | tf_op jit(solution)/shard_map/to_grid/pallas_call | solution.py:81
  16.1 8.4 %prepare.1 = (bf16[3,8,256,256]{3,2,1,0:T(8,128)(2,1)S(1)}, f32[1024,512]{1,0:T(8,128)S(1)}) custom-call(s32[1]{0:T(128)} %bitcast.1.refs_0_, f32[1,1024]{1,0:T(1,128)} %bitcast.3.refs_1_, f32[1,1024]{1,0:T(1,128)} %bitcast.4.refs_2_, f32[1,1024]{1,0:T(1,128)S(1)} %bitcast.16, s32[8,128]{1,0:T(8,128)S(1)} %bitcast.14, f32[1024,512]{1,0:T(8,128)S(1)} %copy-done.3, ...), custom_call_target="tpu_custom_call" | custom-call | flops 999999995904 | bytes 1 | tf_op jit(solution)/shard_map/prepare/pallas_call | solution.py:81
  24.5 9.4 %collective-permute-done.3.refs_3_ = f32[1024,256]{1,0:T(8,128)} collective-permute-done((f32[1024,256]{1,0:T(8,128)}, f32[1024,256]{1,0:T(8,128)}, u32[]{:S(2)}, u32[]{:S(2)}) %collective-permute-start.3) | collective-permute-done | bytes 1048608 | tf_op jit(solution)/shard_map/ppermute | solution.py:568
  33.9 6.1 %apply_h.3 = (f32[1024,256]{1,0:T(8,128)}, f32[1024,512]{1,0:T(8,128)S(1)}, bf16[512,1024]{1,0:T(8,128)(2,1)S(1)}, bf16[512,1024]{1,0:T(8,128)(2,1)S(1)}) custom-call(bf16[3,8,256,256]{3,2,1,0:T(8,128)(2,1)S(1)} %get-tuple-element.40.refs_0_, f32[1024,512]{1,0:T(8,128)} %get-tuple-element.39.refs_6_.refs_1_, f32[1024,512]{1,0:T(8,128)} %collective-permute-done.1.refs_2_, ...), custom_call_target="tpu_custom_call" | custom-call | flops 999999995904 | bytes 1 | tf_op jit(solution)/shard_map/apply_h/pallas_call | solution.py:81
  45.1 11.2 %collective-permute-done.2.refs_3_ = f32[1024,256]{1,0:T(8,128)} collective-permute-done((f32[1024,256]{1,0:T(8,128)}, f32[1024,256]{1,0:T(8,128)}, u32[]{:S(2)}, u32[]{:S(2)}) %collective-permute-start.2) | collective-permute-done | bytes 1048608 | tf_op jit(solution)/shard_map/ppermute | solution.py:568
  56.4 6.1 %apply_h.4 = (f32[1024,256]{1,0:T(8,128)}, f32[1024,512]{1,0:T(8,128)S(1)}, bf16[512,1024]{1,0:T(8,128)(2,1)S(1)}, bf16[512,1024]{1,0:T(8,128)(2,1)S(1)}) custom-call(bf16[3,8,256,256]{3,2,1,0:T(8,128)(2,1)S(1)} %get-tuple-element.40.refs_0_, ...), custom_call_target="tpu_custom_call", output_to_operand_aliasing={{1}: (5, {}), {2}: (6, {}), {3}: (7, {})} | custom-call | flops 999999995904 | bytes 1 | tf_op jit(solution)/shard_map/apply_h/pallas_call | solution.py:81
  69.3 8.8 %collective-permute-done.6.refs_5_.refs_3_ = f32[1024,256]{1,0:T(8,128)} collective-permute-done((f32[1024,256]{1,0:T(8,128)}, f32[1024,256]{1,0:T(8,128)}, u32[]{:S(2)}, u32[]{:S(2)}) %collective-permute-start.6) | collective-permute-done | bytes 1048608 | tf_op jit(solution)/shard_map/ppermute | solution.py:568
  78.1 5.0 %from_grid.1 = (f32[1024,512]{1,0:T(8,128)}, f32[1024,512]{1,0:T(8,128)}, f32[1024,256]{1,0:T(8,128)}, f32[1024,256]{1,0:T(8,128)}) custom-call(s32[1,1024]{1,0:T(1,128)S(1)} %bitcast.15, f32[1024,512]{1,0:T(8,128)S(1)} %get-tuple-element.47.refs_1_, f32[1024,256]{1,0:T(8,128)} %copy.27.refs_2_, ...), custom_call_target="tpu_custom_call", output_to_operand_aliasing={{3}: (2, {})} | custom-call | flops 999999995904 | bytes 1 | tf_op jit(solution)/shard_map/from_grid/pallas_call | solution.py:81
  87.0 4.5 %collective-permute-start.13 = (f32[1024,256]{1,0:T(8,128)}, f32[1024,256]{1,0:T(8,128)}, u32[]{:S(2)}, u32[]{:S(2)}) collective-permute-start(f32[1024,256]{1,0:T(8,128)} %get-tuple-element.60.refs_4_), channel_id=1, source_target_pairs={{2,3},{1,0},{6,7},{5,4},{10,11},{9,8},{14,15},{13,12},{18,19},{17,... | collective-permute-start | bytes 3145736 | tf_op jit(solution)/shard_map/ppermute | solution.py:647
  94.8 7.4 %sorted_products.2 = (f32[1024,512]{1,0:T(8,128)S(1)}, f32[1024,512]{1,0:T(8,128)}, f32[1024,256]{1,0:T(8,128)}) custom-call(s32[1]{0:T(128)} %bitcast.10.refs_0_, bf16[512,1024]{1,0:T(8,128)(2,1)S(1)} %copy-done.6, bf16[512,1024]{1,0:T(8,128)(2,1)S(1)} %get-tuple-element.52.refs_2_.refs_1_, ...), custom_call_target="tpu_custom_call", output_to_operand_aliasing={{2}: (7, {})} | custom-call | flops 999999995904 | bytes 1 | tf_op jit(solution)/shard_map/sorted_products/pallas_call | solution.py:81
  104.5 5.2 %collective-permute-done.8.refs_4_ = f32[1024,256]{1,0:T(8,128)} collective-permute-done((f32[1024,256]{1,0:T(8,128)}, f32[1024,256]{1,0:T(8,128)}, u32[]{:S(2)}, u32[]{:S(2)}) %collective-permute-start.8) | collective-permute-done | bytes 1048608 | tf_op jit(solution)/shard_map/ppermute | solution.py:568
  109.8 8.0 %apply_h.5 = (bf16[512,1024]{1,0:T(8,128)(2,1)S(1)}, bf16[512,1024]{1,0:T(8,128)(2,1)S(1)}) custom-call(bf16[3,8,256,256]{3,2,1,0:T(8,128)(2,1)S(1)} %get-tuple-element.40.refs_0_, f32[1024,512]{1,0:T(8,128)S(1)} %get-tuple-element.47.refs_1_, f32[1024,512]{1,0:T(8,128)} %collective-permute-done.7.refs_2_, ...), custom_call_target="tpu_custom_call" | custom-call | flops 999999995904 | bytes 1 | tf_op jit(solution)/shard_map/apply_h/pallas_call | solution.py:81
  123.8 7.4 %sorted_products.3 = (f32[1024,512]{1,0:T(8,128)S(1)}, f32[1024,512]{1,0:T(8,128)}, f32[1024,256]{1,0:T(8,128)}) custom-call(s32[1]{0:T(128)} %bitcast.10.refs_0_, bf16[512,1024]{1,0:T(8,128)(2,1)S(1)} %get-tuple-element.55.refs_1_.refs_2_.refs_3_, ...), custom_call_target="tpu_custom_call", output_to_operand_aliasing={{0}: (7, {}), {1}: (8, {}), {2}: (9, {})} | custom-call | flops 999999995904 | bytes 1 | tf_op jit(solution)/shard_map/sorted_products/pallas_call | solution.py:81
  131.2 4.9 %both_products.3.refs_2_.refs_0_ = f32[1024,256]{1,0:T(8,128)} custom-call(bf16[512,1024]{1,0:T(8,128)(2,1)S(1)} %copy-done.6, bf16[512,1024]{1,0:T(8,128)(2,1)S(1)} %copy-done.8, bf16[512,1024]{1,0:T(8,128)(2,1)S(1)} %get-tuple-element.55.refs_1_.refs_2_.refs_3_, bf16[512,1024]{1,0:T(8,128)(2,1)S(1)} %get-tuple-element.56.refs_2_.refs_3_.refs_4_, ...), custom_call_target="tpu_custom_call" | custom-call | flops 999999995904 | bytes 1 | tf_op jit(solution)/shard_map/both_products/pallas_call | solution.py:81
  136.2 3.4 %collective-permute-start.15 = (f32[1024,256]{1,0:T(8,128)}, f32[1024,256]{1,0:T(8,128)}, u32[]{:S(2)}, u32[]{:S(2)}) collective-permute-start(f32[1024,256]{1,0:T(8,128)} %both_products.3.refs_2_.refs_0_), channel_id=1, source_target_pairs={{12,8},{4,0},{13,9},{5,1},{2,6},{10,14},{3,7},{11,15},{28,24},{20,... | collective-permute-start | bytes 3145736 | tf_op jit(solution)/shard_map/ppermute | solution.py:586
  144.6 4.2 %collective-permute-start.14 = (f32[1024,512]{1,0:T(8,128)}, f32[1024,512]{1,0:T(8,128)}, u32[]{:S(2)}, u32[]{:S(2)}) collective-permute-start(f32[1024,512]{1,0:T(8,128)} %plus.4.refs_6_.refs_1_), channel_id=1, source_target_pairs={{8,0},{12,4},{9,1},{13,5},{2,10},{6,14},{3,11},{7,15},{24,16},{28,... | collective-permute-start | bytes 6291464 | tf_op jit(solution)/shard_map/ppermute | solution.py:638
  148.8 4.2 %both_products.4.refs_3_.refs_5_ = f32[1024,256]{1,0:T(8,128)S(1)} custom-call(bf16[512,1024]{1,0:T(8,128)(2,1)S(1)} %copy-done.6, bf16[512,1024]{1,0:T(8,128)(2,1)S(1)} %copy-done.8, bf16[512,1024]{1,0:T(8,128)(2,1)S(1)} %get-tuple-element.55.refs_1_.refs_2_.refs_3_, bf16[512,1024]{1,0:T(8,128)(2,1)S(1)} %copy-done.10, ...), custom_call_target="tpu_custom_call" | custom-call | flops 999999995904 | bytes 1 | tf_op jit(solution)/shard_map/both_products/pallas_call | solution.py:81
  159.5 5.3 %collective-permute-done.19.refs_7_ = f32[1024,256]{1,0:T(8,128)} collective-permute-done((f32[1024,256]{1,0:T(8,128)}, f32[1024,256]{1,0:T(8,128)}, u32[]{:S(2)}, u32[]{:S(2)}) %collective-permute-start.19) | collective-permute-done | bytes 1048608 | tf_op jit(solution)/shard_map/ppermute | solution.py:657
  164.8 4.9 %pair_products.1 = (f32[1024,256]{1,0:T(8,128)S(1)}, f32[1024,256]{1,0:T(8,128)}) custom-call(s32[1]{0:T(128)} %bitcast.11.refs_0_, bf16[512,1024]{1,0:T(8,128)(2,1)S(1)} %copy-done.6, bf16[512,1024]{1,0:T(8,128)(2,1)S(1)} %copy-done.8, bf16[512,1024]{1,0:T(8,128)(2,1)S(1)} %get-tuple-element.55.refs_1_.refs_2_.refs_3_, bf16[512,1024]{1,0:T(8,128)(2,1)S(1)} %copy-done.11, ...), custom_call_target="tpu_custom_call" | custom-call | flops 999999995904 | bytes 1 | tf_op jit(solution)/shard_map/pair_products/pallas_call | solution.py:81
  176.1 8.8 %collective-permute-done.18.refs_5_ = f32[1024,256]{1,0:T(8,128)} collective-permute-done((f32[1024,256]{1,0:T(8,128)}, f32[1024,256]{1,0:T(8,128)}, u32[]{:S(2)}, u32[]{:S(2)}) %collective-permute-start.18) | collective-permute-done | bytes 1048608 | tf_op jit(solution)/shard_map/ppermute | solution.py:667
  184.9 4.9 %both_products.5.refs_3_.refs_0_ = f32[1024,256]{1,0:T(8,128)} custom-call(bf16[512,1024]{1,0:T(8,128)(2,1)S(1)} %copy-done.6, bf16[512,1024]{1,0:T(8,128)(2,1)S(1)} %copy-done.8, bf16[512,1024]{1,0:T(8,128)(2,1)S(1)} %get-tuple-element.55.refs_1_.refs_2_.refs_3_, bf16[512,1024]{1,0:T(8,128)(2,1)S(1)} %copy-done.11, f32[1024,256]{1,0:T(8,128)} %get-tuple-element.62.refs_4_, ...), custom_call_target="tpu_custom_call" | custom-call | flops 999999995904 | bytes 1 | tf_op jit(solution)/shard_map/both_products/pallas_call | solution.py:81
  198.4 3.8 %collective-permute-done.22.refs_5_.refs_3_ = f32[1024,256]{1,0:T(8,128)} collective-permute-done((f32[1024,256]{1,0:T(8,128)}, f32[1024,256]{1,0:T(8,128)}, u32[]{:S(2)}, u32[]{:S(2)}) %collective-permute-start.22) | collective-permute-done | bytes 1048608 | tf_op jit(solution)/shard_map/ppermute | solution.py:676
  205.5 8.6 %collective-permute-done.24.refs_5_ = f32[1024,256]{1,0:T(8,128)} collective-permute-done((f32[1024,256]{1,0:T(8,128)}, f32[1024,256]{1,0:T(8,128)}, u32[]{:S(2)}, u32[]{:S(2)}) %collective-permute-start.24) | collective-permute-done | bytes 1048608 | tf_op jit(solution)/shard_map/ppermute | solution.py:586
  214.1 3.3 %finish.3 = (f32[512,512]{1,0:T(8,128)}, f32[512,512]{1,0:T(8,128)}) custom-call(s32[3]{0:T(128)S(1)} %add_convert_fusion.refs_0_, f32[1024,512]{1,0:T(8,128)S(1)} %near_rows.1.refs_2_.refs_1_, f32[1024,256]{1,0:T(8,128)} %plus.6.refs_6_.refs_4_.refs_2_, ...), custom_call_target="tpu_custom_call", output_to_operand_aliasing={{0}: (6, {}), {1}: (7, {})} | custom-call | flops 999999995904 | bytes 1 | tf_op jit(solution)/shard_map/finish/pallas_call | solution.py:81
  (81 shorter events, 68.9 us)
Async XLA Ops:
  3.2 12.9 %collective-permute-start = (f32[1024]{0:T(1024)}, f32[1024]{0:T(1024)}, u32[]{:S(2)}, u32[]{:S(2)}) collective-permute-start(f32[1024]{0:T(1024)} %select_reduce_fusion.1), channel_id=1, source_target_pairs={{0,4},{4,8},{8,12},{12,0},{1,5},{5,9},{9,13},{13,1},{2,6},{6,10},{... | collective-permute-start | bytes 12296 | tf_op jit(solution)/shard_map/ppermute | solution.py:599
  8.3 25.6 %collective-permute-start.3 = (f32[1024,256]{1,0:T(8,128)}, f32[1024,256]{1,0:T(8,128)}, u32[]{:S(2)}, u32[]{:S(2)}) collective-permute-start(f32[1024,256]{1,0:T(8,128)} %get-tuple-element.38.refs_3_), channel_id=1, source_target_pairs={{4,8},{12,0},{8,4},{0,12},{5,9},{13,1},{9,5},{1,13},{6,10},{14,2},... | collective-permute-start | bytes 3145736 | tf_op jit(solution)/shard_map/ppermute | solution.py:568
  13.8 20.1 %collective-permute-start.1 = (f32[1024,512]{1,0:T(8,128)}, f32[1024,512]{1,0:T(8,128)}, u32[]{:S(2)}, u32[]{:S(2)}) collective-permute-start(f32[1024,512]{1,0:T(8,128)} %get-tuple-element.39.refs_6_.refs_1_), channel_id=1, source_target_pairs={{0,4},{8,12},{4,0},{12,8},{1,5},{9,13},{5,1},{13,9},{2,6},{10,14},... | collective-permute-start | bytes 6291464 | tf_op jit(solution)/shard_map/ppermute | solution.py:568
  13.8 42.6 %collective-permute-start.2 = (f32[1024,256]{1,0:T(8,128)}, f32[1024,256]{1,0:T(8,128)}, u32[]{:S(2)}, u32[]{:S(2)}) collective-permute-start(f32[1024,256]{1,0:T(8,128)} %get-tuple-element.41), channel_id=1, source_target_pairs={{4,8},{12,0},{8,4},{0,12},{5,9},{13,1},{9,5},{1,13},{6,10},{14,2},... | collective-permute-start | bytes 3145736 | tf_op jit(solution)/shard_map/ppermute | solution.py:568
  40.0 27.0 %collective-permute-start.4 = (f32[1024,256]{1,0:T(8,128)}, f32[1024,256]{1,0:T(8,128)}, u32[]{:S(2)}, u32[]{:S(2)}) collective-permute-start(f32[1024,256]{1,0:T(8,128)} %get-tuple-element.46.refs_8_.refs_3_), channel_id=1, source_target_pairs={{1,2},{2,1},{5,6},{6,5},{9,10},{10,9},{13,14},{14,13},{17,18},{18,... | collective-permute-start | bytes 3145736 | tf_op jit(solution)/shard_map/ppermute | solution.py:568
  42.3 26.9 %collective-permute-start.5 = (f32[1024,256]{1,0:T(8,128)}, f32[1024,256]{1,0:T(8,128)}, u32[]{:S(2)}, u32[]{:S(2)}) collective-permute-start(f32[1024,256]{1,0:T(8,128)} %get-tuple-element.46.refs_8_.refs_3_), channel_id=1, source_target_pairs={{0,1},{2,3},{1,0},{3,2},{4,5},{6,7},{5,4},{7,6},{8,9},{10,11},{9,8... | collective-permute-start | bytes 3145736 | tf_op jit(solution)/shard_map/ppermute | solution.py:568
  43.2 34.9 %collective-permute-start.6 = (f32[1024,256]{1,0:T(8,128)}, f32[1024,256]{1,0:T(8,128)}, u32[]{:S(2)}, u32[]{:S(2)}) collective-permute-start(f32[1024,256]{1,0:T(8,128)} %get-tuple-element.46.refs_8_.refs_3_), channel_id=1, source_target_pairs={{4,8},{12,0},{8,4},{0,12},{5,9},{13,1},{9,5},{1,13},{6,10},{14,2},... | collective-permute-start | bytes 3145736 | tf_op jit(solution)/shard_map/ppermute | solution.py:568
  62.5 29.0 %collective-permute-start.9 = (f32[1024,256]{1,0:T(8,128)}, f32[1024,256]{1,0:T(8,128)}, u32[]{:S(2)}, u32[]{:S(2)}) collective-permute-start(f32[1024,256]{1,0:T(8,128)} %get-tuple-element.53.refs_4_), channel_id=1, source_target_pairs={{1,2},{2,1},{5,6},{6,5},{9,10},{10,9},{13,14},{14,13},{17,18},{18,... | collective-permute-start | bytes 3145736 | tf_op jit(solution)/shard_map/ppermute | solution.py:568
  64.9 29.9 %collective-permute-start.10 = (f32[1024,256]{1,0:T(8,128)}, f32[1024,256]{1,0:T(8,128)}, u32[]{:S(2)}, u32[]{:S(2)}) collective-permute-start(f32[1024,256]{1,0:T(8,128)} %get-tuple-element.53.refs_4_), channel_id=1, source_target_pairs={{0,1},{2,3},{1,0},{3,2},{4,5},{6,7},{5,4},{7,6},{8,9},{10,11},{9,8... | collective-permute-start | bytes 3145736 | tf_op jit(solution)/shard_map/ppermute | solution.py:568
  83.1 8.4 %collective-permute-start.7 = (f32[1024,512]{1,0:T(8,128)}, f32[1024,512]{1,0:T(8,128)}, u32[]{:S(2)}, u32[]{:S(2)}) collective-permute-start(f32[1024,512]{1,0:T(8,128)} %get-tuple-element.49), channel_id=1, source_target_pairs={{0,4},{8,12},{4,0},{12,8},{1,5},{9,13},{5,1},{13,9},{2,6},{10,14},... | collective-permute-start | bytes 6291464 | tf_op jit(solution)/shard_map/ppermute | solution.py:568
  84.2 25.5 %collective-permute-start.8 = (f32[1024,256]{1,0:T(8,128)}, f32[1024,256]{1,0:T(8,128)}, u32[]{:S(2)}, u32[]{:S(2)}) collective-permute-start(f32[1024,256]{1,0:T(8,128)} %get-tuple-element.50), channel_id=1, source_target_pairs={{4,8},{12,0},{8,4},{0,12},{5,9},{13,1},{9,5},{1,13},{6,10},{14,2},... | collective-permute-start | bytes 3145736 | tf_op jit(solution)/shard_map/ppermute | solution.py:568
  87.0 44.2 %collective-permute-start.13 = (f32[1024,256]{1,0:T(8,128)}, f32[1024,256]{1,0:T(8,128)}, u32[]{:S(2)}, u32[]{:S(2)}) collective-permute-start(f32[1024,256]{1,0:T(8,128)} %get-tuple-element.60.refs_4_), channel_id=1, source_target_pairs={{2,3},{1,0},{6,7},{5,4},{10,11},{9,8},{14,15},{13,12},{18,19},{17,... | collective-permute-start | bytes 3145736 | tf_op jit(solution)/shard_map/ppermute | solution.py:647
  92.9 27.4 %collective-permute-start.11 = (f32[1024,256]{1,0:T(8,128)}, f32[1024,256]{1,0:T(8,128)}, u32[]{:S(2)}, u32[]{:S(2)}) collective-permute-start(f32[1024,256]{1,0:T(8,128)} %gate.2.refs_5_), channel_id=1, source_target_pairs={{1,2},{2,1},{5,6},{6,5},{9,10},{10,9},{13,14},{14,13},{17,18},{18,... | collective-permute-start | bytes 3145736 | tf_op jit(solution)/shard_map/ppermute | solution.py:568
  102.2 46.6 %collective-permute-start.17 = (f32[1024,256]{1,0:T(8,128)}, f32[1024,256]{1,0:T(8,128)}, u32[]{:S(2)}, u32[]{:S(2)}) collective-permute-start(f32[1024,256]{1,0:T(8,128)} %get-tuple-element.61.refs_4_), channel_id=1, source_target_pairs={{2,3},{1,0},{6,7},{5,4},{10,11},{9,8},{14,15},{13,12},{18,19},{17,... | collective-permute-start | bytes 3145736 | tf_op jit(solution)/shard_map/ppermute | solution.py:652
  121.6 27.2 %collective-permute-start.16 = (f32[1024,256]{1,0:T(8,128)}, f32[1024,256]{1,0:T(8,128)}, u32[]{:S(2)}, u32[]{:S(2)}) collective-permute-start(f32[1024,256]{1,0:T(8,128)} %gate.3.refs_6_), channel_id=1, source_target_pairs={{1,2},{2,1},{5,6},{6,5},{9,10},{10,9},{13,14},{14,13},{17,18},{18,... | collective-permute-start | bytes 3145736 | tf_op jit(solution)/shard_map/ppermute | solution.py:568
  131.2 10.6 %collective-permute-start.12 = (f32[1024,512]{1,0:T(8,128)}, f32[1024,512]{1,0:T(8,128)}, u32[]{:S(2)}, u32[]{:S(2)}) collective-permute-start(f32[1024,512]{1,0:T(8,128)} %get-tuple-element.59), channel_id=1, source_target_pairs={{0,4},{8,12},{4,0},{12,8},{1,5},{9,13},{5,1},{13,9},{2,6},{10,14},... | collective-permute-start | bytes 6291464 | tf_op jit(solution)/shard_map/ppermute | solution.py:568
  136.2 16.8 %collective-permute-start.15 = (f32[1024,256]{1,0:T(8,128)}, f32[1024,256]{1,0:T(8,128)}, u32[]{:S(2)}, u32[]{:S(2)}) collective-permute-start(f32[1024,256]{1,0:T(8,128)} %both_products.3.refs_2_.refs_0_), channel_id=1, source_target_pairs={{12,8},{4,0},{13,9},{5,1},{2,6},{10,14},{3,7},{11,15},{28,24},{20,... | collective-permute-start | bytes 3145736 | tf_op jit(solution)/shard_map/ppermute | solution.py:586
  139.6 25.2 %collective-permute-start.19 = (f32[1024,256]{1,0:T(8,128)}, f32[1024,256]{1,0:T(8,128)}, u32[]{:S(2)}, u32[]{:S(2)}) collective-permute-start(f32[1024,256]{1,0:T(8,128)} %get-tuple-element.63.refs_6_), channel_id=1, source_target_pairs={{2,3},{1,0},{6,7},{5,4},{10,11},{9,8},{14,15},{13,12},{18,19},{17,... | collective-permute-start | bytes 3145736 | tf_op jit(solution)/shard_map/ppermute | solution.py:657
  144.6 46.6 %collective-permute-start.14 = (f32[1024,512]{1,0:T(8,128)}, f32[1024,512]{1,0:T(8,128)}, u32[]{:S(2)}, u32[]{:S(2)}) collective-permute-start(f32[1024,512]{1,0:T(8,128)} %plus.4.refs_6_.refs_1_), channel_id=1, source_target_pairs={{8,0},{12,4},{9,1},{13,5},{2,10},{6,14},{3,11},{7,15},{24,16},{28,... | collective-permute-start | bytes 6291464 | tf_op jit(solution)/shard_map/ppermute | solution.py:638
  155.5 29.4 %collective-permute-start.18 = (f32[1024,256]{1,0:T(8,128)}, f32[1024,256]{1,0:T(8,128)}, u32[]{:S(2)}, u32[]{:S(2)}) collective-permute-start(f32[1024,256]{1,0:T(8,128)} %get-tuple-element.62.refs_4_), channel_id=1, source_target_pairs={{2,3},{1,0},{6,7},{5,4},{10,11},{9,8},{14,15},{13,12},{18,19},{17,... | collective-permute-start | bytes 3145736 | tf_op jit(solution)/shard_map/ppermute | solution.py:667
  157.8 33.3 %collective-permute-start.21 = (f32[1024,256]{1,0:T(8,128)}, f32[1024,256]{1,0:T(8,128)}, u32[]{:S(2)}, u32[]{:S(2)}) collective-permute-start(f32[1024,256]{1,0:T(8,128)} %get-tuple-element.64.refs_8_.refs_2_), channel_id=1, source_target_pairs={{0,8},{1,9},{14,6},{15,7},{16,24},{17,25},{30,22},{31,23}} | collective-permute-start | bytes 3145736 | tf_op jit(solution)/shard_map/ppermute | solution.py:586
  174.8 27.4 %collective-permute-start.22 = (f32[1024,256]{1,0:T(8,128)}, f32[1024,256]{1,0:T(8,128)}, u32[]{:S(2)}, u32[]{:S(2)}) collective-permute-start(f32[1024,256]{1,0:T(8,128)} %plus.6.refs_6_.refs_4_.refs_2_), channel_id=1, source_target_pairs={{0,8},{4,12},{1,9},{5,13},{10,2},{14,6},{11,3},{15,7},{16,24},{20,... | collective-permute-start | bytes 3145736 | tf_op jit(solution)/shard_map/ppermute | solution.py:676
  189.8 4.9 %collective-permute-start.23 = (f32[1024,256]{1,0:T(8,128)}, f32[1024,256]{1,0:T(8,128)}, u32[]{:S(2)}, u32[]{:S(2)}) collective-permute-start(f32[1024,256]{1,0:T(8,128)} %both_products.5.refs_3_.refs_0_), channel_id=1, source_target_pairs={{8,12},{0,4},{9,13},{1,5},{6,2},{14,10},{7,3},{15,11},{24,28},{16,... | collective-permute-start | bytes 3145736 | tf_op jit(solution)/shard_map/ppermute | solution.py:586
  197.1 17.0 %collective-permute-start.24 = (f32[1024,256]{1,0:T(8,128)}, f32[1024,256]{1,0:T(8,128)}, u32[]{:S(2)}, u32[]{:S(2)}) collective-permute-start(f32[1024,256]{1,0:T(8,128)} %plus.7.refs_6_.refs_4_), channel_id=1, source_target_pairs={{4,12},{5,13},{10,2},{11,3},{20,28},{21,29},{26,18},{27,19}} | collective-permute-start | bytes 3145736 | tf_op jit(solution)/shard_map/ppermute | solution.py:586
  (14 other events, 119.5 us)

commit v2 on v1

--- a/solution.py
+++ b/solution.py
@@ -52,18 +52,18 @@
 
 def call(kernel, after, *, in_specs, out_specs, out_shape, name, into=(), passed=(), **options):
     count = len(in_specs)
-    extra = [*[array for _, array in into], *passed, *after]
+    extra = [*[array for _, array in into], *after, *passed]
     aliases = {count + at: out for at, (out, _) in enumerate(into)}
     outs = len(out_shape) if isinstance(out_shape, (list, tuple)) else 1
     if passed:
         out_specs = [*out_specs, *map(corner, passed)]
         out_shape = [*out_shape, *[jax.ShapeDtypeStruct(x.shape, x.dtype) for x in passed]]
-        aliases |= {count + len(into) + at: outs + at for at in range(len(passed))}
+        aliases |= {count + len(extra) - len(passed) + at: outs + at for at in range(len(passed))}
 
     def body(*refs):
         rest = refs[count + len(extra) :]
         kernel(*refs[:count], *rest[:outs], *rest[outs + len(passed) :])
-        first = count + len(into)
+        first = count + len(extra) - len(passed)
         for x_ref, out_ref in zip(refs[first : first + len(passed)], rest[outs : outs + len(passed)]):
             out_ref[...] = x_ref[...]
 
@@ -282,67 +282,112 @@
     )
 
 
-def apply_kernel(filtered, pieces, band_ref, own_ref, paired_ref, *refs):
-    far_refs, refs, wide = refs[:pieces], refs[pieces:], refs[-1]
+def fill(wide, plane, ref, start, width):
+    nodes = ref.shape[0]
+    for first, part in zip((start, width + start), halves(ref[...])):
+        columns = slice(first, first + part.shape[1])
+        wide[plane, pl.ds(MARGIN, nodes), columns] = part
+        wide[plane, pl.ds(0, MARGIN), columns] = part[nodes - MARGIN :]
+        wide[plane, pl.ds(MARGIN + nodes, MARGIN), columns] = part[:MARGIN]
+
+
+def applied_rows(band_ref, at, wide, first):
+    total = None
+    for plane in range(band_ref.shape[0]):
+        term = dot(band_ref[plane, at], wide[plane, pl.ds(first, WINDOW), :])
+        total = term if total is None else total + term
+    total = total[:BLOCK] + total[BLOCK:]
+    width = total.shape[1] // 2
+    return total[:, :width] + total[:, width:]
+
+
+def on_chip_kernel(filtered, band_ref, own_ref, paired_ref, *refs):
+    last_ref, (out_ref, wide) = refs[0], refs[-2:]
     step = pl.program_id(0)
-    nodes, width = own_ref.shape
+    width = own_ref.shape[1]
 
     @pl.when(step == 0)
     def _():
-        sources = [(0, 0, own_ref), (1, 0, paired_ref)]
-        sources += [(2, at * width // pieces, ref) for at, ref in enumerate(far_refs)]
-        for plane, first, ref in sources:
-            for start, part in zip((first, width + first), halves(ref[...])):
-                columns = slice(start, start + part.shape[1])
-                wide[plane, pl.ds(MARGIN, nodes), columns] = part
-                wide[plane, pl.ds(0, MARGIN), columns] = part[nodes - MARGIN :]
-                wide[plane, pl.ds(MARGIN + nodes, MARGIN), columns] = part[:MARGIN]
+        for plane, ref in enumerate((own_ref, paired_ref)):
+            fill(wide, plane, ref, 0, width)
 
     per_step = band_ref.shape[1]
     for at in range(per_step):
-        block = step * per_step + at
-        first = pl.multiple_of(block * BLOCK, BLOCK)
-        total = None
-        for plane in range(3):
-            term = dot(band_ref[plane, at], wide[plane, pl.ds(first, WINDOW), :])
-            total = term if total is None else total + term
-        total = total[:BLOCK] + total[BLOCK:]
-        total = total[:, :width] + total[:, width:]
+        first = pl.multiple_of((step * per_step + at) * BLOCK, BLOCK)
+        total = applied_rows(band_ref, at, wide, first)
         rows = pl.ds(at * BLOCK, BLOCK)
         if filtered:
-            last_ref, out_ref, whole_ref, turned_high, turned_low = refs[:5]
-            mine = own_ref[pl.ds(first, BLOCK), :]
-            total = (2.0 / half_width) * (total - centre * mine) - last_ref[rows, :]
+            total = (2.0 / half_width) * (total - centre * own_ref[pl.ds(first, BLOCK), :]) - last_ref[rows, :]
+        out_ref[rows, :] = total
+
+
+def across_kernel(filtered, pieces, band_ref, part_ref, *refs):
+    far_refs, outs, wide = refs[:pieces], refs[pieces:-1], refs[-1]
+    step = pl.program_id(0)
+    width = part_ref.shape[1]
+
+    @pl.when(step == 0)
+    def _():
+        for at, ref in enumerate(far_refs):
+            fill(wide, 0, ref, at * width // pieces, width)
+
+    per_step = band_ref.shape[1]
+    for at in range(per_step):
+        first = pl.multiple_of((step * per_step + at) * BLOCK, BLOCK)
+        total = applied_rows(band_ref, at, wide, first)
+        rows = pl.ds(at * BLOCK, BLOCK)
+        if filtered:
+            total = (2.0 / half_width) * total
+        total = part_ref[rows, :] + total
+        for out_ref in outs[:-2]:
             out_ref[rows, :] = total
-            whole_ref[rows, :] = total
-        else:
-            turned_high, turned_low = refs[:2]
-        turned_high[:, rows], turned_low[:, rows] = halves(total.T)
-
-
-def apply_specs(nodes, width):
-    per_step = 2
-    rows = per_step * BLOCK
+        for out_ref, half in zip(outs[-2:], halves(total.T)):
+            out_ref[:, rows] = half
+
+
+PER_STEP = 2
+
+
+def on_chip(band, own, paired, last, after=()):
+    nodes, states = own.shape
+    rows = PER_STEP * BLOCK
+    whole = pl.BlockSpec((nodes, states), lambda i: (0, 0))
+    part = pl.BlockSpec((rows, states), lambda i: (i, 0))
+    return call(
+        functools.partial(on_chip_kernel, last is not None),
+        after,
+        grid=(nodes // rows,),
+        in_specs=[pl.BlockSpec((2, PER_STEP, 2 * BLOCK, WINDOW), lambda i: (0, i, 0, 0)), whole, whole]
+        + [part] * (last is not None),
+        out_specs=part,
+        out_shape=jax.ShapeDtypeStruct((nodes, states), jnp.float32),
+        scratch_shapes=[pltpu.VMEM((2, nodes + 2 * MARGIN, 2 * states), jnp.bfloat16)],
+        name="on_chip",
+    )(band, own, paired, *([] if last is None else [last]))
+
+
+def across_specs(nodes, width):
+    rows = PER_STEP * BLOCK
     return dict(
         grid=(nodes // rows,),
-        scratch_shapes=[pltpu.VMEM((3, nodes + 2 * MARGIN, 2 * width), jnp.bfloat16)],
-        name="apply_h",
-    ), pl.BlockSpec((3, per_step, 2 * BLOCK, WINDOW), lambda i: (0, i, 0, 0)), rows
-
-
-def next_degree(band, own, paired, far, last, at, so_far, after):
+        scratch_shapes=[pltpu.VMEM((1, nodes + 2 * MARGIN, 2 * width), jnp.bfloat16)],
+        name="across",
+    ), pl.BlockSpec((1, PER_STEP, 2 * BLOCK, WINDOW), lambda i: (2, i, 0, 0))
+
+
+def next_degree(band, terms, far, at, so_far, after):
     nodes, width = far.shape
-    states = own.shape[1]
-    options, band_spec, rows = apply_specs(nodes, width)
-    column = pl.BlockSpec((nodes, width), lambda i: (0, at))
+    states = terms.shape[1]
+    rows = PER_STEP * BLOCK
+    options, band_spec = across_specs(nodes, width)
     part = pl.BlockSpec((rows, width), lambda i: (i, at))
     turned = pl.BlockSpec((width, rows), lambda i: (at, i))
     turned_shape = jax.ShapeDtypeStruct((states, nodes), jnp.bfloat16)
     return call(
-        functools.partial(apply_kernel, True, 1),
+        functools.partial(across_kernel, True, 1),
         after,
         into=[(out, so_far[out - 1]) for out in (1, 2, 3) if at],
-        in_specs=[band_spec, column, column, pl.BlockSpec((nodes, width), lambda i: (0, 0)), part],
+        in_specs=[band_spec, part, pl.BlockSpec((nodes, width), lambda i: (0, 0))],
         out_specs=[pl.BlockSpec((rows, width), lambda i: (i, 0)), part, turned, turned],
         out_shape=[
             jax.ShapeDtypeStruct((nodes, width), jnp.float32),
@@ -351,23 +396,24 @@
             turned_shape,
         ],
         **options,
-    )(band, own, paired, far, last)
-
-
-def applied_next(band, own, paired, far, after=()):
-    nodes, states = own.shape
-    options, band_spec, rows = apply_specs(nodes, states)
-    whole = pl.BlockSpec((nodes, states), lambda i: (0, 0))
+    )(band, terms, far)
+
+
+def applied_next(band, terms, far, after=()):
+    nodes, states = terms.shape
+    rows = PER_STEP * BLOCK
+    options, band_spec = across_specs(nodes, states)
     turned = pl.BlockSpec((states, rows), lambda i: (0, i))
     turned_shape = jax.ShapeDtypeStruct((states, nodes), jnp.bfloat16)
     return call(
-        functools.partial(apply_kernel, False, len(far)),
-        after,
-        in_specs=[band_spec, whole, whole] + [pl.BlockSpec(x.shape, lambda i: (0, 0)) for x in far],
+        functools.partial(across_kernel, False, len(far)),
+        after,
+        in_specs=[band_spec, pl.BlockSpec((rows, states), lambda i: (i, 0))]
+        + [pl.BlockSpec(x.shape, lambda i: (0, 0)) for x in far],
         out_specs=[turned, turned],
         out_shape=[turned_shape, turned_shape],
         **options,
-    )(band, own, paired, *far)
+    )(band, terms, *far)
 
 
 def split_columns(pieces, high_ref, low_ref, first):
@@ -536,32 +582,64 @@
     return call(kernel, after, in_specs=[], grid=(1,), out_specs=corner(shape), out_shape=shape, name="mark")()
 
 
-def finish_kernel(weight, flags_ref, base_ref, one_ref, one_far, two_ref, two_far, *outs):
+def most_kernel(weight, flags_ref, base_ref, one_ref, one_far, two_ref, two_far, *refs):
+    third_refs, outs, rest_ref = refs[:-3], refs[-3:-1], refs[-1]
     one, two = [jnp.where(flags_ref[band] == 1, 1.0, 0.0) for band in (1, 2)]
-    states = outs[0].shape[0]
+    states, width = outs[0].shape
     for half, out_ref in enumerate(outs):
         rows = slice(half * states, (half + 1) * states)
-        total = base_ref[rows, :] + one * (one_ref[rows, :] + one_far[rows, :])
-        out_ref[...] = weight * (total + two * (two_ref[rows, :] + two_far[rows, :]))
-
-
-def finish(weight, at, flags, base, one, one_far, two, two_far, so_far, after):
+        total = base_ref[rows, :width] + one * (one_ref[rows, :] + one_far[rows, :])
+        pair = two_ref[rows, :] + two_far[rows, :]
+        out_ref[...] = weight * (total + two * pair)
+        rest = base_ref[rows, width:] + one * pair
+        third = jnp.concatenate([x[rows, :] for x in third_refs], axis=1)
+        rest_ref[rows, :] = weight * (rest + two * third)
+
+
+def finish_most(weight, flags, base, one, one_far, two, two_far, *third):
     rows, width = one.shape
     states = rows // 2
     whole = pl.BlockSpec((rows, width), lambda i: (0, 0))
-    part = pl.BlockSpec((states, width), lambda i: (0, at))
     shape = jax.ShapeDtypeStruct((states, base.shape[1]), jnp.float32)
     return call(
+        functools.partial(most_kernel, weight),
+        (),
+        grid=(1,),
+        in_specs=[pl.BlockSpec(memory_space=pltpu.SMEM), pl.BlockSpec(base.shape, lambda i: (0, 0))]
+        + [whole] * 4
+        + [pl.BlockSpec(x.shape, lambda i: (0, 0)) for x in third],
+        out_specs=[pl.BlockSpec((states, width), lambda i: (0, 0))] * 2 + [whole],
+        out_shape=[shape, shape, jax.ShapeDtypeStruct((rows, width), jnp.float32)],
+        name="finish_most",
+    )(flags, base, one, one_far, two, two_far, *third)
+
+
+def finish_kernel(weight, upper_ref, lower_ref, *refs):
+    far_refs, outs = refs[:-2], refs[-2:]
+    far_refs = far_refs[: len(far_refs) // 2], far_refs[len(far_refs) // 2 :]
+    for rest_ref, far, out_ref in zip((upper_ref, lower_ref), far_refs, outs):
+        arrived = jnp.concatenate([x[...] for x in far], axis=1)
+        out_ref[...] = rest_ref[...] + weight * arrived
+
+
+def finish(weight, outs, rest, far):
+    states, width = outs[0].shape
+    steps, half = 2, width // 2
+    rows = states // steps
+    upper = lambda size: pl.BlockSpec((rows, size), lambda i: (i, 0))
+    lower = lambda size: pl.BlockSpec((rows, size), lambda i: (i + steps, 0))
+    return call(
         functools.partial(finish_kernel, weight),
-        after,
-        into=[(out, x) for out, x in enumerate(so_far)],
-        grid=(1,),
-        in_specs=[pl.BlockSpec(memory_space=pltpu.SMEM), pl.BlockSpec((rows, width), lambda i: (0, at))]
-        + [whole] * 4,
-        out_specs=[part, part],
-        out_shape=[shape, shape],
+        (),
+        into=list(enumerate(outs)),
+        grid=(steps,),
+        in_specs=[upper(half), lower(half)]
+        + [upper(x.shape[1]) for x in far]
+        + [lower(x.shape[1]) for x in far],
+        out_specs=[pl.BlockSpec((rows, half), lambda i: (i, 1))] * 2,
+        out_shape=[jax.ShapeDtypeStruct((states, width), jnp.float32)] * 2,
         name="finish",
-    )(flags, base, one, one_far, two, two_far)
+    )(rest, rest, *far, *far)
 
 
 def exchange(block, axis, pairs):
@@ -609,9 +687,10 @@
     current_paired = paired(current)
     band, last = prepare(stiff, odd, own, before, at_grid, face_map, y_prev, (current,))
 
+    terms = on_chip(band, current, current_paired, last)
     following, so_far, waited = [], [None] * 3, ()
     for at, piece in enumerate(far):
-        chunk, *so_far = next_degree(band, current, current_paired, piece, last, at, so_far, waited)
+        chunk, *so_far = next_degree(band, terms, piece, at, so_far, waited)
         following.append(chunk)
         waited = (chunk,)
     whole, *y_turned = so_far
@@ -620,7 +699,7 @@
     if not swaps:
         y_next, again, other = from_grid(face_map, whole)
         next_far.append(crossed(other))
-        h_turned = applied_next(band, whole, paired(again), next_far)
+        h_turned = applied_next(band, on_chip(band, whole, paired(again), None), next_far)
         piece = lax.all_gather(whole, "band", axis=1, tiled=True)
         (block,) = both_products(y_turned, h_turned, [piece])
         parts = [
@@ -641,7 +720,7 @@
     ends, middle = [(0, 1), (2, 3)], [(1, 2)]
     first = [exchange(x, "band", ends) for x in following]
     second_middle = [exchange(x, "band", middle) for x in following]
-    waited = (first[0], second_middle[0], next_far[0])
+    waited = (first[0], next_far[0])
     y_next, again, other, second_middle[0] = from_grid(face_map, whole, waited, second_middle[:1])
     next_far.append(crossed(other))
     second_out = [lax.ppermute(second_middle[0], "band", outward)]
@@ -650,7 +729,7 @@
     third_middle = [exchange(first[0], "band", middle)]
     *near, second_middle[1] = sorted_products(keep, y_turned, following, first, 0, (), (), second_middle[1:])
     second_out.append(lax.ppermute(second_middle[1], "band", outward))
-    h_turned = applied_next(band, whole, whole_paired, next_far, (near[0],))
+    h_turned = applied_next(band, on_chip(band, whole, whole_paired, None, near[:1]), next_far)
     (first[1],) = gate(first[1:], (h_turned[0], third_middle[0]))
     third_middle.append(exchange(first[1], "band", middle))
     kept, sent, third_middle[0] = sorted_products(keep, h_turned, following, first, 1, near, (), third_middle[:1])
@@ -661,29 +740,37 @@
     cores = [to_owner(blocks[0], second_owner, 1)]
     (near,) = plus(kept, sent, (blocks[0],))
     near_far = near_across(near)
-    blocks += both_products(y_turned, h_turned, [second_middle[1], second_out[1]], 2, (near, third_middle[1]))
-    second, third_middle[1] = plus(blocks[0], cores[0], (blocks[1],), third_middle[1:])
+    pieces = [second_middle[1], second_out[1]]
+    block, third_middle[1] = both_products(y_turned, h_turned, pieces, 2, (near,), third_middle[1:])
+    blocks.append(block)
+    tails = [third_middle[1][:, : half // 2], third_middle[1][:, half // 2 :]]
+    (second,) = plus(blocks[0], cores[0], (blocks[1],))
     second_far = to_owner(second, second_owner, 2)
-    third_out.append(lax.ppermute(third_middle[1], "band", outward))
+    tails_out = [lax.ppermute(tails[0], "band", outward)]
     keep = jnp.where(core == upper, 1, 0).astype(jnp.int32).reshape(1)
     pieces = (blocks[1], third_middle[0], third_out[0])
     kept, sent = pair_products(keep, y_turned, h_turned, *pieces, (second,))
     sent = paired(sent)
-    (pair,) = plus(kept, sent, (mark((kept,)),))
+    (tails[1],) = gate(tails[1:], (kept, second_far))
+    tails_out.append(lax.ppermute(tails[1], "band", outward))
+    (pair,) = plus(kept, sent, tails[1:])
     pair_route = [
         (((2 - b // 2 * 2 + c) ^ 2) * 4 + b, (2 - b // 2 * 2 + c) * 4 + b) for b in range(4) for c in (0, 1)
     ]
     pair_far = lax.ppermute(pair, ("dom", "band"), pair_route)
-    (block,) = both_products(y_turned, h_turned, [third_middle[1], third_out[1]], 2, (pair,))
-    cores.append(to_owner(block, third_owner, 1))
+    blocks, waited = [], (pair,)
+    for piece in zip(tails, tails_out):
+        blocks += both_products(y_turned, h_turned, list(piece), 2, waited)
+        waited = blocks[-1:]
+    cores = [to_owner(block, third_owner, 1) for block in blocks]
+    third = [*plus(blocks[0], cores[0], blocks[1:])]
+    third += plus(blocks[1], cores[1], third)
+    third_far = [to_owner(block, third_owner, 2) for block in third]
     is_near, is_second = chip == upper, core == upper
     flags = jnp.stack([is_near, ~is_near & is_second, ~is_near & ~is_second]).astype(jnp.int32)
-    base = near_rows(flags, near, near_far, (block, second_far))
-    (third,) = plus(block, cores[1], (base,))
-    third_far = to_owner(third, third_owner, 2)
-    pieces = (second, second_far, pair, pair_far, third, third_far)
-    outs = finish(weight, 0, flags, base, *pieces[:4], (), (third,))
-    return (y_next, *finish(weight, 1, flags, base, *pieces[2:], outs, ()))
+    base = near_rows(flags, near, near_far, (third[1],))
+    *outs, rest = finish_most(weight, flags, base, second, second_far, pair, pair_far, *third)
+    return (y_next, *finish(weight, outs, rest, third_far))
 
 
 def solution(mesh):

time: 220 us -> 216 us (0.982)
  waiting for transfers between devices: 69 us -> 49.9 us
  Pallas kernels: 95.4 us -> 105 us
  starting transfers between devices: 42.7 us -> 47 us
    pallas_call x24 -> x28, Pallas kernels: 95.4 us -> 105 us  [call(): return lambda *args: made(*args, *extra)]
    ppermute x1 -> x2, waiting for transfers between devices: 8.83 us -> 0.47 us  [the longest x1 0.47 us: on_device(): tails_out.append(lax.ppermute(tails[1], 'band', outward))]
    ppermute x14, waiting for transfers between devices: 41.3 us -> 35.5 us  [exchange(): return lax.ppermute(block, axis, pairs + [(b, a) for a, b in pairs])]
    ppermute x1, waiting for transfers between devices: 5.3 us -> 0.01 us  [on_device(): third_out = [lax.ppermute(third_middle[0], 'band', outward)]]
    ppermute x4 -> x6, starting transfers between devices: 7.56 us -> 10.3 us  [to_owner(): return lax.ppermute(block, ('dom', 'band'), route)]
    slice x0 -> x1, local copies, waits for them, and re-layouts: none -> 2.22 us  [on_device(): tails = [third_middle[1][:, :half // 2], third_middle[1][:, half // 2:]]]
    ppermute x4 -> x6, waiting for transfers between devices: 9.67 us -> 11.4 us  [to_owner(): return lax.ppermute(block, ('dom', 'band'), route)]
    unnamed x27 -> x38, local copies, waits for them, and re-layouts: 6.21 us -> 5.89 us
  transfers between devices with their start and end apart: 25 -> 28, of which waited for: 13 -> 10; matrix products, arithmetic and copies ran while one was open for 1% -> 1% of each run, Pallas kernels for 42% -> 48%
where the time goes in v2:
time: 216 us; the launch traced here: 214 us
  Pallas kernels  105 us (49%)
  waiting for transfers between devices  49.9 us (23%)
  starting transfers between devices  47 us (22%)
  local copies, waits for them, and re-layouts  8.11 us (4%)
  other arithmetic  3.2 us (1%)
    pallas_call x28, Pallas kernels, call(): return lambda *args: made(*args, *extra)  105 us
    ppermute x14, waiting for transfers between devices, exchange(): return lax.ppermute(block, axis, pairs + [(b, a) for a, b in pairs])  35.5 us
    ppermute x14, starting transfers between devices, exchange(): return lax.ppermute(block, axis, pairs + [(b, a) for a, b in pairs])  18.3 us
    ppermute x6, waiting for transfers between devices, to_owner(): return lax.ppermute(block, ('dom', 'band'), route)  11.4 us
    ppermute x6, starting transfers between devices, to_owner(): return lax.ppermute(block, ('dom', 'band'), route)  10.3 us
    unnamed x38, local copies, waits for them, and re-layouts  5.89 us
    ppermute x1, starting transfers between devices, on_device(): second_out = [lax.ppermute(second_middle[0], 'band', outward)]  4.52 us
  transfers between devices with their start and end apart: 28, of which 10 were waited for; matrix products, arithmetic and copies ran while one was open for 1% of the time, Pallas kernels for 48%

profile of v2, /device:TPU:18, one launch (start us, length us, event | category | flops | bytes accessed | tf_op | source)
XLA Modules:
  0.0 214.3 jit_solution(16982970605626559986)
XLA Ops:
  10.1 3.7 %to_grid.3 = (f32[1024,256]{1,0:T(8,128)}, f32[1024,512]{1,0:T(8,128)}) custom-call(s32[8,128]{1,0:T(8,128)S(1)} %bitcast.13, f32[1024,512]{1,0:T(8,128)S(1)} %copy-done.2, f32[1024,512]{1,0:T(8,128)} %get-tuple-element.38.refs_2_, f32[1024,256]{1,0:T(8,128)} %get-tuple-element.39.refs_3_), custom_call_target="tpu_custom_call", output_to_operand_aliasing={{1}: (2, {})} | custom-call | flops 999999995904 | bytes 1 | tf_op jit(solution)/shard_map/to_grid/pallas_call | solution.py:81
  16.1 8.4 %prepare.1 = (bf16[3,8,256,256]{3,2,1,0:T(8,128)(2,1)S(1)}, f32[1024,512]{1,0:T(8,128)S(1)}) custom-call(s32[1]{0:T(128)} %bitcast.1.refs_0_, f32[1,1024]{1,0:T(1,128)} %bitcast.3.refs_1_, f32[1,1024]{1,0:T(1,128)} %bitcast.4.refs_2_, f32[1,1024]{1,0:T(1,128)S(1)} %bitcast.16, s32[8,128]{1,0:T(8,128)S(1)} %bitcast.14, f32[1024,512]{1,0:T(8,128)S(1)} %copy-done.3, ...), custom_call_target="tpu_custom_call" | custom-call | flops 999999995904 | bytes 1 | tf_op jit(solution)/shard_map/prepare/pallas_call | solution.py:81
  24.6 5.9 %on_chip.2.refs_1_ = f32[1024,512]{1,0:T(8,128)S(1)} custom-call(bf16[3,8,256,256]{3,2,1,0:T(8,128)(2,1)S(1)} %get-tuple-element.41.refs_0_, f32[1024,512]{1,0:T(8,128)} %get-tuple-element.40.refs_6_.refs_1_, f32[1024,512]{1,0:T(8,128)} %collective-permute-done.1.refs_2_, f32[1024,512]{1,0:T(8,128)S(1)} %get-tuple-element.42.refs_3_), custom_call_target="tpu_custom_call" | custom-call | flops 999999995904 | bytes 1 | tf_op jit(solution)/shard_map/on_chip/pallas_call | solution.py:81
  33.9 3.9 %across.3 = (f32[1024,256]{1,0:T(8,128)}, f32[1024,512]{1,0:T(8,128)S(1)}, bf16[512,1024]{1,0:T(8,128)(2,1)S(1)}, bf16[512,1024]{1,0:T(8,128)(2,1)S(1)}) custom-call(bf16[3,8,256,256]{3,2,1,0:T(8,128)(2,1)S(1)} %get-tuple-element.41.refs_0_, f32[1024,512]{1,0:T(8,128)S(1)} %on_chip.2.refs_1_, f32[1024,256]{1,0:T(8,128)} %collective-permute-done.3.refs_2_), custom_call_target="tpu_custom_call" | custom-call | flops 999999995904 | bytes 1 | tf_op jit(solution)/shard_map/across/pallas_call | solution.py:81
  43.3 13.1 %collective-permute-done.2.refs_2_ = f32[1024,256]{1,0:T(8,128)} collective-permute-done((f32[1024,256]{1,0:T(8,128)}, f32[1024,256]{1,0:T(8,128)}, u32[]{:S(2)}, u32[]{:S(2)}) %collective-permute-start.2) | collective-permute-done | bytes 1048608 | tf_op jit(solution)/shard_map/ppermute | solution.py:646
  56.4 3.9 %across.4 = (f32[1024,256]{1,0:T(8,128)}, f32[1024,512]{1,0:T(8,128)S(1)}, bf16[512,1024]{1,0:T(8,128)(2,1)S(1)}, bf16[512,1024]{1,0:T(8,128)(2,1)S(1)}) custom-call(bf16[3,8,256,256]{3,2,1,0:T(8,128)(2,1)S(1)} %get-tuple-element.41.refs_0_, f32[1024,512]{1,0:T(8,128)S(1)} %on_chip.2.refs_1_, ...), custom_call_target="tpu_custom_call", output_to_operand_aliasing={{1}: (3, {}), {2}: (4, {}), {3}: (5, {})} | custom-call | flops 999999995904 | bytes 1 | tf_op jit(solution)/shard_map/across/pallas_call | solution.py:81
  65.5 12.6 %collective-permute-done.5.refs_3_.refs_2_ = f32[1024,256]{1,0:T(8,128)} collective-permute-done((f32[1024,256]{1,0:T(8,128)}, f32[1024,256]{1,0:T(8,128)}, u32[]{:S(2)}, u32[]{:S(2)}) %collective-permute-start.5) | collective-permute-done | bytes 1048608 | tf_op jit(solution)/shard_map/ppermute | solution.py:646
  78.1 5.0 %from_grid.1 = (f32[1024,512]{1,0:T(8,128)}, f32[1024,512]{1,0:T(8,128)}, f32[1024,256]{1,0:T(8,128)}, f32[1024,256]{1,0:T(8,128)}) custom-call(s32[1,1024]{1,0:T(1,128)S(1)} %bitcast.15, f32[1024,512]{1,0:T(8,128)S(1)} %get-tuple-element.48.refs_1_, f32[1024,256]{1,0:T(8,128)} %collective-permute-done.4.refs_2_.refs_3_, ...), custom_call_target="tpu_custom_call", output_to_operand_aliasing={{3}: (4, {})} | custom-call | flops 999999995904 | bytes 1 | tf_op jit(solution)/shard_map/from_grid/pallas_call | solution.py:81
  86.9 4.5 %collective-permute-start.13 = (f32[1024,256]{1,0:T(8,128)}, f32[1024,256]{1,0:T(8,128)}, u32[]{:S(2)}, u32[]{:S(2)}) collective-permute-start(f32[1024,256]{1,0:T(8,128)} %get-tuple-element.61.refs_4_), channel_id=1, source_target_pairs={{2,3},{1,0},{6,7},{5,4},{10,11},{9,8},{14,15},{13,12},{18,19},{17,... | collective-permute-start | bytes 3145736 | tf_op jit(solution)/shard_map/ppermute | solution.py:726
  94.8 7.4 %sorted_products.2 = (f32[1024,512]{1,0:T(8,128)S(1)}, f32[1024,512]{1,0:T(8,128)}, f32[1024,256]{1,0:T(8,128)}) custom-call(s32[1]{0:T(128)} %bitcast.10.refs_0_, bf16[512,1024]{1,0:T(8,128)(2,1)S(1)} %copy-done.9, bf16[512,1024]{1,0:T(8,128)(2,1)S(1)} %copy-done.14, ...), custom_call_target="tpu_custom_call", output_to_operand_aliasing={{2}: (7, {})} | custom-call | flops 999999995904 | bytes 1 | tf_op jit(solution)/shard_map/sorted_products/pallas_call | solution.py:81
  104.5 5.2 %on_chip.3.refs_1_ = f32[1024,512]{1,0:T(8,128)S(1)} custom-call(bf16[3,8,256,256]{3,2,1,0:T(8,128)(2,1)S(1)} %get-tuple-element.41.refs_0_, f32[1024,512]{1,0:T(8,128)S(1)} %get-tuple-element.48.refs_1_, f32[1024,512]{1,0:T(8,128)} %collective-permute-done.7.refs_1_.refs_2_, f32[1024,512]{1,0:T(8,128)S(1)} %get-tuple-element.54.refs_3_.refs_7_), custom_call_target="tpu_custom_call" | custom-call | flops 999999995904 | bytes 1 | tf_op jit(solution)/shard_map/on_chip/pallas_call | solution.py:81
  111.4 4.4 %across.5 = (bf16[512,1024]{1,0:T(8,128)(2,1)S(1)}, bf16[512,1024]{1,0:T(8,128)(2,1)S(1)}) custom-call(bf16[3,8,256,256]{3,2,1,0:T(8,128)(2,1)S(1)} %get-tuple-element.41.refs_0_, f32[1024,512]{1,0:T(8,128)S(1)} %on_chip.3.refs_1_, f32[1024,256]{1,0:T(8,128)} %collective-permute-done.5.refs_3_.refs_2_, f32[1024,256]{1,0:T(8,128)} %collective-permute-done.10.refs_3_), custom_call_target="tpu_custom_call" | custom-call | flops 999999995904 | bytes 1 | tf_op jit(solution)/shard_map/across/pallas_call | solution.py:81
  115.8 4.6 %collective-permute-done.11.refs_1_.refs_9_ = f32[1024,256]{1,0:T(8,128)} collective-permute-done((f32[1024,256]{1,0:T(8,128)}, f32[1024,256]{1,0:T(8,128)}, u32[]{:S(2)}, u32[]{:S(2)}) %collective-permute-start.11) | collective-permute-done | bytes 1048608 | tf_op jit(solution)/shard_map/ppermute | solution.py:646
  123.9 7.5 %sorted_products.3 = (f32[1024,512]{1,0:T(8,128)S(1)}, f32[1024,512]{1,0:T(8,128)}, f32[1024,256]{1,0:T(8,128)}) custom-call(s32[1]{0:T(128)} %bitcast.10.refs_0_, bf16[512,1024]{1,0:T(8,128)(2,1)S(1)} %get-tuple-element.56.refs_0_.refs_1_.refs_2_.refs_3_, ...), custom_call_target="tpu_custom_call", output_to_operand_aliasing={{0}: (7, {}), {1}: (8, {}), {2}: (9, {})} | custom-call | flops 999999995904 | bytes 1 | tf_op jit(solution)/shard_map/sorted_products/pallas_call | solution.py:81
  133.6 5.0 %both_products.4.refs_2_.refs_0_ = f32[1024,256]{1,0:T(8,128)} custom-call(bf16[512,1024]{1,0:T(8,128)(2,1)S(1)} %copy-done.10, bf16[512,1024]{1,0:T(8,128)(2,1)S(1)} %copy-done.15, bf16[512,1024]{1,0:T(8,128)(2,1)S(1)} %get-tuple-element.56.refs_0_.refs_1_.refs_2_.refs_3_, bf16[512,1024]{1,0:T(8,128)(2,1)S(1)} %get-tuple-element.57.refs_2_.refs_3_.refs_4_, ...), custom_call_target="tpu_custom_call" | custom-call | flops 999999995904 | bytes 1 | tf_op jit(solution)/shard_map/both_products/pallas_call | solution.py:81
  138.6 3.5 %collective-permute-start.18 = (f32[1024,256]{1,0:T(8,128)}, f32[1024,256]{1,0:T(8,128)}, u32[]{:S(2)}, u32[]{:S(2)}) collective-permute-start(f32[1024,256]{1,0:T(8,128)} %both_products.4.refs_2_.refs_0_), channel_id=1, source_target_pairs={{12,8},{4,0},{13,9},{5,1},{2,6},{10,14},{3,7},{11,15},{28,24},{20,... | collective-permute-start | bytes 3145736 | tf_op jit(solution)/shard_map/ppermute | solution.py:664
  144.9 4.0 %collective-permute-start.14 = (f32[1024,512]{1,0:T(8,128)}, f32[1024,512]{1,0:T(8,128)}, u32[]{:S(2)}, u32[]{:S(2)}) collective-permute-start(f32[1024,512]{1,0:T(8,128)} %plus.5.refs_6_.refs_1_), channel_id=1, source_target_pairs={{8,0},{12,4},{9,1},{13,5},{2,10},{6,14},{3,11},{7,15},{24,16},{28,... | collective-permute-start | bytes 6291464 | tf_op jit(solution)/shard_map/ppermute | solution.py:717
  148.9 4.7 %both_products.5 = (f32[1024,256]{1,0:T(8,128)S(1)}, f32[1024,256]{1,0:T(8,128)}) custom-call(bf16[512,1024]{1,0:T(8,128)(2,1)S(1)} %copy-done.11, bf16[512,1024]{1,0:T(8,128)(2,1)S(1)} %copy-done.16, bf16[512,1024]{1,0:T(8,128)(2,1)S(1)} %get-tuple-element.56.refs_0_.refs_1_.refs_2_.refs_3_, ...), custom_call_target="tpu_custom_call", output_to_operand_aliasing={{1}: (7, {})} | custom-call | flops 999999995904 | bytes 1 | tf_op jit(solution)/shard_map/both_products/pallas_call | solution.py:81
  162.2 5.0 %pair_products.1 = (f32[1024,256]{1,0:T(8,128)S(1)}, f32[1024,256]{1,0:T(8,128)}) custom-call(s32[1]{0:T(128)} %bitcast.11.refs_0_, bf16[512,1024]{1,0:T(8,128)(2,1)S(1)} %copy-done.12, bf16[512,1024]{1,0:T(8,128)(2,1)S(1)} %copy-done.17, bf16[512,1024]{1,0:T(8,128)(2,1)S(1)} %get-tuple-element.56.refs_0_.refs_1_.refs_2_.refs_3_, ...), custom_call_target="tpu_custom_call" | custom-call | flops 999999995904 | bytes 1 | tf_op jit(solution)/shard_map/pair_products/pallas_call | solution.py:81
  174.0 4.4 %both_products.6.refs_6_.refs_0_ = f32[1024,128]{1,0:T(8,128)} custom-call(bf16[512,1024]{1,0:T(8,128)(2,1)S(1)} %copy-done.12, bf16[512,1024]{1,0:T(8,128)(2,1)S(1)} %copy-done.17, bf16[512,1024]{1,0:T(8,128)(2,1)S(1)} %get-tuple-element.56.refs_0_.refs_1_.refs_2_.refs_3_, bf16[512,1024]{1,0:T(8,128)(2,1)S(1)} %copy-done.7, ...), custom_call_target="tpu_custom_call" | custom-call | flops 999999995904 | bytes 1 | tf_op jit(solution)/shard_map/both_products/pallas_call | solution.py:81
  180.1 4.3 %both_products.7.refs_2_.refs_0_ = f32[1024,128]{1,0:T(8,128)} custom-call(bf16[512,1024]{1,0:T(8,128)(2,1)S(1)} %copy-done.12, bf16[512,1024]{1,0:T(8,128)(2,1)S(1)} %copy-done.17, bf16[512,1024]{1,0:T(8,128)(2,1)S(1)} %get-tuple-element.56.refs_0_.refs_1_.refs_2_.refs_3_, bf16[512,1024]{1,0:T(8,128)(2,1)S(1)} %copy-done.7, ...), custom_call_target="tpu_custom_call" | custom-call | flops 999999995904 | bytes 1 | tf_op jit(solution)/shard_map/both_products/pallas_call | solution.py:81
  198.9 3.6 %finish_most.1 = (f32[512,512]{1,0:T(8,128)}, f32[512,512]{1,0:T(8,128)}, f32[1024,256]{1,0:T(8,128)S(1)}) custom-call(s32[3]{0:T(128)S(1)} %add_convert_fusion.refs_0_, f32[1024,512]{1,0:T(8,128)S(1)} %near_rows.1.refs_1_, f32[1024,256]{1,0:T(8,128)} %plus.6.refs_8_.refs_2_, f32[1024,256]{1,0:T(8,128)} %collective-permute-done.19.refs_1_.refs_3_, ...), custom_call_target="tpu_custom_call" | custom-call | flops 999999995904 | bytes 1 | tf_op jit(solution)/shard_map/finish_most/pallas_call | solution.py:81
  202.5 4.0 %collective-permute-done.26.refs_2_.refs_4_ = f32[1024,128]{1,0:T(8,128)} collective-permute-done((f32[1024,128]{1,0:T(8,128)}, f32[1024,128]{1,0:T(8,128)}, u32[]{:S(2)}, u32[]{:S(2)}) %collective-permute-start.26) | collective-permute-done | bytes 524320 | tf_op jit(solution)/shard_map/ppermute | solution.py:664
  206.5 5.6 %collective-permute-done.27.refs_3_.refs_5_ = f32[1024,128]{1,0:T(8,128)} collective-permute-done((f32[1024,128]{1,0:T(8,128)}, f32[1024,128]{1,0:T(8,128)}, u32[]{:S(2)}, u32[]{:S(2)}) %collective-permute-start.27) | collective-permute-done | bytes 524320 | tf_op jit(solution)/shard_map/ppermute | solution.py:664
  (103 shorter events, 79.1 us)
Async XLA Ops:
  3.2 12.9 %collective-permute-start = (f32[1024]{0:T(1024)}, f32[1024]{0:T(1024)}, u32[]{:S(2)}, u32[]{:S(2)}) collective-permute-start(f32[1024]{0:T(1024)} %select_reduce_fusion.1), channel_id=1, source_target_pairs={{0,4},{4,8},{8,12},{12,0},{1,5},{5,9},{9,13},{13,1},{2,6},{6,10},{... | collective-permute-start | bytes 12296 | tf_op jit(solution)/shard_map/ppermute | solution.py:677
  8.3 25.6 %collective-permute-start.3 = (f32[1024,256]{1,0:T(8,128)}, f32[1024,256]{1,0:T(8,128)}, u32[]{:S(2)}, u32[]{:S(2)}) collective-permute-start(f32[1024,256]{1,0:T(8,128)} %get-tuple-element.39.refs_3_), channel_id=1, source_target_pairs={{4,8},{12,0},{8,4},{0,12},{5,9},{13,1},{9,5},{1,13},{6,10},{14,2},... | collective-permute-start | bytes 3145736 | tf_op jit(solution)/shard_map/ppermute | solution.py:646
  13.8 10.8 %collective-permute-start.1 = (f32[1024,512]{1,0:T(8,128)}, f32[1024,512]{1,0:T(8,128)}, u32[]{:S(2)}, u32[]{:S(2)}) collective-permute-start(f32[1024,512]{1,0:T(8,128)} %get-tuple-element.40.refs_6_.refs_1_), channel_id=1, source_target_pairs={{0,4},{8,12},{4,0},{12,8},{1,5},{9,13},{5,1},{13,9},{2,6},{10,14},... | collective-permute-start | bytes 6291464 | tf_op jit(solution)/shard_map/ppermute | solution.py:646
  13.8 42.6 %collective-permute-start.2 = (f32[1024,256]{1,0:T(8,128)}, f32[1024,256]{1,0:T(8,128)}, u32[]{:S(2)}, u32[]{:S(2)}) collective-permute-start(f32[1024,256]{1,0:T(8,128)} %get-tuple-element.43), channel_id=1, source_target_pairs={{4,8},{12,0},{8,4},{0,12},{5,9},{13,1},{9,5},{1,13},{6,10},{14,2},... | collective-permute-start | bytes 3145736 | tf_op jit(solution)/shard_map/ppermute | solution.py:646
  37.8 27.6 %collective-permute-start.4 = (f32[1024,256]{1,0:T(8,128)}, f32[1024,256]{1,0:T(8,128)}, u32[]{:S(2)}, u32[]{:S(2)}) collective-permute-start(f32[1024,256]{1,0:T(8,128)} %get-tuple-element.47.refs_6_.refs_3_), channel_id=1, source_target_pairs={{0,1},{2,3},{1,0},{3,2},{4,5},{6,7},{5,4},{7,6},{8,9},{10,11},{9,8... | collective-permute-start | bytes 3145736 | tf_op jit(solution)/shard_map/ppermute | solution.py:646
  39.4 38.7 %collective-permute-start.5 = (f32[1024,256]{1,0:T(8,128)}, f32[1024,256]{1,0:T(8,128)}, u32[]{:S(2)}, u32[]{:S(2)}) collective-permute-start(f32[1024,256]{1,0:T(8,128)} %get-tuple-element.47.refs_6_.refs_3_), channel_id=1, source_target_pairs={{4,8},{12,0},{8,4},{0,12},{5,9},{13,1},{9,5},{1,13},{6,10},{14,2},... | collective-permute-start | bytes 3145736 | tf_op jit(solution)/shard_map/ppermute | solution.py:646
  41.3 36.8 %collective-permute-start.6 = (f32[1024,256]{1,0:T(8,128)}, f32[1024,256]{1,0:T(8,128)}, u32[]{:S(2)}, u32[]{:S(2)}) collective-permute-start(f32[1024,256]{1,0:T(8,128)} %get-tuple-element.47.refs_6_.refs_3_), channel_id=1, source_target_pairs={{1,2},{2,1},{5,6},{6,5},{9,10},{10,9},{13,14},{14,13},{17,18},{18,... | collective-permute-start | bytes 3145736 | tf_op jit(solution)/shard_map/ppermute | solution.py:646
  62.3 29.1 %collective-permute-start.8 = (f32[1024,256]{1,0:T(8,128)}, f32[1024,256]{1,0:T(8,128)}, u32[]{:S(2)}, u32[]{:S(2)}) collective-permute-start(f32[1024,256]{1,0:T(8,128)} %get-tuple-element.53.refs_4_), channel_id=1, source_target_pairs={{1,2},{2,1},{5,6},{6,5},{9,10},{10,9},{13,14},{14,13},{17,18},{18,... | collective-permute-start | bytes 3145736 | tf_op jit(solution)/shard_map/ppermute | solution.py:646
  64.6 30.2 %collective-permute-start.9 = (f32[1024,256]{1,0:T(8,128)}, f32[1024,256]{1,0:T(8,128)}, u32[]{:S(2)}, u32[]{:S(2)}) collective-permute-start(f32[1024,256]{1,0:T(8,128)} %get-tuple-element.53.refs_4_), channel_id=1, source_target_pairs={{0,1},{2,3},{1,0},{3,2},{4,5},{6,7},{5,4},{7,6},{8,9},{10,11},{9,8... | collective-permute-start | bytes 3145736 | tf_op jit(solution)/shard_map/ppermute | solution.py:646
  85.8 25.6 %collective-permute-start.10 = (f32[1024,256]{1,0:T(8,128)}, f32[1024,256]{1,0:T(8,128)}, u32[]{:S(2)}, u32[]{:S(2)}) collective-permute-start(f32[1024,256]{1,0:T(8,128)} %get-tuple-element.55), channel_id=1, source_target_pairs={{4,8},{12,0},{8,4},{0,12},{5,9},{13,1},{9,5},{1,13},{6,10},{14,2},... | collective-permute-start | bytes 3145736 | tf_op jit(solution)/shard_map/ppermute | solution.py:646
  86.9 46.7 %collective-permute-start.13 = (f32[1024,256]{1,0:T(8,128)}, f32[1024,256]{1,0:T(8,128)}, u32[]{:S(2)}, u32[]{:S(2)}) collective-permute-start(f32[1024,256]{1,0:T(8,128)} %get-tuple-element.61.refs_4_), channel_id=1, source_target_pairs={{2,3},{1,0},{6,7},{5,4},{10,11},{9,8},{14,15},{13,12},{18,19},{17,... | collective-permute-start | bytes 3145736 | tf_op jit(solution)/shard_map/ppermute | solution.py:726
  92.9 27.5 %collective-permute-start.11 = (f32[1024,256]{1,0:T(8,128)}, f32[1024,256]{1,0:T(8,128)}, u32[]{:S(2)}, u32[]{:S(2)}) collective-permute-start(f32[1024,256]{1,0:T(8,128)} %gate.3.refs_5_), channel_id=1, source_target_pairs={{1,2},{2,1},{5,6},{6,5},{9,10},{10,9},{13,14},{14,13},{17,18},{18,... | collective-permute-start | bytes 3145736 | tf_op jit(solution)/shard_map/ppermute | solution.py:646
  102.2 46.7 %collective-permute-start.15 = (f32[1024,256]{1,0:T(8,128)}, f32[1024,256]{1,0:T(8,128)}, u32[]{:S(2)}, u32[]{:S(2)}) collective-permute-start(f32[1024,256]{1,0:T(8,128)} %get-tuple-element.62.refs_4_), channel_id=1, source_target_pairs={{2,3},{1,0},{6,7},{5,4},{10,11},{9,8},{14,15},{13,12},{18,19},{17,... | collective-permute-start | bytes 3145736 | tf_op jit(solution)/shard_map/ppermute | solution.py:731
  121.6 27.2 %collective-permute-start.16 = (f32[1024,256]{1,0:T(8,128)}, f32[1024,256]{1,0:T(8,128)}, u32[]{:S(2)}, u32[]{:S(2)}) collective-permute-start(f32[1024,256]{1,0:T(8,128)} %gate.4.refs_6_), channel_id=1, source_target_pairs={{1,2},{2,1},{5,6},{6,5},{9,10},{10,9},{13,14},{14,13},{17,18},{18,... | collective-permute-start | bytes 3145736 | tf_op jit(solution)/shard_map/ppermute | solution.py:646
  131.3 10.7 %collective-permute-start.12 = (f32[1024,512]{1,0:T(8,128)}, f32[1024,512]{1,0:T(8,128)}, u32[]{:S(2)}, u32[]{:S(2)}) collective-permute-start(f32[1024,512]{1,0:T(8,128)} %get-tuple-element.60), channel_id=1, source_target_pairs={{0,4},{8,12},{4,0},{12,8},{1,5},{9,13},{5,1},{13,9},{2,6},{10,14},... | collective-permute-start | bytes 6291464 | tf_op jit(solution)/shard_map/ppermute | solution.py:646
  131.3 30.8 %collective-permute-start.17 = (f32[1024,256]{1,0:T(8,128)}, f32[1024,256]{1,0:T(8,128)}, u32[]{:S(2)}, u32[]{:S(2)}) collective-permute-start(f32[1024,256]{1,0:T(8,128)} %get-tuple-element.64.refs_6_), channel_id=1, source_target_pairs={{2,3},{1,0},{6,7},{5,4},{10,11},{9,8},{14,15},{13,12},{18,19},{17,... | collective-permute-start | bytes 3145736 | tf_op jit(solution)/shard_map/ppermute | solution.py:736
  138.6 15.1 %collective-permute-start.18 = (f32[1024,256]{1,0:T(8,128)}, f32[1024,256]{1,0:T(8,128)}, u32[]{:S(2)}, u32[]{:S(2)}) collective-permute-start(f32[1024,256]{1,0:T(8,128)} %both_products.4.refs_2_.refs_0_), channel_id=1, source_target_pairs={{12,8},{4,0},{13,9},{5,1},{2,6},{10,14},{3,7},{11,15},{28,24},{20,... | collective-permute-start | bytes 3145736 | tf_op jit(solution)/shard_map/ppermute | solution.py:664
  144.9 49.0 %collective-permute-start.14 = (f32[1024,512]{1,0:T(8,128)}, f32[1024,512]{1,0:T(8,128)}, u32[]{:S(2)}, u32[]{:S(2)}) collective-permute-start(f32[1024,512]{1,0:T(8,128)} %plus.5.refs_6_.refs_1_), channel_id=1, source_target_pairs={{8,0},{12,4},{9,1},{13,5},{2,10},{6,14},{3,11},{7,15},{24,16},{28,... | collective-permute-start | bytes 6291464 | tf_op jit(solution)/shard_map/ppermute | solution.py:717
  156.2 11.0 %collective-permute-start.19 = (f32[1024,256]{1,0:T(8,128)}, f32[1024,256]{1,0:T(8,128)}, u32[]{:S(2)}, u32[]{:S(2)}) collective-permute-start(f32[1024,256]{1,0:T(8,128)} %plus.6.refs_8_.refs_2_), channel_id=1, source_target_pairs={{0,8},{1,9},{14,6},{15,7},{16,24},{17,25},{30,22},{31,23}} | collective-permute-start | bytes 3145736 | tf_op jit(solution)/shard_map/ppermute | solution.py:664
  160.1 13.9 %collective-permute-start.21 = (f32[1024,128]{1,0:T(8,128)}, f32[1024,128]{1,0:T(8,128)}, u32[]{:S(2)}, u32[]{:S(2)}) collective-permute-start(f32[1024,128]{1,0:T(8,128)} %get-tuple-element.73.refs_4_), channel_id=1, source_target_pairs={{2,3},{1,0},{6,7},{5,4},{10,11},{9,8},{14,15},{13,12},{18,19},{17,... | collective-permute-start | bytes 1572872 | tf_op jit(solution)/shard_map/ppermute | solution.py:749
  168.5 11.6 %collective-permute-start.20 = (f32[1024,128]{1,0:T(8,128)}, f32[1024,128]{1,0:T(8,128)}, u32[]{:S(2)}, u32[]{:S(2)}) collective-permute-start(f32[1024,128]{1,0:T(8,128)} %gate.5.refs_2_.refs_4_), channel_id=1, source_target_pairs={{2,3},{1,0},{6,7},{5,4},{10,11},{9,8},{14,15},{13,12},{18,19},{17,... | collective-permute-start | bytes 1572872 | tf_op jit(solution)/shard_map/ppermute | solution.py:755
  172.7 26.2 %collective-permute-start.25 = (f32[1024,256]{1,0:T(8,128)}, f32[1024,256]{1,0:T(8,128)}, u32[]{:S(2)}, u32[]{:S(2)}) collective-permute-start(f32[1024,256]{1,0:T(8,128)} %plus.7.refs_6_.refs_4_), channel_id=1, source_target_pairs={{0,8},{4,12},{1,9},{5,13},{10,2},{14,6},{11,3},{15,7},{16,24},{20,... | collective-permute-start | bytes 3145736 | tf_op jit(solution)/shard_map/ppermute | solution.py:760
  187.7 18.9 %collective-permute-start.26 = (f32[1024,128]{1,0:T(8,128)}, f32[1024,128]{1,0:T(8,128)}, u32[]{:S(2)}, u32[]{:S(2)}) collective-permute-start(f32[1024,128]{1,0:T(8,128)} %plus.8.refs_2_.refs_6_), channel_id=1, source_target_pairs={{4,12},{5,13},{10,2},{11,3},{20,28},{21,29},{26,18},{27,19}} | collective-permute-start | bytes 1572872 | tf_op jit(solution)/shard_map/ppermute | solution.py:664
  192.6 19.5 %collective-permute-start.27 = (f32[1024,128]{1,0:T(8,128)}, f32[1024,128]{1,0:T(8,128)}, u32[]{:S(2)}, u32[]{:S(2)}) collective-permute-start(f32[1024,128]{1,0:T(8,128)} %plus.9.refs_3_.refs_7_), channel_id=1, source_target_pairs={{4,12},{5,13},{10,2},{11,3},{20,28},{21,29},{26,18},{27,19}} | collective-permute-start | bytes 1572872 | tf_op jit(solution)/shard_map/ppermute | solution.py:664
  (23 other events, 138.2 us)

commit v3 on v2

--- a/solution.py
+++ b/solution.py
@@ -50,7 +50,7 @@
     return pl.BlockSpec((rows, 128), lambda *_: (0, 0))
 
 
-def call(kernel, after, *, in_specs, out_specs, out_shape, name, into=(), passed=(), **options):
+def call(kernel, after, *, in_specs, out_specs, out_shape, name, into=(), passed=(), params=None, **options):
     count = len(in_specs)
     extra = [*[array for _, array in into], *after, *passed]
     aliases = {count + at: out for at, (out, _) in enumerate(into)}
@@ -73,7 +73,7 @@
         out_specs=out_specs,
         out_shape=out_shape,
         input_output_aliases=aliases,
-        compiler_params=PARAMS,
+        compiler_params=params or PARAMS,
         cost_estimate=COST,
         name=name,
         **options,
@@ -104,22 +104,31 @@
     )(left, right)
 
 
-def to_grid_kernel(map_ref, x_ref, out_ref, whole_ref, high_ref, low_ref):
+def to_grid_kernel(at, map_hbm, x_hbm, out_ref, whole_ref, map_ref, x_ref, high_ref, low_ref, sems):
     step = pl.program_id(0)
+    width = x_ref.shape[1]
 
     @pl.when(step == 0)
     def _():
+        copies = [
+            pltpu.make_async_copy(x_hbm.at[:, pl.ds(at * width, width)], x_ref, sems.at[0]),
+            pltpu.make_async_copy(map_hbm, map_ref, sems.at[1]),
+        ]
+        for copy in copies:
+            copy.start()
+        for copy in copies:
+            copy.wait()
         high_ref[...], low_ref[...] = halves(x_ref[...])
 
     rows, nodes = out_ref.shape[0], x_ref.shape[0]
     place = lax.broadcasted_iota(jnp.int32, (BLOCK, nodes), 1)
-    for at in range(rows // BLOCK):
-        row = map_ref[pl.ds(step * (rows // BLOCK) + at, 1), :]
+    for part in range(rows // BLOCK):
+        row = map_ref[pl.ds(step * (rows // BLOCK) + part, 1), :]
         column = jnp.broadcast_to(row, (BLOCK, BLOCK)).T
         column = jnp.concatenate([column] * (nodes // BLOCK), axis=1)
         pick = jnp.where(place == column, 1.0, 0.0).astype(jnp.bfloat16)
         moved = dot(pick, high_ref[...]) + dot(pick, low_ref[...])
-        out = slice(at * BLOCK, (at + 1) * BLOCK)
+        out = slice(part * BLOCK, (part + 1) * BLOCK)
         out_ref[out, :] = moved
         whole_ref[out, :] = moved
 
@@ -127,56 +136,66 @@
 def to_grid(face_map, x, at, width, so_far, after):
     nodes, states = x.shape
     rows = 512
-    return call(
-        to_grid_kernel,
-        after,
+    places = (nodes // BLOCK, BLOCK)
+    return call(
+        functools.partial(to_grid_kernel, at),
+        after,
+        params=pltpu.CompilerParams(vmem_limit_bytes=(60 if at == 0 else 32) * 1024 * 1024),
         into=[(1, so_far)] if at else [],
         grid=(nodes // rows,),
-        in_specs=[
-            pl.BlockSpec((nodes // BLOCK, BLOCK), lambda i: (0, 0)),
-            pl.BlockSpec((nodes, width), lambda i: (0, at)),
-        ],
+        in_specs=[pl.BlockSpec(memory_space=pltpu.HBM)] * 2,
         out_specs=[pl.BlockSpec((rows, width), lambda i: (i, 0)), pl.BlockSpec((rows, width), lambda i: (i, at))],
         out_shape=[
             jax.ShapeDtypeStruct((nodes, width), jnp.float32),
             jax.ShapeDtypeStruct((nodes, states), jnp.float32),
         ],
-        scratch_shapes=[pltpu.VMEM((nodes, width), jnp.bfloat16)] * 2,
+        scratch_shapes=[pltpu.VMEM(places, jnp.int32), pltpu.VMEM((nodes, width), jnp.float32)]
+        + [pltpu.VMEM((nodes, width), jnp.bfloat16)] * 2
+        + [pltpu.SemaphoreType.DMA((2,))],
         name="to_grid",
-    )(face_map.reshape(nodes // BLOCK, BLOCK), x)
-
-
-def from_grid_kernel(map_ref, x_ref, out_ref, again_ref, half_ref, high_ref, low_ref):
+    )(face_map.reshape(places), x)
+
+
+def from_grid_kernel(map_ref, *refs):
+    pieces, refs = refs[:-7], refs[-7:]
+    out_ref, again_ref, half_ref, turned_high, turned_low, high_ref, low_ref = refs
     step = pl.program_id(0)
 
     @pl.when(step == 0)
     def _():
-        high_ref[...], low_ref[...] = halves(x_ref[...])
+        split_columns([[x] for x in pieces], high_ref, low_ref, 0)
 
     rows, nodes = out_ref.shape[0], high_ref.shape[0]
     node = lax.broadcasted_iota(jnp.int32, (rows, nodes), 0) + step * rows
     pick = jnp.where(node == map_ref[...], 1.0, 0.0).astype(jnp.bfloat16)
     out_ref[...] = dot(pick, high_ref[...]) + dot(pick, low_ref[...])
-    again = x_ref[pl.ds(pl.multiple_of(step * rows, rows), rows), :]
+    here = pl.ds(pl.multiple_of(step * rows, rows), rows)
+    again = jnp.concatenate([x[here, :] for x in pieces], axis=1)
     again_ref[...] = again
     half_ref[...] = again[:, half_ref.shape[1] :]
-
-
-def from_grid(face_map, x, after=(), passed=()):
-    nodes, states = x.shape
+    turned_high[...], turned_low[...] = halves(again.T)
+
+
+def from_grid(face_map, pieces, after=(), passed=()):
+    nodes = pieces[0].shape[0]
+    states = sum(x.shape[1] for x in pieces)
     rows = 256
     part = pl.BlockSpec((rows, states), lambda i: (i, 0))
+    turned = pl.BlockSpec((states, rows), lambda i: (0, i))
+    sizes = (states, states, states // 2)
     return call(
         from_grid_kernel,
         after,
         passed=passed,
         grid=(nodes // rows,),
-        in_specs=[pl.BlockSpec((1, nodes), lambda i: (0, 0)), pl.BlockSpec((nodes, states), lambda i: (0, 0))],
-        out_specs=[part, part, pl.BlockSpec((rows, states // 2), lambda i: (i, 0))],
-        out_shape=[jax.ShapeDtypeStruct((nodes, size), jnp.float32) for size in (states, states, states // 2)],
+        in_specs=[pl.BlockSpec((1, nodes), lambda i: (0, 0))]
+        + [pl.BlockSpec(x.shape, lambda i: (0, 0)) for x in pieces],
+        out_specs=[part, part, pl.BlockSpec((rows, states // 2), lambda i: (i, 0)), turned, turned],
+        out_shape=[jax.ShapeDtypeStruct((nodes, size), jnp.float32) for size in sizes]
+        + [jax.ShapeDtypeStruct((states, nodes), jnp.bfloat16)] * 2,
         scratch_shapes=[pltpu.VMEM((nodes, states), jnp.bfloat16)] * 2,
         name="from_grid",
-    )(face_map.reshape(1, nodes), x)
+    )(face_map.reshape(1, nodes), *pieces)
 
 
 def plane_terms(shifted, stiff, layer):
@@ -337,31 +356,29 @@
         total = applied_rows(band_ref, at, wide, first)
         rows = pl.ds(at * BLOCK, BLOCK)
         if filtered:
-            total = (2.0 / half_width) * total
-        total = part_ref[rows, :] + total
-        for out_ref in outs[:-2]:
-            out_ref[rows, :] = total
-        for out_ref, half in zip(outs[-2:], halves(total.T)):
-            out_ref[:, rows] = half
+            outs[0][rows, :] = part_ref[rows, :] + (2.0 / half_width) * total
+        else:
+            outs[0][:, rows], outs[1][:, rows] = halves((part_ref[rows, :] + total).T)
 
 
 PER_STEP = 2
 
 
-def on_chip(band, own, paired, last, after=()):
+def on_chip(band, own, paired, last, first=0, width=None, after=()):
     nodes, states = own.shape
-    rows = PER_STEP * BLOCK
-    whole = pl.BlockSpec((nodes, states), lambda i: (0, 0))
-    part = pl.BlockSpec((rows, states), lambda i: (i, 0))
+    rows, width = PER_STEP * BLOCK, width or states
+    at = first // width
+    column = pl.BlockSpec((nodes, width), lambda i: (0, at))
+    part = pl.BlockSpec((rows, width), lambda i: (i, at))
     return call(
         functools.partial(on_chip_kernel, last is not None),
         after,
         grid=(nodes // rows,),
-        in_specs=[pl.BlockSpec((2, PER_STEP, 2 * BLOCK, WINDOW), lambda i: (0, i, 0, 0)), whole, whole]
+        in_specs=[pl.BlockSpec((2, PER_STEP, 2 * BLOCK, WINDOW), lambda i: (0, i, 0, 0)), column, column]
         + [part] * (last is not None),
-        out_specs=part,
-        out_shape=jax.ShapeDtypeStruct((nodes, states), jnp.float32),
-        scratch_shapes=[pltpu.VMEM((2, nodes + 2 * MARGIN, 2 * states), jnp.bfloat16)],
+        out_specs=pl.BlockSpec((rows, width), lambda i: (i, 0)),
+        out_shape=jax.ShapeDtypeStruct((nodes, width), jnp.float32),
+        scratch_shapes=[pltpu.VMEM((2, nodes + 2 * MARGIN, 2 * width), jnp.bfloat16)],
         name="on_chip",
     )(band, own, paired, *([] if last is None else [last]))
 
@@ -375,26 +392,17 @@
     ), pl.BlockSpec((1, PER_STEP, 2 * BLOCK, WINDOW), lambda i: (2, i, 0, 0))
 
 
-def next_degree(band, terms, far, at, so_far, after):
+def next_degree(band, terms, far, after):
     nodes, width = far.shape
-    states = terms.shape[1]
     rows = PER_STEP * BLOCK
     options, band_spec = across_specs(nodes, width)
-    part = pl.BlockSpec((rows, width), lambda i: (i, at))
-    turned = pl.BlockSpec((width, rows), lambda i: (at, i))
-    turned_shape = jax.ShapeDtypeStruct((states, nodes), jnp.bfloat16)
+    part = pl.BlockSpec((rows, width), lambda i: (i, 0))
     return call(
         functools.partial(across_kernel, True, 1),
         after,
-        into=[(out, so_far[out - 1]) for out in (1, 2, 3) if at],
         in_specs=[band_spec, part, pl.BlockSpec((nodes, width), lambda i: (0, 0))],
-        out_specs=[pl.BlockSpec((rows, width), lambda i: (i, 0)), part, turned, turned],
-        out_shape=[
-            jax.ShapeDtypeStruct((nodes, width), jnp.float32),
-            jax.ShapeDtypeStruct((nodes, states), jnp.float32),
-            turned_shape,
-            turned_shape,
-        ],
+        out_specs=part,
+        out_shape=jax.ShapeDtypeStruct((nodes, width), jnp.float32),
         **options,
     )(band, terms, far)
 
@@ -687,19 +695,16 @@
     current_paired = paired(current)
     band, last = prepare(stiff, odd, own, before, at_grid, face_map, y_prev, (current,))
 
-    terms = on_chip(band, current, current_paired, last)
-    following, so_far, waited = [], [None] * 3, ()
+    following = []
     for at, piece in enumerate(far):
-        chunk, *so_far = next_degree(band, terms, piece, at, so_far, waited)
-        following.append(chunk)
-        waited = (chunk,)
-    whole, *y_turned = so_far
+        terms = on_chip(band, current, current_paired, last, at * half, half, following)
+        following.append(next_degree(band, terms, piece, ()))
     next_far = [crossed(following[0])]
 
     if not swaps:
-        y_next, again, other = from_grid(face_map, whole)
+        y_next, whole, other, *y_turned = from_grid(face_map, following)
         next_far.append(crossed(other))
-        h_turned = applied_next(band, on_chip(band, whole, paired(again), None), next_far)
+        h_turned = applied_next(band, on_chip(band, whole, paired(whole), None), next_far)
         piece = lax.all_gather(whole, "band", axis=1, tiled=True)
         (block,) = both_products(y_turned, h_turned, [piece])
         parts = [
@@ -721,15 +726,15 @@
     first = [exchange(x, "band", ends) for x in following]
     second_middle = [exchange(x, "band", middle) for x in following]
     waited = (first[0], next_far[0])
-    y_next, again, other, second_middle[0] = from_grid(face_map, whole, waited, second_middle[:1])
+    y_next, whole, other, *y_turned, second_middle[0] = from_grid(face_map, following, waited, second_middle[:1])
     next_far.append(crossed(other))
     second_out = [lax.ppermute(second_middle[0], "band", outward)]
-    whole_paired = paired(again)
+    whole_paired = paired(whole)
     (first[0],) = gate(first[:1], (mark((y_next,)), whole_paired, second_middle[1]))
     third_middle = [exchange(first[0], "band", middle)]
     *near, second_middle[1] = sorted_products(keep, y_turned, following, first, 0, (), (), second_middle[1:])
     second_out.append(lax.ppermute(second_middle[1], "band", outward))
-    h_turned = applied_next(band, on_chip(band, whole, whole_paired, None, near[:1]), next_far)
+    h_turned = applied_next(band, on_chip(band, whole, whole_paired, None, after=near[:1]), next_far)
     (first[1],) = gate(first[1:], (h_turned[0], third_middle[0]))
     third_middle.append(exchange(first[1], "band", middle))
     kept, sent, third_middle[0] = sorted_products(keep, h_turned, following, first, 1, near, (), third_middle[:1])

time: 216 us -> 215 us (level)
  Pallas kernels: 105 us -> 111 us
  waiting for transfers between devices: 49.9 us -> 44.2 us
    pallas_call x28 -> x29, Pallas kernels: 105 us -> 111 us  [call(): return lambda *args: made(*args, *extra)]
    ppermute x14, waiting for transfers between devices: 35.5 us -> 29.8 us  [exchange(): return lax.ppermute(block, axis, pairs + [(b, a) for a, b in pairs])]
    unnamed x38 -> x42, local copies, waits for them, and re-layouts: 5.89 us -> 4.51 us
  transfers between devices with their start and end apart: 28 -> 28, of which waited for: 10 -> 9; matrix products, arithmetic and copies ran while one was open for 1% -> 1% of each run, Pallas kernels for 48% -> 51%
where the time goes in v3:
time: 215 us; the launch traced here: 214 us
  Pallas kernels  111 us (52%)
  starting transfers between devices  47.7 us (22%)
  waiting for transfers between devices  44.2 us (21%)
  local copies, waits for them, and re-layouts  6.8 us (3%)
  other arithmetic  3.2 us (1%)
    pallas_call x29, Pallas kernels, call(): return lambda *args: made(*args, *extra)  111 us
    ppermute x14, waiting for transfers between devices, exchange(): return lax.ppermute(block, axis, pairs + [(b, a) for a, b in pairs])  29.8 us
    ppermute x14, starting transfers between devices, exchange(): return lax.ppermute(block, axis, pairs + [(b, a) for a, b in pairs])  19.2 us
    ppermute x6, waiting for transfers between devices, to_owner(): return lax.ppermute(block, ('dom', 'band'), route)  11.5 us
    ppermute x6, starting transfers between devices, to_owner(): return lax.ppermute(block, ('dom', 'band'), route)  10.1 us
    unnamed x42, local copies, waits for them, and re-layouts  4.51 us
    ppermute x1, starting transfers between devices, on_device(): second_out = [lax.ppermute(second_middle[0], 'band', outward)]  4.44 us
  transfers between devices with their start and end apart: 28, of which 9 were waited for; matrix products, arithmetic and copies ran while one was open for 1% of the time, Pallas kernels for 51%

profile of v3, /device:TPU:18, one launch (start us, length us, event | category | flops | bytes accessed | tf_op | source)
XLA Modules:
  0.0 214.0 jit_solution(15649425990720084445)
XLA Ops:
  3.2 4.2 %to_grid.2 = (f32[1024,256]{1,0:T(8,128)}, f32[1024,512]{1,0:T(8,128)}) custom-call(s32[8,128]{1,0:T(8,128)} %bitcast.12, f32[1024,512]{1,0:T(8,128)} %refs_1_.3), custom_call_target="tpu_custom_call" | custom-call | flops 999999995904 | bytes 1 | tf_op jit(solution)/shard_map/to_grid/pallas_call | solution.py:81
  10.5 3.6 %to_grid.3 = (f32[1024,256]{1,0:T(8,128)}, f32[1024,512]{1,0:T(8,128)}) custom-call(s32[8,128]{1,0:T(8,128)S(1)} %bitcast.13, f32[1024,512]{1,0:T(8,128)S(1)} %copy-done.1, f32[1024,512]{1,0:T(8,128)} %get-tuple-element.32.refs_2_, f32[1024,256]{1,0:T(8,128)S(1)} %copy-done.3), custom_call_target="tpu_custom_call", output_to_operand_aliasing={{1}: (2, {})} | custom-call | flops 999999995904 | bytes 1 | tf_op jit(solution)/shard_map/to_grid/pallas_call | solution.py:81
  18.1 8.4 %prepare.1 = (bf16[3,8,256,256]{3,2,1,0:T(8,128)(2,1)S(1)}, f32[1024,512]{1,0:T(8,128)S(1)}) custom-call(s32[1]{0:T(128)} %bitcast.1.refs_0_, f32[1,1024]{1,0:T(1,128)} %bitcast.3.refs_1_, f32[1,1024]{1,0:T(1,128)} %bitcast.4.refs_2_, f32[1,1024]{1,0:T(1,128)S(1)} %bitcast.16, s32[8,128]{1,0:T(8,128)S(1)} %bitcast.14, f32[1024,512]{1,0:T(8,128)S(1)} %copy-done.2, ...), custom_call_target="tpu_custom_call" | custom-call | flops 999999995904 | bytes 1 | tf_op jit(solution)/shard_map/prepare/pallas_call | solution.py:81
  26.5 5.5 %on_chip.3.refs_1_ = f32[1024,256]{1,0:T(8,128)S(1)} custom-call(bf16[3,8,256,256]{3,2,1,0:T(8,128)(2,1)S(1)} %get-tuple-element.35.refs_0_, f32[1024,512]{1,0:T(8,128)} %get-tuple-element.34.refs_6_.refs_1_, f32[1024,512]{1,0:T(8,128)} %collective-permute-done.1.refs_2_, f32[1024,512]{1,0:T(8,128)S(1)} %get-tuple-element.36.refs_3_), custom_call_target="tpu_custom_call" | custom-call | flops 999999995904 | bytes 1 | tf_op jit(solution)/shard_map/on_chip/pallas_call | solution.py:81
  33.0 3.9 %across.3.refs_4_.refs_1_.refs_3_ = f32[1024,256]{1,0:T(8,128)} custom-call(bf16[3,8,256,256]{3,2,1,0:T(8,128)(2,1)S(1)} %get-tuple-element.35.refs_0_, f32[1024,256]{1,0:T(8,128)S(1)} %on_chip.3.refs_1_, f32[1024,256]{1,0:T(8,128)} %collective-permute-done.2.refs_2_), custom_call_target="tpu_custom_call" | custom-call | flops 999999995904 | bytes 1 | tf_op jit(solution)/shard_map/across/pallas_call | solution.py:81
  42.3 3.9 %on_chip.4.refs_1_ = f32[1024,256]{1,0:T(8,128)S(1)} custom-call(bf16[3,8,256,256]{3,2,1,0:T(8,128)(2,1)S(1)} %get-tuple-element.35.refs_0_, f32[1024,512]{1,0:T(8,128)} %get-tuple-element.34.refs_6_.refs_1_, f32[1024,512]{1,0:T(8,128)} %collective-permute-done.1.refs_2_, f32[1024,512]{1,0:T(8,128)S(1)} %copy-done.8, f32[1024,256]{1,0:T(8,128)} %across.3.refs_4_.refs_1_.refs_3_), custom_call_target="tpu_custom_call" | custom-call | flops 999999995904 | bytes 1 | tf_op jit(solution)/shard_map/on_chip/pallas_call | solution.py:81
  46.2 9.3 %collective-permute-done.3.refs_2_ = f32[1024,256]{1,0:T(8,128)} collective-permute-done((f32[1024,256]{1,0:T(8,128)}, f32[1024,256]{1,0:T(8,128)}, u32[]{:S(2)}, u32[]{:S(2)}) %collective-permute-start.3) | collective-permute-done | bytes 1048608 | tf_op jit(solution)/shard_map/ppermute | solution.py:654
  55.5 3.7 %across.4.refs_2_.refs_4_ = f32[1024,256]{1,0:T(8,128)} custom-call(bf16[3,8,256,256]{3,2,1,0:T(8,128)(2,1)S(1)} %get-tuple-element.35.refs_0_, f32[1024,256]{1,0:T(8,128)S(1)} %on_chip.4.refs_1_, f32[1024,256]{1,0:T(8,128)} %collective-permute-done.3.refs_2_), custom_call_target="tpu_custom_call" | custom-call | flops 999999995904 | bytes 1 | tf_op jit(solution)/shard_map/across/pallas_call | solution.py:81
  62.4 14.8 %collective-permute-done.5.refs_4_.refs_2_ = f32[1024,256]{1,0:T(8,128)} collective-permute-done((f32[1024,256]{1,0:T(8,128)}, f32[1024,256]{1,0:T(8,128)}, u32[]{:S(2)}, u32[]{:S(2)}) %collective-permute-start.5) | collective-permute-done | bytes 1048608 | tf_op jit(solution)/shard_map/ppermute | solution.py:654
  77.2 5.8 %from_grid.1 = (f32[1024,512]{1,0:T(8,128)}, f32[1024,512]{1,0:T(8,128)}, f32[1024,256]{1,0:T(8,128)}, bf16[512,1024]{1,0:T(8,128)(2,1)S(1)}, bf16[512,1024]{1,0:T(8,128)(2,1)S(1)}, /*index=5*/f32[1024,256]{1,0:T(8,128)}) custom-call(s32[1,1024]{1,0:T(1,128)S(1)} %bitcast.15, ...), custom_call_target="tpu_custom_call", output_to_operand_aliasing={{5}: (5, {})} | custom-call | flops 999999995904 | bytes 1 | tf_op jit(solution)/shard_map/from_grid/pallas_call | solution.py:81
  87.6 4.4 %collective-permute-start.13 = (f32[1024,256]{1,0:T(8,128)}, f32[1024,256]{1,0:T(8,128)}, u32[]{:S(2)}, u32[]{:S(2)}) collective-permute-start(f32[1024,256]{1,0:T(8,128)} %get-tuple-element.49.refs_4_), channel_id=1, source_target_pairs={{2,3},{1,0},{6,7},{5,4},{10,11},{9,8},{14,15},{13,12},{18,19},{17,... | collective-permute-start | bytes 3145736 | tf_op jit(solution)/shard_map/ppermute | solution.py:731
  95.3 7.5 %sorted_products.2 = (f32[1024,512]{1,0:T(8,128)S(1)}, f32[1024,512]{1,0:T(8,128)}, f32[1024,256]{1,0:T(8,128)}) custom-call(s32[1]{0:T(128)} %bitcast.10.refs_0_, bf16[512,1024]{1,0:T(8,128)(2,1)S(1)} %get-tuple-element.40.refs_1_.refs_0_, bf16[512,1024]{1,0:T(8,128)(2,1)S(1)} %get-tuple-element.41.refs_2_.refs_1_, ...), custom_call_target="tpu_custom_call", output_to_operand_aliasing={{2}: (7, {})} | custom-call | flops 999999995904 | bytes 1 | tf_op jit(solution)/shard_map/sorted_products/pallas_call | solution.py:81
  105.2 5.8 %on_chip.5.refs_1_ = f32[1024,512]{1,0:T(8,128)S(1)} custom-call(bf16[3,8,256,256]{3,2,1,0:T(8,128)(2,1)S(1)} %copy-done.6, f32[1024,512]{1,0:T(8,128)} %get-tuple-element.39.refs_1_, f32[1024,512]{1,0:T(8,128)} %collective-permute-done.7.refs_1_.refs_2_, f32[1024,512]{1,0:T(8,128)S(1)} %get-tuple-element.42.refs_3_.refs_7_), custom_call_target="tpu_custom_call" | custom-call | flops 999999995904 | bytes 1 | tf_op jit(solution)/shard_map/on_chip/pallas_call | solution.py:81
  111.0 4.4 %across.5 = (bf16[512,1024]{1,0:T(8,128)(2,1)S(1)}, bf16[512,1024]{1,0:T(8,128)(2,1)S(1)}) custom-call(bf16[3,8,256,256]{3,2,1,0:T(8,128)(2,1)S(1)} %copy-done.6, f32[1024,512]{1,0:T(8,128)S(1)} %on_chip.5.refs_1_, f32[1024,256]{1,0:T(8,128)} %collective-permute-done.5.refs_4_.refs_2_, f32[1024,256]{1,0:T(8,128)} %collective-permute-done.10.refs_3_), custom_call_target="tpu_custom_call" | custom-call | flops 999999995904 | bytes 1 | tf_op jit(solution)/shard_map/across/pallas_call | solution.py:81
  115.5 4.7 %collective-permute-done.11.refs_1_.refs_9_ = f32[1024,256]{1,0:T(8,128)} collective-permute-done((f32[1024,256]{1,0:T(8,128)}, f32[1024,256]{1,0:T(8,128)}, u32[]{:S(2)}, u32[]{:S(2)}) %collective-permute-start.11) | collective-permute-done | bytes 1048608 | tf_op jit(solution)/shard_map/ppermute | solution.py:654
  123.6 7.5 %sorted_products.3 = (f32[1024,512]{1,0:T(8,128)S(1)}, f32[1024,512]{1,0:T(8,128)}, f32[1024,256]{1,0:T(8,128)}) custom-call(s32[1]{0:T(128)} %bitcast.10.refs_0_, bf16[512,1024]{1,0:T(8,128)(2,1)S(1)} %get-tuple-element.44.refs_0_.refs_1_.refs_2_.refs_3_, ...), custom_call_target="tpu_custom_call", output_to_operand_aliasing={{0}: (7, {}), {1}: (8, {}), {2}: (9, {})} | custom-call | flops 999999995904 | bytes 1 | tf_op jit(solution)/shard_map/sorted_products/pallas_call | solution.py:81
  133.4 5.0 %both_products.4.refs_2_.refs_0_ = f32[1024,256]{1,0:T(8,128)} custom-call(bf16[512,1024]{1,0:T(8,128)(2,1)S(1)} %copy-done.13, bf16[512,1024]{1,0:T(8,128)(2,1)S(1)} %copy-done.17, bf16[512,1024]{1,0:T(8,128)(2,1)S(1)} %get-tuple-element.44.refs_0_.refs_1_.refs_2_.refs_3_, bf16[512,1024]{1,0:T(8,128)(2,1)S(1)} %get-tuple-element.45.refs_2_.refs_3_.refs_4_, ...), custom_call_target="tpu_custom_call" | custom-call | flops 999999995904 | bytes 1 | tf_op jit(solution)/shard_map/both_products/pallas_call | solution.py:81
  144.6 3.9 %collective-permute-start.14 = (f32[1024,512]{1,0:T(8,128)}, f32[1024,512]{1,0:T(8,128)}, u32[]{:S(2)}, u32[]{:S(2)}) collective-permute-start(f32[1024,512]{1,0:T(8,128)} %plus.5.refs_6_.refs_1_), channel_id=1, source_target_pairs={{8,0},{12,4},{9,1},{13,5},{2,10},{6,14},{3,11},{7,15},{24,16},{28,... | collective-permute-start | bytes 6291464 | tf_op jit(solution)/shard_map/ppermute | solution.py:722
  148.5 4.8 %both_products.5 = (f32[1024,256]{1,0:T(8,128)S(1)}, f32[1024,256]{1,0:T(8,128)}) custom-call(bf16[512,1024]{1,0:T(8,128)(2,1)S(1)} %copy-done.14, bf16[512,1024]{1,0:T(8,128)(2,1)S(1)} %copy-done.18, bf16[512,1024]{1,0:T(8,128)(2,1)S(1)} %get-tuple-element.44.refs_0_.refs_1_.refs_2_.refs_3_, ...), custom_call_target="tpu_custom_call", output_to_operand_aliasing={{1}: (7, {})} | custom-call | flops 999999995904 | bytes 1 | tf_op jit(solution)/shard_map/both_products/pallas_call | solution.py:81
  161.9 5.0 %pair_products.1 = (f32[1024,256]{1,0:T(8,128)S(1)}, f32[1024,256]{1,0:T(8,128)}) custom-call(s32[1]{0:T(128)} %bitcast.11.refs_0_, bf16[512,1024]{1,0:T(8,128)(2,1)S(1)} %copy-done.15, bf16[512,1024]{1,0:T(8,128)(2,1)S(1)} %copy-done.19, bf16[512,1024]{1,0:T(8,128)(2,1)S(1)} %get-tuple-element.44.refs_0_.refs_1_.refs_2_.refs_3_, ...), custom_call_target="tpu_custom_call" | custom-call | flops 999999995904 | bytes 1 | tf_op jit(solution)/shard_map/pair_products/pallas_call | solution.py:81
  173.6 4.4 %both_products.6.refs_6_.refs_0_ = f32[1024,128]{1,0:T(8,128)} custom-call(bf16[512,1024]{1,0:T(8,128)(2,1)S(1)} %copy-done.15, bf16[512,1024]{1,0:T(8,128)(2,1)S(1)} %copy-done.19, bf16[512,1024]{1,0:T(8,128)(2,1)S(1)} %get-tuple-element.44.refs_0_.refs_1_.refs_2_.refs_3_, bf16[512,1024]{1,0:T(8,128)(2,1)S(1)} %copy-done.11, ...), custom_call_target="tpu_custom_call" | custom-call | flops 999999995904 | bytes 1 | tf_op jit(solution)/shard_map/both_products/pallas_call | solution.py:81
  179.7 4.3 %both_products.7.refs_2_.refs_0_ = f32[1024,128]{1,0:T(8,128)} custom-call(bf16[512,1024]{1,0:T(8,128)(2,1)S(1)} %copy-done.15, bf16[512,1024]{1,0:T(8,128)(2,1)S(1)} %copy-done.19, bf16[512,1024]{1,0:T(8,128)(2,1)S(1)} %get-tuple-element.44.refs_0_.refs_1_.refs_2_.refs_3_, bf16[512,1024]{1,0:T(8,128)(2,1)S(1)} %copy-done.11, ...), custom_call_target="tpu_custom_call" | custom-call | flops 999999995904 | bytes 1 | tf_op jit(solution)/shard_map/both_products/pallas_call | solution.py:81
  202.1 4.1 %collective-permute-done.26.refs_2_.refs_4_ = f32[1024,128]{1,0:T(8,128)} collective-permute-done((f32[1024,128]{1,0:T(8,128)}, f32[1024,128]{1,0:T(8,128)}, u32[]{:S(2)}, u32[]{:S(2)}) %collective-permute-start.26) | collective-permute-done | bytes 524320 | tf_op jit(solution)/shard_map/ppermute | solution.py:672
  206.2 5.6 %collective-permute-done.27.refs_3_.refs_5_ = f32[1024,128]{1,0:T(8,128)} collective-permute-done((f32[1024,128]{1,0:T(8,128)}, f32[1024,128]{1,0:T(8,128)}, u32[]{:S(2)}, u32[]{:S(2)}) %collective-permute-start.27) | collective-permute-done | bytes 524320 | tf_op jit(solution)/shard_map/ppermute | solution.py:672
  (108 shorter events, 78.5 us)
Async XLA Ops:
  3.2 13.2 %collective-permute-start = (f32[1024]{0:T(1024)}, f32[1024]{0:T(1024)}, u32[]{:S(2)}, u32[]{:S(2)}) collective-permute-start(f32[1024]{0:T(1024)} %select_reduce_fusion.1), channel_id=1, source_target_pairs={{0,4},{4,8},{8,12},{12,0},{1,5},{5,9},{9,13},{13,1},{2,6},{6,10},{... | collective-permute-start | bytes 12296 | tf_op jit(solution)/shard_map/ppermute | solution.py:685
  7.4 25.6 %collective-permute-start.2 = (f32[1024,256]{1,0:T(8,128)}, f32[1024,256]{1,0:T(8,128)}, u32[]{:S(2)}, u32[]{:S(2)}) collective-permute-start(f32[1024,256]{1,0:T(8,128)} %get-tuple-element.33.refs_3_), channel_id=1, source_target_pairs={{4,8},{12,0},{8,4},{0,12},{5,9},{13,1},{9,5},{1,13},{6,10},{14,2},... | collective-permute-start | bytes 3145736 | tf_op jit(solution)/shard_map/ppermute | solution.py:654
  14.1 12.4 %collective-permute-start.1 = (f32[1024,512]{1,0:T(8,128)}, f32[1024,512]{1,0:T(8,128)}, u32[]{:S(2)}, u32[]{:S(2)}) collective-permute-start(f32[1024,512]{1,0:T(8,128)} %get-tuple-element.34.refs_6_.refs_1_), channel_id=1, source_target_pairs={{0,4},{8,12},{4,0},{12,8},{1,5},{9,13},{5,1},{13,9},{2,6},{10,14},... | collective-permute-start | bytes 6291464 | tf_op jit(solution)/shard_map/ppermute | solution.py:654
  14.2 41.3 %collective-permute-start.3 = (f32[1024,256]{1,0:T(8,128)}, f32[1024,256]{1,0:T(8,128)}, u32[]{:S(2)}, u32[]{:S(2)}) collective-permute-start(f32[1024,256]{1,0:T(8,128)} %get-tuple-element.37), channel_id=1, source_target_pairs={{4,8},{12,0},{8,4},{0,12},{5,9},{13,1},{9,5},{1,13},{6,10},{14,2},... | collective-permute-start | bytes 3145736 | tf_op jit(solution)/shard_map/ppermute | solution.py:654
  36.9 25.5 %collective-permute-start.4 = (f32[1024,256]{1,0:T(8,128)}, f32[1024,256]{1,0:T(8,128)}, u32[]{:S(2)}, u32[]{:S(2)}) collective-permute-start(f32[1024,256]{1,0:T(8,128)} %across.3.refs_4_.refs_1_.refs_3_), channel_id=1, source_target_pairs={{0,1},{2,3},{1,0},{3,2},{4,5},{6,7},{5,4},{7,6},{8,9},{10,11},{9,8... | collective-permute-start | bytes 3145736 | tf_op jit(solution)/shard_map/ppermute | solution.py:654
  38.5 38.7 %collective-permute-start.5 = (f32[1024,256]{1,0:T(8,128)}, f32[1024,256]{1,0:T(8,128)}, u32[]{:S(2)}, u32[]{:S(2)}) collective-permute-start(f32[1024,256]{1,0:T(8,128)} %across.3.refs_4_.refs_1_.refs_3_), channel_id=1, source_target_pairs={{4,8},{12,0},{8,4},{0,12},{5,9},{13,1},{9,5},{1,13},{6,10},{14,2},... | collective-permute-start | bytes 3145736 | tf_op jit(solution)/shard_map/ppermute | solution.py:654
  40.4 36.8 %collective-permute-start.6 = (f32[1024,256]{1,0:T(8,128)}, f32[1024,256]{1,0:T(8,128)}, u32[]{:S(2)}, u32[]{:S(2)}) collective-permute-start(f32[1024,256]{1,0:T(8,128)} %across.3.refs_4_.refs_1_.refs_3_), channel_id=1, source_target_pairs={{1,2},{2,1},{5,6},{6,5},{9,10},{10,9},{13,14},{14,13},{17,18},{18,... | collective-permute-start | bytes 3145736 | tf_op jit(solution)/shard_map/ppermute | solution.py:654
  59.2 32.8 %collective-permute-start.8 = (f32[1024,256]{1,0:T(8,128)}, f32[1024,256]{1,0:T(8,128)}, u32[]{:S(2)}, u32[]{:S(2)}) collective-permute-start(f32[1024,256]{1,0:T(8,128)} %across.4.refs_2_.refs_4_), channel_id=1, source_target_pairs={{1,2},{2,1},{5,6},{6,5},{9,10},{10,9},{13,14},{14,13},{17,18},{18,... | collective-permute-start | bytes 3145736 | tf_op jit(solution)/shard_map/ppermute | solution.py:654
  61.6 33.7 %collective-permute-start.9 = (f32[1024,256]{1,0:T(8,128)}, f32[1024,256]{1,0:T(8,128)}, u32[]{:S(2)}, u32[]{:S(2)}) collective-permute-start(f32[1024,256]{1,0:T(8,128)} %across.4.refs_2_.refs_4_), channel_id=1, source_target_pairs={{0,1},{2,3},{1,0},{3,2},{4,5},{6,7},{5,4},{7,6},{8,9},{10,11},{9,8... | collective-permute-start | bytes 3145736 | tf_op jit(solution)/shard_map/ppermute | solution.py:654
  85.8 25.2 %collective-permute-start.10 = (f32[1024,256]{1,0:T(8,128)}, f32[1024,256]{1,0:T(8,128)}, u32[]{:S(2)}, u32[]{:S(2)}) collective-permute-start(f32[1024,256]{1,0:T(8,128)} %get-tuple-element.43), channel_id=1, source_target_pairs={{4,8},{12,0},{8,4},{0,12},{5,9},{13,1},{9,5},{1,13},{6,10},{14,2},... | collective-permute-start | bytes 3145736 | tf_op jit(solution)/shard_map/ppermute | solution.py:654
  87.6 45.8 %collective-permute-start.13 = (f32[1024,256]{1,0:T(8,128)}, f32[1024,256]{1,0:T(8,128)}, u32[]{:S(2)}, u32[]{:S(2)}) collective-permute-start(f32[1024,256]{1,0:T(8,128)} %get-tuple-element.49.refs_4_), channel_id=1, source_target_pairs={{2,3},{1,0},{6,7},{5,4},{10,11},{9,8},{14,15},{13,12},{18,19},{17,... | collective-permute-start | bytes 3145736 | tf_op jit(solution)/shard_map/ppermute | solution.py:731
  93.4 26.8 %collective-permute-start.11 = (f32[1024,256]{1,0:T(8,128)}, f32[1024,256]{1,0:T(8,128)}, u32[]{:S(2)}, u32[]{:S(2)}) collective-permute-start(f32[1024,256]{1,0:T(8,128)} %gate.3.refs_5_), channel_id=1, source_target_pairs={{1,2},{2,1},{5,6},{6,5},{9,10},{10,9},{13,14},{14,13},{17,18},{18,... | collective-permute-start | bytes 3145736 | tf_op jit(solution)/shard_map/ppermute | solution.py:654
  102.8 45.6 %collective-permute-start.15 = (f32[1024,256]{1,0:T(8,128)}, f32[1024,256]{1,0:T(8,128)}, u32[]{:S(2)}, u32[]{:S(2)}) collective-permute-start(f32[1024,256]{1,0:T(8,128)} %get-tuple-element.50.refs_4_), channel_id=1, source_target_pairs={{2,3},{1,0},{6,7},{5,4},{10,11},{9,8},{14,15},{13,12},{18,19},{17,... | collective-permute-start | bytes 3145736 | tf_op jit(solution)/shard_map/ppermute | solution.py:736
  121.4 27.0 %collective-permute-start.16 = (f32[1024,256]{1,0:T(8,128)}, f32[1024,256]{1,0:T(8,128)}, u32[]{:S(2)}, u32[]{:S(2)}) collective-permute-start(f32[1024,256]{1,0:T(8,128)} %gate.4.refs_6_), channel_id=1, source_target_pairs={{1,2},{2,1},{5,6},{6,5},{9,10},{10,9},{13,14},{14,13},{17,18},{18,... | collective-permute-start | bytes 3145736 | tf_op jit(solution)/shard_map/ppermute | solution.py:654
  131.2 10.6 %collective-permute-start.12 = (f32[1024,512]{1,0:T(8,128)}, f32[1024,512]{1,0:T(8,128)}, u32[]{:S(2)}, u32[]{:S(2)}) collective-permute-start(f32[1024,512]{1,0:T(8,128)} %get-tuple-element.48), channel_id=1, source_target_pairs={{0,4},{8,12},{4,0},{12,8},{1,5},{9,13},{5,1},{13,9},{2,6},{10,14},... | collective-permute-start | bytes 6291464 | tf_op jit(solution)/shard_map/ppermute | solution.py:654
  131.2 30.7 %collective-permute-start.17 = (f32[1024,256]{1,0:T(8,128)}, f32[1024,256]{1,0:T(8,128)}, u32[]{:S(2)}, u32[]{:S(2)}) collective-permute-start(f32[1024,256]{1,0:T(8,128)} %get-tuple-element.52.refs_6_), channel_id=1, source_target_pairs={{2,3},{1,0},{6,7},{5,4},{10,11},{9,8},{14,15},{13,12},{18,19},{17,... | collective-permute-start | bytes 3145736 | tf_op jit(solution)/shard_map/ppermute | solution.py:741
  138.4 14.9 %collective-permute-start.18 = (f32[1024,256]{1,0:T(8,128)}, f32[1024,256]{1,0:T(8,128)}, u32[]{:S(2)}, u32[]{:S(2)}) collective-permute-start(f32[1024,256]{1,0:T(8,128)} %both_products.4.refs_2_.refs_0_), channel_id=1, source_target_pairs={{12,8},{4,0},{13,9},{5,1},{2,6},{10,14},{3,7},{11,15},{28,24},{20,... | collective-permute-start | bytes 3145736 | tf_op jit(solution)/shard_map/ppermute | solution.py:672
  144.6 49.0 %collective-permute-start.14 = (f32[1024,512]{1,0:T(8,128)}, f32[1024,512]{1,0:T(8,128)}, u32[]{:S(2)}, u32[]{:S(2)}) collective-permute-start(f32[1024,512]{1,0:T(8,128)} %plus.5.refs_6_.refs_1_), channel_id=1, source_target_pairs={{8,0},{12,4},{9,1},{13,5},{2,10},{6,14},{3,11},{7,15},{24,16},{28,... | collective-permute-start | bytes 6291464 | tf_op jit(solution)/shard_map/ppermute | solution.py:722
  155.8 11.1 %collective-permute-start.19 = (f32[1024,256]{1,0:T(8,128)}, f32[1024,256]{1,0:T(8,128)}, u32[]{:S(2)}, u32[]{:S(2)}) collective-permute-start(f32[1024,256]{1,0:T(8,128)} %plus.6.refs_8_.refs_2_), channel_id=1, source_target_pairs={{0,8},{1,9},{14,6},{15,7},{16,24},{17,25},{30,22},{31,23}} | collective-permute-start | bytes 3145736 | tf_op jit(solution)/shard_map/ppermute | solution.py:672
  159.7 13.9 %collective-permute-start.21 = (f32[1024,128]{1,0:T(8,128)}, f32[1024,128]{1,0:T(8,128)}, u32[]{:S(2)}, u32[]{:S(2)}) collective-permute-start(f32[1024,128]{1,0:T(8,128)} %get-tuple-element.61.refs_4_), channel_id=1, source_target_pairs={{2,3},{1,0},{6,7},{5,4},{10,11},{9,8},{14,15},{13,12},{18,19},{17,... | collective-permute-start | bytes 1572872 | tf_op jit(solution)/shard_map/ppermute | solution.py:754
  168.1 11.6 %collective-permute-start.20 = (f32[1024,128]{1,0:T(8,128)}, f32[1024,128]{1,0:T(8,128)}, u32[]{:S(2)}, u32[]{:S(2)}) collective-permute-start(f32[1024,128]{1,0:T(8,128)} %gate.5.refs_2_.refs_4_), channel_id=1, source_target_pairs={{2,3},{1,0},{6,7},{5,4},{10,11},{9,8},{14,15},{13,12},{18,19},{17,... | collective-permute-start | bytes 1572872 | tf_op jit(solution)/shard_map/ppermute | solution.py:760
  172.3 26.2 %collective-permute-start.25 = (f32[1024,256]{1,0:T(8,128)}, f32[1024,256]{1,0:T(8,128)}, u32[]{:S(2)}, u32[]{:S(2)}) collective-permute-start(f32[1024,256]{1,0:T(8,128)} %plus.7.refs_6_.refs_4_), channel_id=1, source_target_pairs={{0,8},{4,12},{1,9},{5,13},{10,2},{14,6},{11,3},{15,7},{16,24},{20,... | collective-permute-start | bytes 3145736 | tf_op jit(solution)/shard_map/ppermute | solution.py:765
  187.3 18.9 %collective-permute-start.26 = (f32[1024,128]{1,0:T(8,128)}, f32[1024,128]{1,0:T(8,128)}, u32[]{:S(2)}, u32[]{:S(2)}) collective-permute-start(f32[1024,128]{1,0:T(8,128)} %plus.8.refs_2_.refs_6_), channel_id=1, source_target_pairs={{4,12},{5,13},{10,2},{11,3},{20,28},{21,29},{26,18},{27,19}} | collective-permute-start | bytes 1572872 | tf_op jit(solution)/shard_map/ppermute | solution.py:672
  192.3 19.5 %collective-permute-start.27 = (f32[1024,128]{1,0:T(8,128)}, f32[1024,128]{1,0:T(8,128)}, u32[]{:S(2)}, u32[]{:S(2)}) collective-permute-start(f32[1024,128]{1,0:T(8,128)} %plus.9.refs_3_.refs_7_), channel_id=1, source_target_pairs={{4,12},{5,13},{10,2},{11,3},{20,28},{21,29},{26,18},{27,19}} | collective-permute-start | bytes 1572872 | tf_op jit(solution)/shard_map/ppermute | solution.py:672
  (25 other events, 209.5 us)

commit v4 on v3

--- a/solution.py
+++ b/solution.py
@@ -461,7 +461,7 @@
 
 def sorted_products(keep, turned, own, first, at, so_far, after=(), passed=()):
     states, nodes = turned[0].shape
-    rows = 256
+    rows = 512 if turned[0].shape[0] % 512 == 0 else 256
     steps = states // rows
     width = sum(piece.shape[1] for piece in own)
     left = pl.BlockSpec((rows, nodes), lambda i: (i, 0))
@@ -502,7 +502,7 @@
 
 def both_products(y_turned, h_turned, pieces, summed=1, after=(), passed=()):
     states, nodes = y_turned[0].shape
-    rows = 256
+    rows = 512 if y_turned[0].shape[0] % 512 == 0 else 256
     steps = states // rows
     width = sum(piece.shape[1] for piece in pieces) // summed
     first = pl.BlockSpec((rows, nodes), lambda i: (jnp.minimum(i, steps - 1), 0))
@@ -545,7 +545,7 @@
 
 def pair_products(keep, y_turned, h_turned, block, piece, other, after):
     states, nodes = y_turned[0].shape
-    rows = 256
+    rows = 512 if y_turned[0].shape[0] % 512 == 0 else 256
     steps = states // rows
     width = piece.shape[1]
     first = pl.BlockSpec((rows, nodes), lambda i: (jnp.minimum(i, steps - 1), 0))

time: 215 us -> 215 us (level)
  transfers between devices with their start and end apart: 28 -> 28, of which waited for: 9 -> 9; matrix products, arithmetic and copies ran while one was open for 1% -> 1% of each run, Pallas kernels for 51% -> 50%
where the time goes in v4:
time: 215 us; the launch traced here: 214 us
  Pallas kernels  109 us (51%)
  starting transfers between devices  48.8 us (23%)
  waiting for transfers between devices  44.7 us (21%)
  local copies, waits for them, and re-layouts  6.8 us (3%)
  other arithmetic  3.2 us (1%)
    pallas_call x29, Pallas kernels, call(): return lambda *args: made(*args, *extra)  109 us
    ppermute x14, waiting for transfers between devices, exchange(): return lax.ppermute(block, axis, pairs + [(b, a) for a, b in pairs])  29.9 us
    ppermute x14, starting transfers between devices, exchange(): return lax.ppermute(block, axis, pairs + [(b, a) for a, b in pairs])  19.2 us
    ppermute x6, starting transfers between devices, to_owner(): return lax.ppermute(block, ('dom', 'band'), route)  10.1 us
    ppermute x6, waiting for transfers between devices, to_owner(): return lax.ppermute(block, ('dom', 'band'), route)  10 us
    unnamed x42, local copies, waits for them, and re-layouts  4.51 us
    ppermute x1, starting transfers between devices, on_device(): second_out = [lax.ppermute(second_middle[0], 'band', outward)]  4.44 us
  transfers between devices with their start and end apart: 28, of which 9 were waited for; matrix products, arithmetic and copies ran while one was open for 1% of the time, Pallas kernels for 50%

profile of v4, /device:TPU:18, one launch (start us, length us, event | category | flops | bytes accessed | tf_op | source)
XLA Modules:
  0.0 213.5 jit_solution(8767375217904238177)
XLA Ops:
  3.2 4.2 %to_grid.2 = (f32[1024,256]{1,0:T(8,128)}, f32[1024,512]{1,0:T(8,128)}) custom-call(s32[8,128]{1,0:T(8,128)} %bitcast.12, f32[1024,512]{1,0:T(8,128)} %refs_1_.3), custom_call_target="tpu_custom_call" | custom-call | flops 999999995904 | bytes 1 | tf_op jit(solution)/shard_map/to_grid/pallas_call | solution.py:81
  10.5 3.6 %to_grid.3 = (f32[1024,256]{1,0:T(8,128)}, f32[1024,512]{1,0:T(8,128)}) custom-call(s32[8,128]{1,0:T(8,128)S(1)} %bitcast.13, f32[1024,512]{1,0:T(8,128)S(1)} %copy-done.1, f32[1024,512]{1,0:T(8,128)} %get-tuple-element.32.refs_2_, f32[1024,256]{1,0:T(8,128)S(1)} %copy-done.3), custom_call_target="tpu_custom_call", output_to_operand_aliasing={{1}: (2, {})} | custom-call | flops 999999995904 | bytes 1 | tf_op jit(solution)/shard_map/to_grid/pallas_call | solution.py:81
  18.1 8.4 %prepare.1 = (bf16[3,8,256,256]{3,2,1,0:T(8,128)(2,1)S(1)}, f32[1024,512]{1,0:T(8,128)S(1)}) custom-call(s32[1]{0:T(128)} %bitcast.1.refs_0_, f32[1,1024]{1,0:T(1,128)} %bitcast.3.refs_1_, f32[1,1024]{1,0:T(1,128)} %bitcast.4.refs_2_, f32[1,1024]{1,0:T(1,128)S(1)} %bitcast.16, s32[8,128]{1,0:T(8,128)S(1)} %bitcast.14, f32[1024,512]{1,0:T(8,128)S(1)} %copy-done.2, ...), custom_call_target="tpu_custom_call" | custom-call | flops 999999995904 | bytes 1 | tf_op jit(solution)/shard_map/prepare/pallas_call | solution.py:81
  26.5 5.5 %on_chip.3.refs_1_ = f32[1024,256]{1,0:T(8,128)S(1)} custom-call(bf16[3,8,256,256]{3,2,1,0:T(8,128)(2,1)S(1)} %get-tuple-element.35.refs_0_, f32[1024,512]{1,0:T(8,128)} %get-tuple-element.34.refs_6_.refs_1_, f32[1024,512]{1,0:T(8,128)} %collective-permute-done.1.refs_2_, f32[1024,512]{1,0:T(8,128)S(1)} %get-tuple-element.36.refs_3_), custom_call_target="tpu_custom_call" | custom-call | flops 999999995904 | bytes 1 | tf_op jit(solution)/shard_map/on_chip/pallas_call | solution.py:81
  33.0 3.9 %across.3.refs_4_.refs_1_.refs_3_ = f32[1024,256]{1,0:T(8,128)} custom-call(bf16[3,8,256,256]{3,2,1,0:T(8,128)(2,1)S(1)} %get-tuple-element.35.refs_0_, f32[1024,256]{1,0:T(8,128)S(1)} %on_chip.3.refs_1_, f32[1024,256]{1,0:T(8,128)} %collective-permute-done.2.refs_2_), custom_call_target="tpu_custom_call" | custom-call | flops 999999995904 | bytes 1 | tf_op jit(solution)/shard_map/across/pallas_call | solution.py:81
  42.3 3.9 %on_chip.4.refs_1_ = f32[1024,256]{1,0:T(8,128)S(1)} custom-call(bf16[3,8,256,256]{3,2,1,0:T(8,128)(2,1)S(1)} %get-tuple-element.35.refs_0_, f32[1024,512]{1,0:T(8,128)} %get-tuple-element.34.refs_6_.refs_1_, f32[1024,512]{1,0:T(8,128)} %collective-permute-done.1.refs_2_, f32[1024,512]{1,0:T(8,128)S(1)} %copy-done.8, f32[1024,256]{1,0:T(8,128)} %across.3.refs_4_.refs_1_.refs_3_), custom_call_target="tpu_custom_call" | custom-call | flops 999999995904 | bytes 1 | tf_op jit(solution)/shard_map/on_chip/pallas_call | solution.py:81
  46.2 9.3 %collective-permute-done.3.refs_2_ = f32[1024,256]{1,0:T(8,128)} collective-permute-done((f32[1024,256]{1,0:T(8,128)}, f32[1024,256]{1,0:T(8,128)}, u32[]{:S(2)}, u32[]{:S(2)}) %collective-permute-start.3) | collective-permute-done | bytes 1048608 | tf_op jit(solution)/shard_map/ppermute | solution.py:654
  55.5 3.7 %across.4.refs_2_.refs_4_ = f32[1024,256]{1,0:T(8,128)} custom-call(bf16[3,8,256,256]{3,2,1,0:T(8,128)(2,1)S(1)} %get-tuple-element.35.refs_0_, f32[1024,256]{1,0:T(8,128)S(1)} %on_chip.4.refs_1_, f32[1024,256]{1,0:T(8,128)} %collective-permute-done.3.refs_2_), custom_call_target="tpu_custom_call" | custom-call | flops 999999995904 | bytes 1 | tf_op jit(solution)/shard_map/across/pallas_call | solution.py:81
  62.4 14.8 %collective-permute-done.5.refs_4_.refs_2_ = f32[1024,256]{1,0:T(8,128)} collective-permute-done((f32[1024,256]{1,0:T(8,128)}, f32[1024,256]{1,0:T(8,128)}, u32[]{:S(2)}, u32[]{:S(2)}) %collective-permute-start.5) | collective-permute-done | bytes 1048608 | tf_op jit(solution)/shard_map/ppermute | solution.py:654
  77.2 5.8 %from_grid.1 = (f32[1024,512]{1,0:T(8,128)}, f32[1024,512]{1,0:T(8,128)}, f32[1024,256]{1,0:T(8,128)}, bf16[512,1024]{1,0:T(8,128)(2,1)S(1)}, bf16[512,1024]{1,0:T(8,128)(2,1)S(1)}, /*index=5*/f32[1024,256]{1,0:T(8,128)}) custom-call(s32[1,1024]{1,0:T(1,128)S(1)} %bitcast.15, ...), custom_call_target="tpu_custom_call", output_to_operand_aliasing={{5}: (5, {})} | custom-call | flops 999999995904 | bytes 1 | tf_op jit(solution)/shard_map/from_grid/pallas_call | solution.py:81
  87.6 4.4 %collective-permute-start.13 = (f32[1024,256]{1,0:T(8,128)}, f32[1024,256]{1,0:T(8,128)}, u32[]{:S(2)}, u32[]{:S(2)}) collective-permute-start(f32[1024,256]{1,0:T(8,128)} %get-tuple-element.49.refs_4_), channel_id=1, source_target_pairs={{2,3},{1,0},{6,7},{5,4},{10,11},{9,8},{14,15},{13,12},{18,19},{17,... | collective-permute-start | bytes 3145736 | tf_op jit(solution)/shard_map/ppermute | solution.py:731
  95.3 7.5 %sorted_products.2 = (f32[1024,512]{1,0:T(8,128)S(1)}, f32[1024,512]{1,0:T(8,128)}, f32[1024,256]{1,0:T(8,128)}) custom-call(s32[1]{0:T(128)} %bitcast.10.refs_0_, bf16[512,1024]{1,0:T(8,128)(2,1)S(1)} %get-tuple-element.40.refs_1_.refs_0_, bf16[512,1024]{1,0:T(8,128)(2,1)S(1)} %get-tuple-element.41.refs_2_.refs_1_, ...), custom_call_target="tpu_custom_call", output_to_operand_aliasing={{2}: (7, {})} | custom-call | flops 999999995904 | bytes 1 | tf_op jit(solution)/shard_map/sorted_products/pallas_call | solution.py:81
  105.1 5.8 %on_chip.5.refs_1_ = f32[1024,512]{1,0:T(8,128)S(1)} custom-call(bf16[3,8,256,256]{3,2,1,0:T(8,128)(2,1)S(1)} %copy-done.6, f32[1024,512]{1,0:T(8,128)} %get-tuple-element.39.refs_1_, f32[1024,512]{1,0:T(8,128)} %collective-permute-done.7.refs_1_.refs_2_, f32[1024,512]{1,0:T(8,128)S(1)} %get-tuple-element.42.refs_3_.refs_7_), custom_call_target="tpu_custom_call" | custom-call | flops 999999995904 | bytes 1 | tf_op jit(solution)/shard_map/on_chip/pallas_call | solution.py:81
  111.0 4.4 %across.5 = (bf16[512,1024]{1,0:T(8,128)(2,1)S(1)}, bf16[512,1024]{1,0:T(8,128)(2,1)S(1)}) custom-call(bf16[3,8,256,256]{3,2,1,0:T(8,128)(2,1)S(1)} %copy-done.6, f32[1024,512]{1,0:T(8,128)S(1)} %on_chip.5.refs_1_, f32[1024,256]{1,0:T(8,128)} %collective-permute-done.5.refs_4_.refs_2_, f32[1024,256]{1,0:T(8,128)} %collective-permute-done.10.refs_3_), custom_call_target="tpu_custom_call" | custom-call | flops 999999995904 | bytes 1 | tf_op jit(solution)/shard_map/across/pallas_call | solution.py:81
  115.4 4.7 %collective-permute-done.11.refs_1_.refs_9_ = f32[1024,256]{1,0:T(8,128)} collective-permute-done((f32[1024,256]{1,0:T(8,128)}, f32[1024,256]{1,0:T(8,128)}, u32[]{:S(2)}, u32[]{:S(2)}) %collective-permute-start.11) | collective-permute-done | bytes 1048608 | tf_op jit(solution)/shard_map/ppermute | solution.py:654
  123.6 7.5 %sorted_products.3 = (f32[1024,512]{1,0:T(8,128)S(1)}, f32[1024,512]{1,0:T(8,128)}, f32[1024,256]{1,0:T(8,128)}) custom-call(s32[1]{0:T(128)} %bitcast.10.refs_0_, bf16[512,1024]{1,0:T(8,128)(2,1)S(1)} %get-tuple-element.44.refs_0_.refs_1_.refs_2_.refs_3_, ...), custom_call_target="tpu_custom_call", output_to_operand_aliasing={{0}: (7, {}), {1}: (8, {}), {2}: (9, {})} | custom-call | flops 999999995904 | bytes 1 | tf_op jit(solution)/shard_map/sorted_products/pallas_call | solution.py:81
  133.4 4.6 %both_products.4.refs_2_.refs_0_ = f32[1024,256]{1,0:T(8,128)} custom-call(bf16[512,1024]{1,0:T(8,128)(2,1)S(1)} %copy-done.13, bf16[512,1024]{1,0:T(8,128)(2,1)S(1)} %copy-done.17, bf16[512,1024]{1,0:T(8,128)(2,1)S(1)} %get-tuple-element.44.refs_0_.refs_1_.refs_2_.refs_3_, bf16[512,1024]{1,0:T(8,128)(2,1)S(1)} %get-tuple-element.45.refs_2_.refs_3_.refs_4_, ...), custom_call_target="tpu_custom_call" | custom-call | flops 999999995904 | bytes 1 | tf_op jit(solution)/shard_map/both_products/pallas_call | solution.py:81
  144.2 3.8 %collective-permute-start.14 = (f32[1024,512]{1,0:T(8,128)}, f32[1024,512]{1,0:T(8,128)}, u32[]{:S(2)}, u32[]{:S(2)}) collective-permute-start(f32[1024,512]{1,0:T(8,128)} %plus.5.refs_6_.refs_1_), channel_id=1, source_target_pairs={{8,0},{12,4},{9,1},{13,5},{2,10},{6,14},{3,11},{7,15},{24,16},{28,... | collective-permute-start | bytes 6291464 | tf_op jit(solution)/shard_map/ppermute | solution.py:722
  148.0 4.3 %both_products.5 = (f32[1024,256]{1,0:T(8,128)S(1)}, f32[1024,256]{1,0:T(8,128)}) custom-call(bf16[512,1024]{1,0:T(8,128)(2,1)S(1)} %copy-done.14, bf16[512,1024]{1,0:T(8,128)(2,1)S(1)} %copy-done.18, bf16[512,1024]{1,0:T(8,128)(2,1)S(1)} %get-tuple-element.44.refs_0_.refs_1_.refs_2_.refs_3_, ...), custom_call_target="tpu_custom_call", output_to_operand_aliasing={{1}: (7, {})} | custom-call | flops 999999995904 | bytes 1 | tf_op jit(solution)/shard_map/both_products/pallas_call | solution.py:81
  161.0 4.6 %pair_products.1 = (f32[1024,256]{1,0:T(8,128)S(1)}, f32[1024,256]{1,0:T(8,128)}) custom-call(s32[1]{0:T(128)} %bitcast.11.refs_0_, bf16[512,1024]{1,0:T(8,128)(2,1)S(1)} %copy-done.15, bf16[512,1024]{1,0:T(8,128)(2,1)S(1)} %copy-done.19, bf16[512,1024]{1,0:T(8,128)(2,1)S(1)} %get-tuple-element.44.refs_0_.refs_1_.refs_2_.refs_3_, ...), custom_call_target="tpu_custom_call" | custom-call | flops 999999995904 | bytes 1 | tf_op jit(solution)/shard_map/pair_products/pallas_call | solution.py:81
  173.4 4.0 %both_products.6.refs_6_.refs_0_ = f32[1024,128]{1,0:T(8,128)} custom-call(bf16[512,1024]{1,0:T(8,128)(2,1)S(1)} %copy-done.15, bf16[512,1024]{1,0:T(8,128)(2,1)S(1)} %copy-done.19, bf16[512,1024]{1,0:T(8,128)(2,1)S(1)} %get-tuple-element.44.refs_0_.refs_1_.refs_2_.refs_3_, bf16[512,1024]{1,0:T(8,128)(2,1)S(1)} %copy-done.11, ...), custom_call_target="tpu_custom_call" | custom-call | flops 999999995904 | bytes 1 | tf_op jit(solution)/shard_map/both_products/pallas_call | solution.py:81
  179.7 4.0 %both_products.7.refs_2_.refs_0_ = f32[1024,128]{1,0:T(8,128)} custom-call(bf16[512,1024]{1,0:T(8,128)(2,1)S(1)} %copy-done.15, bf16[512,1024]{1,0:T(8,128)(2,1)S(1)} %copy-done.19, bf16[512,1024]{1,0:T(8,128)(2,1)S(1)} %get-tuple-element.44.refs_0_.refs_1_.refs_2_.refs_3_, bf16[512,1024]{1,0:T(8,128)(2,1)S(1)} %copy-done.11, ...), custom_call_target="tpu_custom_call" | custom-call | flops 999999995904 | bytes 1 | tf_op jit(solution)/shard_map/both_products/pallas_call | solution.py:81
  194.7 3.8 %collective-permute-done.25.refs_5_ = f32[1024,256]{1,0:T(8,128)} collective-permute-done((f32[1024,256]{1,0:T(8,128)}, f32[1024,256]{1,0:T(8,128)}, u32[]{:S(2)}, u32[]{:S(2)}) %collective-permute-start.25) | collective-permute-done | bytes 1048608 | tf_op jit(solution)/shard_map/ppermute | solution.py:765
  205.7 5.6 %collective-permute-done.27.refs_3_.refs_5_ = f32[1024,128]{1,0:T(8,128)} collective-permute-done((f32[1024,128]{1,0:T(8,128)}, f32[1024,128]{1,0:T(8,128)}, u32[]{:S(2)}, u32[]{:S(2)}) %collective-permute-start.27) | collective-permute-done | bytes 524320 | tf_op jit(solution)/shard_map/ppermute | solution.py:672
  (108 shorter events, 80.4 us)
Async XLA Ops:
  3.2 13.2 %collective-permute-start = (f32[1024]{0:T(1024)}, f32[1024]{0:T(1024)}, u32[]{:S(2)}, u32[]{:S(2)}) collective-permute-start(f32[1024]{0:T(1024)} %select_reduce_fusion.1), channel_id=1, source_target_pairs={{0,4},{4,8},{8,12},{12,0},{1,5},{5,9},{9,13},{13,1},{2,6},{6,10},{... | collective-permute-start | bytes 12296 | tf_op jit(solution)/shard_map/ppermute | solution.py:685
  7.4 25.6 %collective-permute-start.2 = (f32[1024,256]{1,0:T(8,128)}, f32[1024,256]{1,0:T(8,128)}, u32[]{:S(2)}, u32[]{:S(2)}) collective-permute-start(f32[1024,256]{1,0:T(8,128)} %get-tuple-element.33.refs_3_), channel_id=1, source_target_pairs={{4,8},{12,0},{8,4},{0,12},{5,9},{13,1},{9,5},{1,13},{6,10},{14,2},... | collective-permute-start | bytes 3145736 | tf_op jit(solution)/shard_map/ppermute | solution.py:654
  14.1 12.4 %collective-permute-start.1 = (f32[1024,512]{1,0:T(8,128)}, f32[1024,512]{1,0:T(8,128)}, u32[]{:S(2)}, u32[]{:S(2)}) collective-permute-start(f32[1024,512]{1,0:T(8,128)} %get-tuple-element.34.refs_6_.refs_1_), channel_id=1, source_target_pairs={{0,4},{8,12},{4,0},{12,8},{1,5},{9,13},{5,1},{13,9},{2,6},{10,14},... | collective-permute-start | bytes 6291464 | tf_op jit(solution)/shard_map/ppermute | solution.py:654
  14.2 41.3 %collective-permute-start.3 = (f32[1024,256]{1,0:T(8,128)}, f32[1024,256]{1,0:T(8,128)}, u32[]{:S(2)}, u32[]{:S(2)}) collective-permute-start(f32[1024,256]{1,0:T(8,128)} %get-tuple-element.37), channel_id=1, source_target_pairs={{4,8},{12,0},{8,4},{0,12},{5,9},{13,1},{9,5},{1,13},{6,10},{14,2},... | collective-permute-start | bytes 3145736 | tf_op jit(solution)/shard_map/ppermute | solution.py:654
  36.9 25.5 %collective-permute-start.4 = (f32[1024,256]{1,0:T(8,128)}, f32[1024,256]{1,0:T(8,128)}, u32[]{:S(2)}, u32[]{:S(2)}) collective-permute-start(f32[1024,256]{1,0:T(8,128)} %across.3.refs_4_.refs_1_.refs_3_), channel_id=1, source_target_pairs={{0,1},{2,3},{1,0},{3,2},{4,5},{6,7},{5,4},{7,6},{8,9},{10,11},{9,8... | collective-permute-start | bytes 3145736 | tf_op jit(solution)/shard_map/ppermute | solution.py:654
  38.5 38.7 %collective-permute-start.5 = (f32[1024,256]{1,0:T(8,128)}, f32[1024,256]{1,0:T(8,128)}, u32[]{:S(2)}, u32[]{:S(2)}) collective-permute-start(f32[1024,256]{1,0:T(8,128)} %across.3.refs_4_.refs_1_.refs_3_), channel_id=1, source_target_pairs={{4,8},{12,0},{8,4},{0,12},{5,9},{13,1},{9,5},{1,13},{6,10},{14,2},... | collective-permute-start | bytes 3145736 | tf_op jit(solution)/shard_map/ppermute | solution.py:654
  40.4 36.8 %collective-permute-start.6 = (f32[1024,256]{1,0:T(8,128)}, f32[1024,256]{1,0:T(8,128)}, u32[]{:S(2)}, u32[]{:S(2)}) collective-permute-start(f32[1024,256]{1,0:T(8,128)} %across.3.refs_4_.refs_1_.refs_3_), channel_id=1, source_target_pairs={{1,2},{2,1},{5,6},{6,5},{9,10},{10,9},{13,14},{14,13},{17,18},{18,... | collective-permute-start | bytes 3145736 | tf_op jit(solution)/shard_map/ppermute | solution.py:654
  59.2 32.8 %collective-permute-start.8 = (f32[1024,256]{1,0:T(8,128)}, f32[1024,256]{1,0:T(8,128)}, u32[]{:S(2)}, u32[]{:S(2)}) collective-permute-start(f32[1024,256]{1,0:T(8,128)} %across.4.refs_2_.refs_4_), channel_id=1, source_target_pairs={{1,2},{2,1},{5,6},{6,5},{9,10},{10,9},{13,14},{14,13},{17,18},{18,... | collective-permute-start | bytes 3145736 | tf_op jit(solution)/shard_map/ppermute | solution.py:654
  61.6 33.7 %collective-permute-start.9 = (f32[1024,256]{1,0:T(8,128)}, f32[1024,256]{1,0:T(8,128)}, u32[]{:S(2)}, u32[]{:S(2)}) collective-permute-start(f32[1024,256]{1,0:T(8,128)} %across.4.refs_2_.refs_4_), channel_id=1, source_target_pairs={{0,1},{2,3},{1,0},{3,2},{4,5},{6,7},{5,4},{7,6},{8,9},{10,11},{9,8... | collective-permute-start | bytes 3145736 | tf_op jit(solution)/shard_map/ppermute | solution.py:654
  85.8 25.2 %collective-permute-start.10 = (f32[1024,256]{1,0:T(8,128)}, f32[1024,256]{1,0:T(8,128)}, u32[]{:S(2)}, u32[]{:S(2)}) collective-permute-start(f32[1024,256]{1,0:T(8,128)} %get-tuple-element.43), channel_id=1, source_target_pairs={{4,8},{12,0},{8,4},{0,12},{5,9},{13,1},{9,5},{1,13},{6,10},{14,2},... | collective-permute-start | bytes 3145736 | tf_op jit(solution)/shard_map/ppermute | solution.py:654
  87.6 45.7 %collective-permute-start.13 = (f32[1024,256]{1,0:T(8,128)}, f32[1024,256]{1,0:T(8,128)}, u32[]{:S(2)}, u32[]{:S(2)}) collective-permute-start(f32[1024,256]{1,0:T(8,128)} %get-tuple-element.49.refs_4_), channel_id=1, source_target_pairs={{2,3},{1,0},{6,7},{5,4},{10,11},{9,8},{14,15},{13,12},{18,19},{17,... | collective-permute-start | bytes 3145736 | tf_op jit(solution)/shard_map/ppermute | solution.py:731
  93.4 26.8 %collective-permute-start.11 = (f32[1024,256]{1,0:T(8,128)}, f32[1024,256]{1,0:T(8,128)}, u32[]{:S(2)}, u32[]{:S(2)}) collective-permute-start(f32[1024,256]{1,0:T(8,128)} %gate.3.refs_5_), channel_id=1, source_target_pairs={{1,2},{2,1},{5,6},{6,5},{9,10},{10,9},{13,14},{14,13},{17,18},{18,... | collective-permute-start | bytes 3145736 | tf_op jit(solution)/shard_map/ppermute | solution.py:654
  102.8 45.2 %collective-permute-start.15 = (f32[1024,256]{1,0:T(8,128)}, f32[1024,256]{1,0:T(8,128)}, u32[]{:S(2)}, u32[]{:S(2)}) collective-permute-start(f32[1024,256]{1,0:T(8,128)} %get-tuple-element.50.refs_4_), channel_id=1, source_target_pairs={{2,3},{1,0},{6,7},{5,4},{10,11},{9,8},{14,15},{13,12},{18,19},{17,... | collective-permute-start | bytes 3145736 | tf_op jit(solution)/shard_map/ppermute | solution.py:736
  121.4 26.6 %collective-permute-start.16 = (f32[1024,256]{1,0:T(8,128)}, f32[1024,256]{1,0:T(8,128)}, u32[]{:S(2)}, u32[]{:S(2)}) collective-permute-start(f32[1024,256]{1,0:T(8,128)} %gate.4.refs_6_), channel_id=1, source_target_pairs={{1,2},{2,1},{5,6},{6,5},{9,10},{10,9},{13,14},{14,13},{17,18},{18,... | collective-permute-start | bytes 3145736 | tf_op jit(solution)/shard_map/ppermute | solution.py:654
  131.1 10.2 %collective-permute-start.12 = (f32[1024,512]{1,0:T(8,128)}, f32[1024,512]{1,0:T(8,128)}, u32[]{:S(2)}, u32[]{:S(2)}) collective-permute-start(f32[1024,512]{1,0:T(8,128)} %get-tuple-element.48), channel_id=1, source_target_pairs={{0,4},{8,12},{4,0},{12,8},{1,5},{9,13},{5,1},{13,9},{2,6},{10,14},... | collective-permute-start | bytes 6291464 | tf_op jit(solution)/shard_map/ppermute | solution.py:654
  131.1 29.8 %collective-permute-start.17 = (f32[1024,256]{1,0:T(8,128)}, f32[1024,256]{1,0:T(8,128)}, u32[]{:S(2)}, u32[]{:S(2)}) collective-permute-start(f32[1024,256]{1,0:T(8,128)} %get-tuple-element.52.refs_6_), channel_id=1, source_target_pairs={{2,3},{1,0},{6,7},{5,4},{10,11},{9,8},{14,15},{13,12},{18,19},{17,... | collective-permute-start | bytes 3145736 | tf_op jit(solution)/shard_map/ppermute | solution.py:741
  137.9 14.4 %collective-permute-start.18 = (f32[1024,256]{1,0:T(8,128)}, f32[1024,256]{1,0:T(8,128)}, u32[]{:S(2)}, u32[]{:S(2)}) collective-permute-start(f32[1024,256]{1,0:T(8,128)} %both_products.4.refs_2_.refs_0_), channel_id=1, source_target_pairs={{12,8},{4,0},{13,9},{5,1},{2,6},{10,14},{3,7},{11,15},{28,24},{20,... | collective-permute-start | bytes 3145736 | tf_op jit(solution)/shard_map/ppermute | solution.py:672
  144.2 48.1 %collective-permute-start.14 = (f32[1024,512]{1,0:T(8,128)}, f32[1024,512]{1,0:T(8,128)}, u32[]{:S(2)}, u32[]{:S(2)}) collective-permute-start(f32[1024,512]{1,0:T(8,128)} %plus.5.refs_6_.refs_1_), channel_id=1, source_target_pairs={{8,0},{12,4},{9,1},{13,5},{2,10},{6,14},{3,11},{7,15},{24,16},{28,... | collective-permute-start | bytes 6291464 | tf_op jit(solution)/shard_map/ppermute | solution.py:722
  154.9 10.6 %collective-permute-start.19 = (f32[1024,256]{1,0:T(8,128)}, f32[1024,256]{1,0:T(8,128)}, u32[]{:S(2)}, u32[]{:S(2)}) collective-permute-start(f32[1024,256]{1,0:T(8,128)} %plus.6.refs_8_.refs_2_), channel_id=1, source_target_pairs={{0,8},{1,9},{14,6},{15,7},{16,24},{17,25},{30,22},{31,23}} | collective-permute-start | bytes 3145736 | tf_op jit(solution)/shard_map/ppermute | solution.py:672
  158.8 14.5 %collective-permute-start.21 = (f32[1024,128]{1,0:T(8,128)}, f32[1024,128]{1,0:T(8,128)}, u32[]{:S(2)}, u32[]{:S(2)}) collective-permute-start(f32[1024,128]{1,0:T(8,128)} %get-tuple-element.61.refs_4_), channel_id=1, source_target_pairs={{2,3},{1,0},{6,7},{5,4},{10,11},{9,8},{14,15},{13,12},{18,19},{17,... | collective-permute-start | bytes 1572872 | tf_op jit(solution)/shard_map/ppermute | solution.py:754
  166.8 12.9 %collective-permute-start.20 = (f32[1024,128]{1,0:T(8,128)}, f32[1024,128]{1,0:T(8,128)}, u32[]{:S(2)}, u32[]{:S(2)}) collective-permute-start(f32[1024,128]{1,0:T(8,128)} %gate.5.refs_2_.refs_4_), channel_id=1, source_target_pairs={{2,3},{1,0},{6,7},{5,4},{10,11},{9,8},{14,15},{13,12},{18,19},{17,... | collective-permute-start | bytes 1572872 | tf_op jit(solution)/shard_map/ppermute | solution.py:760
  171.9 26.6 %collective-permute-start.25 = (f32[1024,256]{1,0:T(8,128)}, f32[1024,256]{1,0:T(8,128)}, u32[]{:S(2)}, u32[]{:S(2)}) collective-permute-start(f32[1024,256]{1,0:T(8,128)} %plus.7.refs_6_.refs_4_), channel_id=1, source_target_pairs={{0,8},{4,12},{1,9},{5,13},{10,2},{14,6},{11,3},{15,7},{16,24},{20,... | collective-permute-start | bytes 3145736 | tf_op jit(solution)/shard_map/ppermute | solution.py:765
  186.9 18.8 %collective-permute-start.26 = (f32[1024,128]{1,0:T(8,128)}, f32[1024,128]{1,0:T(8,128)}, u32[]{:S(2)}, u32[]{:S(2)}) collective-permute-start(f32[1024,128]{1,0:T(8,128)} %plus.8.refs_2_.refs_6_), channel_id=1, source_target_pairs={{4,12},{5,13},{10,2},{11,3},{20,28},{21,29},{26,18},{27,19}} | collective-permute-start | bytes 1572872 | tf_op jit(solution)/shard_map/ppermute | solution.py:672
  190.9 20.4 %collective-permute-start.27 = (f32[1024,128]{1,0:T(8,128)}, f32[1024,128]{1,0:T(8,128)}, u32[]{:S(2)}, u32[]{:S(2)}) collective-permute-start(f32[1024,128]{1,0:T(8,128)} %plus.9.refs_3_.refs_7_), channel_id=1, source_target_pairs={{4,12},{5,13},{10,2},{11,3},{20,28},{21,29},{26,18},{27,19}} | collective-permute-start | bytes 1572872 | tf_op jit(solution)/shard_map/ppermute | solution.py:672
  (25 other events, 209.4 us)

commit v5 on v4

--- a/solution.py
+++ b/solution.py
@@ -90,7 +90,7 @@
 
 
 def plus(left, right, after, passed=()):
-    rows = min(512, left.shape[0])
+    rows = min(256 if left.shape[1] <= 128 else 512, left.shape[0])
     part = pl.BlockSpec((rows, left.shape[1]), lambda i: (i, 0))
     return call(
         plus_kernel,

time: 215 us -> 215 us (level)
  Pallas kernels: 109 us -> 112 us
  waiting for transfers between devices: 44.7 us -> 42 us
    pallas_call x29, Pallas kernels: 109 us -> 112 us  [call(): return lambda *args: made(*args, *extra)]
  transfers between devices with their start and end apart: 28 -> 28, of which waited for: 9 -> 8; matrix products, arithmetic and copies ran while one was open for 1% -> 1% of each run, Pallas kernels for 50% -> 51%
where the time goes in v5:
time: 215 us; the launch traced here: 214 us
  Pallas kernels  112 us (52%)
  starting transfers between devices  48.8 us (23%)
  waiting for transfers between devices  42 us (20%)
  local copies, waits for them, and re-layouts  6.8 us (3%)
  other arithmetic  3.2 us (1%)
    pallas_call x29, Pallas kernels, call(): return lambda *args: made(*args, *extra)  112 us
    ppermute x14, waiting for transfers between devices, exchange(): return lax.ppermute(block, axis, pairs + [(b, a) for a, b in pairs])  29.9 us
    ppermute x14, starting transfers between devices, exchange(): return lax.ppermute(block, axis, pairs + [(b, a) for a, b in pairs])  19.2 us
    ppermute x6, starting transfers between devices, to_owner(): return lax.ppermute(block, ('dom', 'band'), route)  10.1 us
    ppermute x6, waiting for transfers between devices, to_owner(): return lax.ppermute(block, ('dom', 'band'), route)  9.24 us
    unnamed x42, local copies, waits for them, and re-layouts  4.51 us
    ppermute x1, starting transfers between devices, on_device(): second_out = [lax.ppermute(second_middle[0], 'band', outward)]  4.44 us
  transfers between devices with their start and end apart: 28, of which 8 were waited for; matrix products, arithmetic and copies ran while one was open for 1% of the time, Pallas kernels for 51%

profile of v5, /device:TPU:18, one launch (start us, length us, event | category | flops | bytes accessed | tf_op | source)
XLA Modules:
  0.0 213.5 jit_solution(8124354361686687619)
XLA Ops:
  3.2 4.2 %to_grid.2 = (f32[1024,256]{1,0:T(8,128)}, f32[1024,512]{1,0:T(8,128)}) custom-call(s32[8,128]{1,0:T(8,128)} %bitcast.12, f32[1024,512]{1,0:T(8,128)} %refs_1_.3), custom_call_target="tpu_custom_call" | custom-call | flops 999999995904 | bytes 1 | tf_op jit(solution)/shard_map/to_grid/pallas_call | solution.py:81
  10.5 3.6 %to_grid.3 = (f32[1024,256]{1,0:T(8,128)}, f32[1024,512]{1,0:T(8,128)}) custom-call(s32[8,128]{1,0:T(8,128)S(1)} %bitcast.13, f32[1024,512]{1,0:T(8,128)S(1)} %copy-done.1, f32[1024,512]{1,0:T(8,128)} %get-tuple-element.32.refs_2_, f32[1024,256]{1,0:T(8,128)S(1)} %copy-done.3), custom_call_target="tpu_custom_call", output_to_operand_aliasing={{1}: (2, {})} | custom-call | flops 999999995904 | bytes 1 | tf_op jit(solution)/shard_map/to_grid/pallas_call | solution.py:81
  18.1 8.4 %prepare.1 = (bf16[3,8,256,256]{3,2,1,0:T(8,128)(2,1)S(1)}, f32[1024,512]{1,0:T(8,128)S(1)}) custom-call(s32[1]{0:T(128)} %bitcast.1.refs_0_, f32[1,1024]{1,0:T(1,128)} %bitcast.3.refs_1_, f32[1,1024]{1,0:T(1,128)} %bitcast.4.refs_2_, f32[1,1024]{1,0:T(1,128)S(1)} %bitcast.16, s32[8,128]{1,0:T(8,128)S(1)} %bitcast.14, f32[1024,512]{1,0:T(8,128)S(1)} %copy-done.2, ...), custom_call_target="tpu_custom_call" | custom-call | flops 999999995904 | bytes 1 | tf_op jit(solution)/shard_map/prepare/pallas_call | solution.py:81
  26.5 5.5 %on_chip.3.refs_1_ = f32[1024,256]{1,0:T(8,128)S(1)} custom-call(bf16[3,8,256,256]{3,2,1,0:T(8,128)(2,1)S(1)} %get-tuple-element.35.refs_0_, f32[1024,512]{1,0:T(8,128)} %get-tuple-element.34.refs_6_.refs_1_, f32[1024,512]{1,0:T(8,128)} %collective-permute-done.1.refs_2_, f32[1024,512]{1,0:T(8,128)S(1)} %get-tuple-element.36.refs_3_), custom_call_target="tpu_custom_call" | custom-call | flops 999999995904 | bytes 1 | tf_op jit(solution)/shard_map/on_chip/pallas_call | solution.py:81
  33.0 3.9 %across.3.refs_4_.refs_1_.refs_3_ = f32[1024,256]{1,0:T(8,128)} custom-call(bf16[3,8,256,256]{3,2,1,0:T(8,128)(2,1)S(1)} %get-tuple-element.35.refs_0_, f32[1024,256]{1,0:T(8,128)S(1)} %on_chip.3.refs_1_, f32[1024,256]{1,0:T(8,128)} %collective-permute-done.2.refs_2_), custom_call_target="tpu_custom_call" | custom-call | flops 999999995904 | bytes 1 | tf_op jit(solution)/shard_map/across/pallas_call | solution.py:81
  42.3 3.9 %on_chip.4.refs_1_ = f32[1024,256]{1,0:T(8,128)S(1)} custom-call(bf16[3,8,256,256]{3,2,1,0:T(8,128)(2,1)S(1)} %get-tuple-element.35.refs_0_, f32[1024,512]{1,0:T(8,128)} %get-tuple-element.34.refs_6_.refs_1_, f32[1024,512]{1,0:T(8,128)} %collective-permute-done.1.refs_2_, f32[1024,512]{1,0:T(8,128)S(1)} %copy-done.8, f32[1024,256]{1,0:T(8,128)} %across.3.refs_4_.refs_1_.refs_3_), custom_call_target="tpu_custom_call" | custom-call | flops 999999995904 | bytes 1 | tf_op jit(solution)/shard_map/on_chip/pallas_call | solution.py:81
  46.2 9.3 %collective-permute-done.3.refs_2_ = f32[1024,256]{1,0:T(8,128)} collective-permute-done((f32[1024,256]{1,0:T(8,128)}, f32[1024,256]{1,0:T(8,128)}, u32[]{:S(2)}, u32[]{:S(2)}) %collective-permute-start.3) | collective-permute-done | bytes 1048608 | tf_op jit(solution)/shard_map/ppermute | solution.py:654
  55.5 3.7 %across.4.refs_2_.refs_4_ = f32[1024,256]{1,0:T(8,128)} custom-call(bf16[3,8,256,256]{3,2,1,0:T(8,128)(2,1)S(1)} %get-tuple-element.35.refs_0_, f32[1024,256]{1,0:T(8,128)S(1)} %on_chip.4.refs_1_, f32[1024,256]{1,0:T(8,128)} %collective-permute-done.3.refs_2_), custom_call_target="tpu_custom_call" | custom-call | flops 999999995904 | bytes 1 | tf_op jit(solution)/shard_map/across/pallas_call | solution.py:81
  62.4 14.8 %collective-permute-done.5.refs_4_.refs_2_ = f32[1024,256]{1,0:T(8,128)} collective-permute-done((f32[1024,256]{1,0:T(8,128)}, f32[1024,256]{1,0:T(8,128)}, u32[]{:S(2)}, u32[]{:S(2)}) %collective-permute-start.5) | collective-permute-done | bytes 1048608 | tf_op jit(solution)/shard_map/ppermute | solution.py:654
  77.2 5.8 %from_grid.1 = (f32[1024,512]{1,0:T(8,128)}, f32[1024,512]{1,0:T(8,128)}, f32[1024,256]{1,0:T(8,128)}, bf16[512,1024]{1,0:T(8,128)(2,1)S(1)}, bf16[512,1024]{1,0:T(8,128)(2,1)S(1)}, /*index=5*/f32[1024,256]{1,0:T(8,128)}) custom-call(s32[1,1024]{1,0:T(1,128)S(1)} %bitcast.15, ...), custom_call_target="tpu_custom_call", output_to_operand_aliasing={{5}: (5, {})} | custom-call | flops 999999995904 | bytes 1 | tf_op jit(solution)/shard_map/from_grid/pallas_call | solution.py:81
  87.6 4.4 %collective-permute-start.13 = (f32[1024,256]{1,0:T(8,128)}, f32[1024,256]{1,0:T(8,128)}, u32[]{:S(2)}, u32[]{:S(2)}) collective-permute-start(f32[1024,256]{1,0:T(8,128)} %get-tuple-element.49.refs_4_), channel_id=1, source_target_pairs={{2,3},{1,0},{6,7},{5,4},{10,11},{9,8},{14,15},{13,12},{18,19},{17,... | collective-permute-start | bytes 3145736 | tf_op jit(solution)/shard_map/ppermute | solution.py:731
  95.3 7.5 %sorted_products.2 = (f32[1024,512]{1,0:T(8,128)S(1)}, f32[1024,512]{1,0:T(8,128)}, f32[1024,256]{1,0:T(8,128)}) custom-call(s32[1]{0:T(128)} %bitcast.10.refs_0_, bf16[512,1024]{1,0:T(8,128)(2,1)S(1)} %get-tuple-element.40.refs_1_.refs_0_, bf16[512,1024]{1,0:T(8,128)(2,1)S(1)} %get-tuple-element.41.refs_2_.refs_1_, ...), custom_call_target="tpu_custom_call", output_to_operand_aliasing={{2}: (7, {})} | custom-call | flops 999999995904 | bytes 1 | tf_op jit(solution)/shard_map/sorted_products/pallas_call | solution.py:81
  105.1 5.8 %on_chip.5.refs_1_ = f32[1024,512]{1,0:T(8,128)S(1)} custom-call(bf16[3,8,256,256]{3,2,1,0:T(8,128)(2,1)S(1)} %copy-done.6, f32[1024,512]{1,0:T(8,128)} %get-tuple-element.39.refs_1_, f32[1024,512]{1,0:T(8,128)} %collective-permute-done.7.refs_1_.refs_2_, f32[1024,512]{1,0:T(8,128)S(1)} %get-tuple-element.42.refs_3_.refs_7_), custom_call_target="tpu_custom_call" | custom-call | flops 999999995904 | bytes 1 | tf_op jit(solution)/shard_map/on_chip/pallas_call | solution.py:81
  111.0 4.4 %across.5 = (bf16[512,1024]{1,0:T(8,128)(2,1)S(1)}, bf16[512,1024]{1,0:T(8,128)(2,1)S(1)}) custom-call(bf16[3,8,256,256]{3,2,1,0:T(8,128)(2,1)S(1)} %copy-done.6, f32[1024,512]{1,0:T(8,128)S(1)} %on_chip.5.refs_1_, f32[1024,256]{1,0:T(8,128)} %collective-permute-done.5.refs_4_.refs_2_, f32[1024,256]{1,0:T(8,128)} %collective-permute-done.10.refs_3_), custom_call_target="tpu_custom_call" | custom-call | flops 999999995904 | bytes 1 | tf_op jit(solution)/shard_map/across/pallas_call | solution.py:81
  115.4 4.7 %collective-permute-done.11.refs_1_.refs_9_ = f32[1024,256]{1,0:T(8,128)} collective-permute-done((f32[1024,256]{1,0:T(8,128)}, f32[1024,256]{1,0:T(8,128)}, u32[]{:S(2)}, u32[]{:S(2)}) %collective-permute-start.11) | collective-permute-done | bytes 1048608 | tf_op jit(solution)/shard_map/ppermute | solution.py:654
  123.6 7.5 %sorted_products.3 = (f32[1024,512]{1,0:T(8,128)S(1)}, f32[1024,512]{1,0:T(8,128)}, f32[1024,256]{1,0:T(8,128)}) custom-call(s32[1]{0:T(128)} %bitcast.10.refs_0_, bf16[512,1024]{1,0:T(8,128)(2,1)S(1)} %get-tuple-element.44.refs_0_.refs_1_.refs_2_.refs_3_, ...), custom_call_target="tpu_custom_call", output_to_operand_aliasing={{0}: (7, {}), {1}: (8, {}), {2}: (9, {})} | custom-call | flops 999999995904 | bytes 1 | tf_op jit(solution)/shard_map/sorted_products/pallas_call | solution.py:81
  133.4 4.6 %both_products.4.refs_2_.refs_0_ = f32[1024,256]{1,0:T(8,128)} custom-call(bf16[512,1024]{1,0:T(8,128)(2,1)S(1)} %copy-done.13, bf16[512,1024]{1,0:T(8,128)(2,1)S(1)} %copy-done.17, bf16[512,1024]{1,0:T(8,128)(2,1)S(1)} %get-tuple-element.44.refs_0_.refs_1_.refs_2_.refs_3_, bf16[512,1024]{1,0:T(8,128)(2,1)S(1)} %get-tuple-element.45.refs_2_.refs_3_.refs_4_, ...), custom_call_target="tpu_custom_call" | custom-call | flops 999999995904 | bytes 1 | tf_op jit(solution)/shard_map/both_products/pallas_call | solution.py:81
  144.2 3.8 %collective-permute-start.14 = (f32[1024,512]{1,0:T(8,128)}, f32[1024,512]{1,0:T(8,128)}, u32[]{:S(2)}, u32[]{:S(2)}) collective-permute-start(f32[1024,512]{1,0:T(8,128)} %plus.5.refs_6_.refs_1_), channel_id=1, source_target_pairs={{8,0},{12,4},{9,1},{13,5},{2,10},{6,14},{3,11},{7,15},{24,16},{28,... | collective-permute-start | bytes 6291464 | tf_op jit(solution)/shard_map/ppermute | solution.py:722
  148.0 4.3 %both_products.5 = (f32[1024,256]{1,0:T(8,128)S(1)}, f32[1024,256]{1,0:T(8,128)}) custom-call(bf16[512,1024]{1,0:T(8,128)(2,1)S(1)} %copy-done.14, bf16[512,1024]{1,0:T(8,128)(2,1)S(1)} %copy-done.18, bf16[512,1024]{1,0:T(8,128)(2,1)S(1)} %get-tuple-element.44.refs_0_.refs_1_.refs_2_.refs_3_, ...), custom_call_target="tpu_custom_call", output_to_operand_aliasing={{1}: (7, {})} | custom-call | flops 999999995904 | bytes 1 | tf_op jit(solution)/shard_map/both_products/pallas_call | solution.py:81
  161.0 4.6 %pair_products.1 = (f32[1024,256]{1,0:T(8,128)S(1)}, f32[1024,256]{1,0:T(8,128)}) custom-call(s32[1]{0:T(128)} %bitcast.11.refs_0_, bf16[512,1024]{1,0:T(8,128)(2,1)S(1)} %copy-done.15, bf16[512,1024]{1,0:T(8,128)(2,1)S(1)} %copy-done.19, bf16[512,1024]{1,0:T(8,128)(2,1)S(1)} %get-tuple-element.44.refs_0_.refs_1_.refs_2_.refs_3_, ...), custom_call_target="tpu_custom_call" | custom-call | flops 999999995904 | bytes 1 | tf_op jit(solution)/shard_map/pair_products/pallas_call | solution.py:81
  173.4 4.0 %both_products.6.refs_6_.refs_0_ = f32[1024,128]{1,0:T(8,128)} custom-call(bf16[512,1024]{1,0:T(8,128)(2,1)S(1)} %copy-done.15, bf16[512,1024]{1,0:T(8,128)(2,1)S(1)} %copy-done.19, bf16[512,1024]{1,0:T(8,128)(2,1)S(1)} %get-tuple-element.44.refs_0_.refs_1_.refs_2_.refs_3_, bf16[512,1024]{1,0:T(8,128)(2,1)S(1)} %copy-done.11, ...), custom_call_target="tpu_custom_call" | custom-call | flops 999999995904 | bytes 1 | tf_op jit(solution)/shard_map/both_products/pallas_call | solution.py:81
  179.7 4.0 %both_products.7.refs_2_.refs_0_ = f32[1024,128]{1,0:T(8,128)} custom-call(bf16[512,1024]{1,0:T(8,128)(2,1)S(1)} %copy-done.15, bf16[512,1024]{1,0:T(8,128)(2,1)S(1)} %copy-done.19, bf16[512,1024]{1,0:T(8,128)(2,1)S(1)} %get-tuple-element.44.refs_0_.refs_1_.refs_2_.refs_3_, bf16[512,1024]{1,0:T(8,128)(2,1)S(1)} %copy-done.11, ...), custom_call_target="tpu_custom_call" | custom-call | flops 999999995904 | bytes 1 | tf_op jit(solution)/shard_map/both_products/pallas_call | solution.py:81
  198.5 3.6 %finish_most.1 = (f32[512,512]{1,0:T(8,128)}, f32[512,512]{1,0:T(8,128)}, f32[1024,256]{1,0:T(8,128)S(1)}) custom-call(s32[3]{0:T(128)S(1)} %add_convert_fusion.refs_0_, f32[1024,512]{1,0:T(8,128)S(1)} %near_rows.1.refs_1_, f32[1024,256]{1,0:T(8,128)} %plus.6.refs_8_.refs_2_, f32[1024,256]{1,0:T(8,128)} %collective-permute-done.19.refs_1_.refs_3_, ...), custom_call_target="tpu_custom_call" | custom-call | flops 999999995904 | bytes 1 | tf_op jit(solution)/shard_map/finish_most/pallas_call | solution.py:81
  205.7 5.6 %collective-permute-done.27.refs_3_.refs_5_ = f32[1024,128]{1,0:T(8,128)} collective-permute-done((f32[1024,128]{1,0:T(8,128)}, f32[1024,128]{1,0:T(8,128)}, u32[]{:S(2)}, u32[]{:S(2)}) %collective-permute-start.27) | collective-permute-done | bytes 524320 | tf_op jit(solution)/shard_map/ppermute | solution.py:672
  (108 shorter events, 80.6 us)
Async XLA Ops:
  3.2 13.2 %collective-permute-start = (f32[1024]{0:T(1024)}, f32[1024]{0:T(1024)}, u32[]{:S(2)}, u32[]{:S(2)}) collective-permute-start(f32[1024]{0:T(1024)} %select_reduce_fusion.1), channel_id=1, source_target_pairs={{0,4},{4,8},{8,12},{12,0},{1,5},{5,9},{9,13},{13,1},{2,6},{6,10},{... | collective-permute-start | bytes 12296 | tf_op jit(solution)/shard_map/ppermute | solution.py:685
  7.4 25.6 %collective-permute-start.2 = (f32[1024,256]{1,0:T(8,128)}, f32[1024,256]{1,0:T(8,128)}, u32[]{:S(2)}, u32[]{:S(2)}) collective-permute-start(f32[1024,256]{1,0:T(8,128)} %get-tuple-element.33.refs_3_), channel_id=1, source_target_pairs={{4,8},{12,0},{8,4},{0,12},{5,9},{13,1},{9,5},{1,13},{6,10},{14,2},... | collective-permute-start | bytes 3145736 | tf_op jit(solution)/shard_map/ppermute | solution.py:654
  14.1 12.4 %collective-permute-start.1 = (f32[1024,512]{1,0:T(8,128)}, f32[1024,512]{1,0:T(8,128)}, u32[]{:S(2)}, u32[]{:S(2)}) collective-permute-start(f32[1024,512]{1,0:T(8,128)} %get-tuple-element.34.refs_6_.refs_1_), channel_id=1, source_target_pairs={{0,4},{8,12},{4,0},{12,8},{1,5},{9,13},{5,1},{13,9},{2,6},{10,14},... | collective-permute-start | bytes 6291464 | tf_op jit(solution)/shard_map/ppermute | solution.py:654
  14.2 41.3 %collective-permute-start.3 = (f32[1024,256]{1,0:T(8,128)}, f32[1024,256]{1,0:T(8,128)}, u32[]{:S(2)}, u32[]{:S(2)}) collective-permute-start(f32[1024,256]{1,0:T(8,128)} %get-tuple-element.37), channel_id=1, source_target_pairs={{4,8},{12,0},{8,4},{0,12},{5,9},{13,1},{9,5},{1,13},{6,10},{14,2},... | collective-permute-start | bytes 3145736 | tf_op jit(solution)/shard_map/ppermute | solution.py:654
  36.9 25.5 %collective-permute-start.4 = (f32[1024,256]{1,0:T(8,128)}, f32[1024,256]{1,0:T(8,128)}, u32[]{:S(2)}, u32[]{:S(2)}) collective-permute-start(f32[1024,256]{1,0:T(8,128)} %across.3.refs_4_.refs_1_.refs_3_), channel_id=1, source_target_pairs={{0,1},{2,3},{1,0},{3,2},{4,5},{6,7},{5,4},{7,6},{8,9},{10,11},{9,8... | collective-permute-start | bytes 3145736 | tf_op jit(solution)/shard_map/ppermute | solution.py:654
  38.5 38.7 %collective-permute-start.5 = (f32[1024,256]{1,0:T(8,128)}, f32[1024,256]{1,0:T(8,128)}, u32[]{:S(2)}, u32[]{:S(2)}) collective-permute-start(f32[1024,256]{1,0:T(8,128)} %across.3.refs_4_.refs_1_.refs_3_), channel_id=1, source_target_pairs={{4,8},{12,0},{8,4},{0,12},{5,9},{13,1},{9,5},{1,13},{6,10},{14,2},... | collective-permute-start | bytes 3145736 | tf_op jit(solution)/shard_map/ppermute | solution.py:654
  40.4 36.8 %collective-permute-start.6 = (f32[1024,256]{1,0:T(8,128)}, f32[1024,256]{1,0:T(8,128)}, u32[]{:S(2)}, u32[]{:S(2)}) collective-permute-start(f32[1024,256]{1,0:T(8,128)} %across.3.refs_4_.refs_1_.refs_3_), channel_id=1, source_target_pairs={{1,2},{2,1},{5,6},{6,5},{9,10},{10,9},{13,14},{14,13},{17,18},{18,... | collective-permute-start | bytes 3145736 | tf_op jit(solution)/shard_map/ppermute | solution.py:654
  59.2 32.8 %collective-permute-start.8 = (f32[1024,256]{1,0:T(8,128)}, f32[1024,256]{1,0:T(8,128)}, u32[]{:S(2)}, u32[]{:S(2)}) collective-permute-start(f32[1024,256]{1,0:T(8,128)} %across.4.refs_2_.refs_4_), channel_id=1, source_target_pairs={{1,2},{2,1},{5,6},{6,5},{9,10},{10,9},{13,14},{14,13},{17,18},{18,... | collective-permute-start | bytes 3145736 | tf_op jit(solution)/shard_map/ppermute | solution.py:654
  61.6 33.7 %collective-permute-start.9 = (f32[1024,256]{1,0:T(8,128)}, f32[1024,256]{1,0:T(8,128)}, u32[]{:S(2)}, u32[]{:S(2)}) collective-permute-start(f32[1024,256]{1,0:T(8,128)} %across.4.refs_2_.refs_4_), channel_id=1, source_target_pairs={{0,1},{2,3},{1,0},{3,2},{4,5},{6,7},{5,4},{7,6},{8,9},{10,11},{9,8... | collective-permute-start | bytes 3145736 | tf_op jit(solution)/shard_map/ppermute | solution.py:654
  85.8 25.2 %collective-permute-start.10 = (f32[1024,256]{1,0:T(8,128)}, f32[1024,256]{1,0:T(8,128)}, u32[]{:S(2)}, u32[]{:S(2)}) collective-permute-start(f32[1024,256]{1,0:T(8,128)} %get-tuple-element.43), channel_id=1, source_target_pairs={{4,8},{12,0},{8,4},{0,12},{5,9},{13,1},{9,5},{1,13},{6,10},{14,2},... | collective-permute-start | bytes 3145736 | tf_op jit(solution)/shard_map/ppermute | solution.py:654
  87.6 45.7 %collective-permute-start.13 = (f32[1024,256]{1,0:T(8,128)}, f32[1024,256]{1,0:T(8,128)}, u32[]{:S(2)}, u32[]{:S(2)}) collective-permute-start(f32[1024,256]{1,0:T(8,128)} %get-tuple-element.49.refs_4_), channel_id=1, source_target_pairs={{2,3},{1,0},{6,7},{5,4},{10,11},{9,8},{14,15},{13,12},{18,19},{17,... | collective-permute-start | bytes 3145736 | tf_op jit(solution)/shard_map/ppermute | solution.py:731
  93.4 26.8 %collective-permute-start.11 = (f32[1024,256]{1,0:T(8,128)}, f32[1024,256]{1,0:T(8,128)}, u32[]{:S(2)}, u32[]{:S(2)}) collective-permute-start(f32[1024,256]{1,0:T(8,128)} %gate.3.refs_5_), channel_id=1, source_target_pairs={{1,2},{2,1},{5,6},{6,5},{9,10},{10,9},{13,14},{14,13},{17,18},{18,... | collective-permute-start | bytes 3145736 | tf_op jit(solution)/shard_map/ppermute | solution.py:654
  102.8 45.2 %collective-permute-start.15 = (f32[1024,256]{1,0:T(8,128)}, f32[1024,256]{1,0:T(8,128)}, u32[]{:S(2)}, u32[]{:S(2)}) collective-permute-start(f32[1024,256]{1,0:T(8,128)} %get-tuple-element.50.refs_4_), channel_id=1, source_target_pairs={{2,3},{1,0},{6,7},{5,4},{10,11},{9,8},{14,15},{13,12},{18,19},{17,... | collective-permute-start | bytes 3145736 | tf_op jit(solution)/shard_map/ppermute | solution.py:736
  121.4 26.6 %collective-permute-start.16 = (f32[1024,256]{1,0:T(8,128)}, f32[1024,256]{1,0:T(8,128)}, u32[]{:S(2)}, u32[]{:S(2)}) collective-permute-start(f32[1024,256]{1,0:T(8,128)} %gate.4.refs_6_), channel_id=1, source_target_pairs={{1,2},{2,1},{5,6},{6,5},{9,10},{10,9},{13,14},{14,13},{17,18},{18,... | collective-permute-start | bytes 3145736 | tf_op jit(solution)/shard_map/ppermute | solution.py:654
  131.1 10.2 %collective-permute-start.12 = (f32[1024,512]{1,0:T(8,128)}, f32[1024,512]{1,0:T(8,128)}, u32[]{:S(2)}, u32[]{:S(2)}) collective-permute-start(f32[1024,512]{1,0:T(8,128)} %get-tuple-element.48), channel_id=1, source_target_pairs={{0,4},{8,12},{4,0},{12,8},{1,5},{9,13},{5,1},{13,9},{2,6},{10,14},... | collective-permute-start | bytes 6291464 | tf_op jit(solution)/shard_map/ppermute | solution.py:654
  131.1 29.8 %collective-permute-start.17 = (f32[1024,256]{1,0:T(8,128)}, f32[1024,256]{1,0:T(8,128)}, u32[]{:S(2)}, u32[]{:S(2)}) collective-permute-start(f32[1024,256]{1,0:T(8,128)} %get-tuple-element.52.refs_6_), channel_id=1, source_target_pairs={{2,3},{1,0},{6,7},{5,4},{10,11},{9,8},{14,15},{13,12},{18,19},{17,... | collective-permute-start | bytes 3145736 | tf_op jit(solution)/shard_map/ppermute | solution.py:741
  137.9 14.4 %collective-permute-start.18 = (f32[1024,256]{1,0:T(8,128)}, f32[1024,256]{1,0:T(8,128)}, u32[]{:S(2)}, u32[]{:S(2)}) collective-permute-start(f32[1024,256]{1,0:T(8,128)} %both_products.4.refs_2_.refs_0_), channel_id=1, source_target_pairs={{12,8},{4,0},{13,9},{5,1},{2,6},{10,14},{3,7},{11,15},{28,24},{20,... | collective-permute-start | bytes 3145736 | tf_op jit(solution)/shard_map/ppermute | solution.py:672
  144.2 50.1 %collective-permute-start.14 = (f32[1024,512]{1,0:T(8,128)}, f32[1024,512]{1,0:T(8,128)}, u32[]{:S(2)}, u32[]{:S(2)}) collective-permute-start(f32[1024,512]{1,0:T(8,128)} %plus.5.refs_6_.refs_1_), channel_id=1, source_target_pairs={{8,0},{12,4},{9,1},{13,5},{2,10},{6,14},{3,11},{7,15},{24,16},{28,... | collective-permute-start | bytes 6291464 | tf_op jit(solution)/shard_map/ppermute | solution.py:722
  154.9 10.6 %collective-permute-start.19 = (f32[1024,256]{1,0:T(8,128)}, f32[1024,256]{1,0:T(8,128)}, u32[]{:S(2)}, u32[]{:S(2)}) collective-permute-start(f32[1024,256]{1,0:T(8,128)} %plus.6.refs_8_.refs_2_), channel_id=1, source_target_pairs={{0,8},{1,9},{14,6},{15,7},{16,24},{17,25},{30,22},{31,23}} | collective-permute-start | bytes 3145736 | tf_op jit(solution)/shard_map/ppermute | solution.py:672
  158.8 14.5 %collective-permute-start.21 = (f32[1024,128]{1,0:T(8,128)}, f32[1024,128]{1,0:T(8,128)}, u32[]{:S(2)}, u32[]{:S(2)}) collective-permute-start(f32[1024,128]{1,0:T(8,128)} %get-tuple-element.61.refs_4_), channel_id=1, source_target_pairs={{2,3},{1,0},{6,7},{5,4},{10,11},{9,8},{14,15},{13,12},{18,19},{17,... | collective-permute-start | bytes 1572872 | tf_op jit(solution)/shard_map/ppermute | solution.py:754
  166.8 12.9 %collective-permute-start.20 = (f32[1024,128]{1,0:T(8,128)}, f32[1024,128]{1,0:T(8,128)}, u32[]{:S(2)}, u32[]{:S(2)}) collective-permute-start(f32[1024,128]{1,0:T(8,128)} %gate.5.refs_2_.refs_4_), channel_id=1, source_target_pairs={{2,3},{1,0},{6,7},{5,4},{10,11},{9,8},{14,15},{13,12},{18,19},{17,... | collective-permute-start | bytes 1572872 | tf_op jit(solution)/shard_map/ppermute | solution.py:760
  171.9 26.6 %collective-permute-start.25 = (f32[1024,256]{1,0:T(8,128)}, f32[1024,256]{1,0:T(8,128)}, u32[]{:S(2)}, u32[]{:S(2)}) collective-permute-start(f32[1024,256]{1,0:T(8,128)} %plus.7.refs_6_.refs_4_), channel_id=1, source_target_pairs={{0,8},{4,12},{1,9},{5,13},{10,2},{14,6},{11,3},{15,7},{16,24},{20,... | collective-permute-start | bytes 3145736 | tf_op jit(solution)/shard_map/ppermute | solution.py:765
  188.3 17.4 %collective-permute-start.26 = (f32[1024,128]{1,0:T(8,128)}, f32[1024,128]{1,0:T(8,128)}, u32[]{:S(2)}, u32[]{:S(2)}) collective-permute-start(f32[1024,128]{1,0:T(8,128)} %plus.8.refs_2_.refs_6_), channel_id=1, source_target_pairs={{4,12},{5,13},{10,2},{11,3},{20,28},{21,29},{26,18},{27,19}} | collective-permute-start | bytes 1572872 | tf_op jit(solution)/shard_map/ppermute | solution.py:672
  192.9 18.4 %collective-permute-start.27 = (f32[1024,128]{1,0:T(8,128)}, f32[1024,128]{1,0:T(8,128)}, u32[]{:S(2)}, u32[]{:S(2)}) collective-permute-start(f32[1024,128]{1,0:T(8,128)} %plus.9.refs_3_.refs_7_), channel_id=1, source_target_pairs={{4,12},{5,13},{10,2},{11,3},{20,28},{21,29},{26,18},{27,19}} | collective-permute-start | bytes 1572872 | tf_op jit(solution)/shard_map/ppermute | solution.py:672
  (25 other events, 210.0 us)
